TPU v7x, 32 devices: a whole 2x2x4 slice. The times are simulated.
32 devices in a mesh: ctx: 8 (over y, x, core), wt: 4 (over z).
Axes of the slice: x: 2, y: 2, z: 4, core: 2. Of those that a mesh axis runs over, the one named last changes fastest.
Arguments:
- inputs: bfloat16 [4, 3584, 768], P('wt', 'ctx'), may hold values from -6 to 6
- block_table: int32 [8, 2], replicated, may hold values from 0 to 15, as said below
- ln1_gain: bfloat16 [2, 768], P(None, 'wt'), may hold values from 0.5 to 1.5
- ln1_bias: bfloat16 [2, 768], P(None, 'wt'), may hold values from -1 to 1
- qkv_weight: bfloat16 [2, 768, 2304], P(None, 'wt'), may hold values from -0.21875 to 0.21875
- query_bias: bfloat16 [2, 768], P(None, 'wt'), may hold values from -1 to 1
- value_bias: bfloat16 [2, 768], P(None, 'wt'), may hold values from -0.25 to 0.25
- out_weight: bfloat16 [2, 768, 768], P(None, 'wt'), may hold values from -0.875 to 0.875
- out_bias: bfloat16 [2, 768], P(None, 'wt'), may hold values from -1 to 1
- ln2_gain: bfloat16 [2, 768], P(None, 'wt'), may hold values from 0.5 to 1.5
- ln2_bias: bfloat16 [2, 768], P(None, 'wt'), may hold values from -1 to 1
- up_weight: bfloat16 [2, 768, 3072], P(None, 'wt'), may hold values from -0.21875 to 0.21875
- up_bias: bfloat16 [2, 3072], P(None, 'wt'), may hold values from -1 to 1
- down_weight: bfloat16 [2, 3072, 768], P(None, 'wt'), may hold values from -0.109375 to 0.109375
- down_bias: bfloat16 [2, 768], P(None, 'wt'), may hold values from -1 to 1
- cotangent: bfloat16 [4, 3584, 768], P('wt', 'ctx'), may hold values from -6 to 6
Outputs:
- outputs: bfloat16 [4, 3584, 768], P('wt', 'ctx')
- inputs_grad: float32 [4, 3584, 768], P('wt', 'ctx')
- ln1_gain_grad: float32 [2, 768], P(None, 'wt')
- ln1_bias_grad: float32 [2, 768], P(None, 'wt')
- qkv_weight_grad: float32 [2, 768, 2304], P(None, 'wt')
- query_bias_grad: float32 [2, 768], P(None, 'wt')
- value_bias_grad: float32 [2, 768], P(None, 'wt')
- out_weight_grad: float32 [2, 768, 768], P(None, 'wt')
- out_bias_grad: float32 [2, 768], P(None, 'wt')
- ln2_gain_grad: float32 [2, 768], P(None, 'wt')
- ln2_bias_grad: float32 [2, 768], P(None, 'wt')
- up_weight_grad: float32 [2, 768, 3072], P(None, 'wt')
- up_bias_grad: float32 [2, 3072], P(None, 'wt')
- down_weight_grad: float32 [2, 3072, 768], P(None, 'wt')
- down_bias_grad: float32 [2, 768], P(None, 'wt')
Inputs may be any that keep to these rules, and one draw needn't show every extreme that they name: `block_table`: row c holds p and 15 - p for some p < 8; the first column is a permutation of 0 to 7.
All inputs are finite; a program needn't handle non-finite values.
Results may differ from a plain program's by a relative error of at most 0.011.
Values may be sent and summed in bfloat16 or wider, within the bound.
No kernel may reach another device: no remote copies, remote signals or barrier semaphores. Data moves between devices by JAX's collectives and lax.ppermute only.
A program may use at most 320 MiB of HBM per device.

v0:
```python
import jax
import jax.numpy as jnp
from jax import lax
from jax.sharding import PartitionSpec as P

HEAD_DIM = 64
LAYERS = 2


epsilon = 1e-05
gelu_coeff = 0.7978845608028654


def norm_rows(values, gain_vec, shift_vec):
    row_mean = jnp.mean(values, axis=-1, keepdims=True)
    centred = values - row_mean
    row_var = jnp.mean(centred * centred, axis=-1, keepdims=True)
    return centred * lax.rsqrt(row_var + epsilon) * gain_vec + shift_vec


def gelu_tanh(values):
    return (
        0.5 * values * (1.0 + jnp.tanh(gelu_coeff * (values + 0.044715 * values * values * values)))
    )


def project(operand, matrix):
    return jnp.einsum("sre,ef->srf", operand, matrix, preferred_element_type=jnp.float32)


def project_back(operand, matrix):
    return jnp.einsum("srf,ef->sre", operand, matrix, preferred_element_type=jnp.float32)


def weight_grad(operand, gradient):
    return jnp.einsum("sre,srf->ef", operand, gradient, preferred_element_type=jnp.float32)


def row_total(values):
    return jnp.sum(values.astype(jnp.float32), axis=(0, 1))


def columns(array, head_index, head_width):
    return lax.dynamic_slice_in_dim(array, head_index * head_width, head_width, 2)


def put_columns(array, update, head_index, head_width):
    return lax.dynamic_update_slice_in_dim(array, update, head_index * head_width, 2)


def gather_forward(shards, layer_index):
    return (
        lax.all_gather(shards[0][layer_index], "wt", axis=0, tiled=True),
        lax.all_gather(shards[1][layer_index], "wt", axis=0, tiled=True),
        lax.all_gather(shards[2][layer_index], "wt", axis=0, tiled=True),
        lax.all_gather(shards[3][layer_index], "wt", axis=0, tiled=True),
        lax.all_gather(shards[4][layer_index], "wt", axis=0, tiled=True),
        lax.all_gather(shards[5][layer_index], "wt", axis=0, tiled=True),
        lax.all_gather(shards[6][layer_index], "wt", axis=0, tiled=True),
        lax.all_gather(shards[7][layer_index], "wt", axis=0, tiled=True),
        lax.all_gather(shards[8][layer_index], "wt", axis=0, tiled=True),
        lax.all_gather(shards[9][layer_index], "wt", axis=0, tiled=True),
        lax.all_gather(shards[10][layer_index], "wt", axis=0, tiled=True),
        lax.all_gather(shards[11][layer_index], "wt", axis=0, tiled=True),
        lax.all_gather(shards[12][layer_index], "wt", axis=0, tiled=True),
    )


def gather_backward(shards, layer_index):
    return (
        lax.all_gather(shards[0][layer_index], "wt", axis=0, tiled=True),
        lax.all_gather(shards[1][layer_index], "wt", axis=0, tiled=True),
        lax.all_gather(shards[2][layer_index], "wt", axis=0, tiled=True),
        lax.all_gather(shards[3][layer_index], "wt", axis=0, tiled=True),
        lax.all_gather(shards[4][layer_index], "wt", axis=0, tiled=True),
        lax.all_gather(shards[5][layer_index], "wt", axis=0, tiled=True),
        lax.all_gather(shards[6][layer_index], "wt", axis=0, tiled=True),
        lax.all_gather(shards[7][layer_index], "wt", axis=0, tiled=True),
        lax.all_gather(shards[8][layer_index], "wt", axis=0, tiled=True),
        lax.all_gather(shards[9][layer_index], "wt", axis=0, tiled=True),
        lax.all_gather(shards[10][layer_index], "wt", axis=0, tiled=True),
        lax.all_gather(shards[11][layer_index], "wt", axis=0, tiled=True),
        lax.all_gather(shards[12][layer_index], "wt", axis=0, tiled=True),
    )


def reduce_grads(grads):
    owned = (
        lax.psum_scatter(grads[0], "wt", scatter_dimension=0, tiled=True),
        lax.psum_scatter(grads[1], "wt", scatter_dimension=0, tiled=True),
        lax.psum_scatter(grads[2], "wt", scatter_dimension=0, tiled=True),
        lax.psum_scatter(grads[3], "wt", scatter_dimension=0, tiled=True),
        lax.psum_scatter(grads[4], "wt", scatter_dimension=0, tiled=True),
        lax.psum_scatter(grads[5], "wt", scatter_dimension=0, tiled=True),
        lax.psum_scatter(grads[6], "wt", scatter_dimension=0, tiled=True),
        lax.psum_scatter(grads[7], "wt", scatter_dimension=0, tiled=True),
        lax.psum_scatter(grads[8], "wt", scatter_dimension=0, tiled=True),
        lax.psum_scatter(grads[9], "wt", scatter_dimension=0, tiled=True),
        lax.psum_scatter(grads[10], "wt", scatter_dimension=0, tiled=True),
        lax.psum_scatter(grads[11], "wt", scatter_dimension=0, tiled=True),
        lax.psum_scatter(grads[12], "wt", scatter_dimension=0, tiled=True),
    )
    return lax.psum(
        (
            owned[0],
            owned[1],
            owned[2],
            owned[3],
            owned[4],
            owned[5],
            owned[6],
            owned[7],
            owned[8],
            owned[9],
            owned[10],
            owned[11],
            owned[12],
        ),
        "ctx",
    )


def head_scores(query_h, key_h, allowed, scale):
    scores = jnp.einsum("sqd,skd->sqk", query_h, key_h, preferred_element_type=jnp.float32) * scale
    return jnp.where(allowed[None], scores, -1e30)


def layer_forward(state, gathered, allowed):
    (
        gain_first,
        shift_first,
        w_mix,
        bias_query,
        bias_value,
        w_proj,
        bias_proj,
        gain_second,
        shift_second,
        w_upper,
        bias_upper,
        w_lower,
        bias_lower,
    ) = gathered
    seq_count, row_count, width = state.shape
    heads_count = width // HEAD_DIM
    scale = HEAD_DIM ** (-0.5)
    normed = norm_rows(
        state, gain_first.astype(jnp.float32), shift_first.astype(jnp.float32)
    ).astype(jnp.bfloat16)
    bias_all = jnp.concatenate(
        [
            bias_query.astype(jnp.float32),
            jnp.zeros((width,), jnp.float32),
            bias_value.astype(jnp.float32),
        ]
    )
    mixed = (project(normed, w_mix) + bias_all).astype(jnp.bfloat16)
    query = mixed[:, :, :width]
    key_part = mixed[:, :, width : 2 * width]
    value_part = mixed[:, :, 2 * width :]
    key_all, value_all = (
        lax.all_gather(key_part, "ctx", axis=1, tiled=True),
        lax.all_gather(value_part, "ctx", axis=1, tiled=True),
    )

    def attend(head_index, carry):
        attended_sum, lse_all = carry
        scores = head_scores(
            columns(query, head_index, HEAD_DIM),
            columns(key_all, head_index, HEAD_DIM),
            allowed,
            scale,
        )
        row_max = jnp.max(scores, axis=-1, keepdims=True)
        expd = jnp.exp(scores - row_max)
        row_sum = jnp.sum(expd, axis=-1, keepdims=True)
        probs = (expd / row_sum).astype(jnp.bfloat16)
        head_out = jnp.einsum(
            "sqk,skd->sqd",
            probs,
            columns(value_all, head_index, HEAD_DIM),
            preferred_element_type=jnp.float32,
        )
        attended_sum = put_columns(attended_sum, head_out, head_index, HEAD_DIM)
        lse_all = lax.dynamic_update_slice_in_dim(
            lse_all, row_max + jnp.log(row_sum), head_index, 2
        )
        return (attended_sum, lse_all)

    start = (
        jnp.zeros((seq_count, row_count, width), jnp.float32),
        jnp.zeros((seq_count, row_count, heads_count), jnp.float32),
    )
    attended_sum, lse_all = lax.fori_loop(0, heads_count, attend, start)
    attended = attended_sum.astype(jnp.bfloat16)
    after_attn = state + project(attended, w_proj) + bias_proj.astype(jnp.float32)
    normed_two = norm_rows(
        after_attn, gain_second.astype(jnp.float32), shift_second.astype(jnp.float32)
    ).astype(jnp.bfloat16)
    hidden_in = project(normed_two, w_upper) + bias_upper.astype(jnp.float32)
    hidden = gelu_tanh(hidden_in).astype(jnp.bfloat16)
    result = after_attn + project(hidden, w_lower) + bias_lower.astype(jnp.float32)
    saved_state = (
        state,
        normed,
        query,
        key_part,
        value_part,
        key_all,
        value_all,
        lse_all,
        attended,
        after_attn,
        normed_two,
        hidden_in,
        hidden,
    )
    return (result, saved_state)


def layer_backward(gradient, gathered, saved_state, allowed, allowed_back):
    (
        gain_first,
        shift_first,
        w_mix,
        bias_query,
        bias_value,
        w_proj,
        bias_proj,
        gain_second,
        shift_second,
        w_upper,
        bias_upper,
        w_lower,
        bias_lower,
    ) = gathered
    (
        state,
        normed,
        query,
        key_part,
        value_part,
        key_all,
        value_all,
        lse_all,
        attended,
        after_attn,
        normed_two,
        hidden_in,
        hidden,
    ) = saved_state
    seq_count, row_count, width = state.shape
    heads_count = width // HEAD_DIM
    scale = HEAD_DIM ** (-0.5)
    grad_mlp = gradient.astype(jnp.bfloat16)
    grad_bias_lower = row_total(grad_mlp)
    grad_lower = weight_grad(hidden, grad_mlp)
    grad_hidden = project_back(grad_mlp, w_lower)
    gelu_value, gelu_back = jax.vjp(gelu_tanh, hidden_in)
    grad_inner = gelu_back(grad_hidden)[0].astype(jnp.bfloat16)
    grad_bias_upper = row_total(grad_inner)
    grad_upper = weight_grad(normed_two, grad_inner)
    grad_normed_two = project_back(grad_inner, w_upper)
    norm_value, norm_back_two = jax.vjp(
        norm_rows, after_attn, gain_second.astype(jnp.float32), shift_second.astype(jnp.float32)
    )
    grad_after, grad_gain_second, grad_shift_second = norm_back_two(grad_normed_two)
    grad_after = gradient + grad_after
    grad_att = grad_after.astype(jnp.bfloat16)
    grad_bias_proj = row_total(grad_att)
    grad_proj = weight_grad(attended, grad_att)
    grad_attended = project_back(grad_att, w_proj).astype(jnp.bfloat16)

    def query_terms(head_index):
        query_h = columns(query, head_index, HEAD_DIM)
        key_h = columns(key_all, head_index, HEAD_DIM)
        value_h = columns(value_all, head_index, HEAD_DIM)
        grad_out_h = columns(grad_attended, head_index, HEAD_DIM)
        scores = head_scores(query_h, key_h, allowed, scale)
        probs = jnp.exp(scores - lax.dynamic_slice_in_dim(lse_all, head_index, 1, 2))
        grad_probs = jnp.einsum(
            "sqd,skd->sqk", grad_out_h, value_h, preferred_element_type=jnp.float32
        )
        delta = jnp.sum(probs * grad_probs, axis=-1, keepdims=True)
        grad_scores = (probs * (grad_probs - delta)).astype(jnp.bfloat16)
        grad_query_h = (
            jnp.einsum("sqk,skd->sqd", grad_scores, key_h, preferred_element_type=jnp.float32)
            * scale
        )
        return (query_h, grad_out_h, probs, grad_scores, delta, grad_query_h)

    def query_loop(head_index, carry):
        grad_query, deltas = carry
        query_h, grad_out_h, probs, grad_scores, delta, grad_query_h = query_terms(head_index)
        grad_query = put_columns(grad_query, grad_query_h, head_index, HEAD_DIM)
        deltas = lax.dynamic_update_slice_in_dim(deltas, delta, head_index, 2)
        return (grad_query, deltas)

    start = (
        jnp.zeros((seq_count, row_count, width), jnp.float32),
        jnp.zeros((seq_count, row_count, heads_count), jnp.float32),
    )
    grad_query, deltas = lax.fori_loop(0, heads_count, query_loop, start)
    query_all, grad_out_all = (
        lax.all_gather(query, "ctx", axis=1, tiled=True),
        lax.all_gather(grad_attended, "ctx", axis=1, tiled=True),
    )
    lse_every, delta_every = (
        lax.all_gather(lse_all, "ctx", axis=1, tiled=True),
        lax.all_gather(deltas, "ctx", axis=1, tiled=True),
    )

    def key_loop(head_index, carry):
        grad_key, grad_value = carry
        query_h = columns(query_all, head_index, HEAD_DIM)
        grad_out_h = columns(grad_out_all, head_index, HEAD_DIM)
        key_h = columns(key_part, head_index, HEAD_DIM)
        value_h = columns(value_part, head_index, HEAD_DIM)
        scores = head_scores(query_h, key_h, allowed_back, scale)
        probs = jnp.exp(scores - lax.dynamic_slice_in_dim(lse_every, head_index, 1, 2))
        grad_probs = jnp.einsum(
            "sqd,skd->sqk", grad_out_h, value_h, preferred_element_type=jnp.float32
        )
        grad_scores = (
            probs * (grad_probs - lax.dynamic_slice_in_dim(delta_every, head_index, 1, 2))
        ).astype(jnp.bfloat16)
        grad_key_h = (
            jnp.einsum("sqk,sqd->skd", grad_scores, query_h, preferred_element_type=jnp.float32)
            * scale
        )
        grad_value_h = jnp.einsum(
            "sqk,sqd->skd",
            probs.astype(jnp.bfloat16),
            grad_out_h,
            preferred_element_type=jnp.float32,
        )
        return (
            put_columns(grad_key, grad_key_h, head_index, HEAD_DIM),
            put_columns(grad_value, grad_value_h, head_index, HEAD_DIM),
        )

    start = (
        jnp.zeros((seq_count, row_count, width), jnp.float32),
        jnp.zeros((seq_count, row_count, width), jnp.float32),
    )
    grad_key, grad_value = lax.fori_loop(0, heads_count, key_loop, start)
    grad_mixed = jnp.concatenate([grad_query, grad_key, grad_value], axis=2).astype(jnp.bfloat16)
    grad_bias_query = row_total(grad_mixed[:, :, :width])
    grad_bias_value = row_total(grad_mixed[:, :, 2 * width :])
    grad_mix = weight_grad(normed, grad_mixed)
    grad_normed = project_back(grad_mixed, w_mix)
    norm_first, norm_back_one = jax.vjp(
        norm_rows, state, gain_first.astype(jnp.float32), shift_first.astype(jnp.float32)
    )
    grad_state, grad_gain_first, grad_shift_first = norm_back_one(grad_normed)
    grad_state = grad_after + grad_state
    grads = (
        grad_gain_first,
        grad_shift_first,
        grad_mix,
        grad_bias_query,
        grad_bias_value,
        grad_proj,
        grad_bias_proj,
        grad_gain_second,
        grad_shift_second,
        grad_upper,
        grad_bias_upper,
        grad_lower,
        grad_bias_lower,
    )
    return (grad_state, grads)


def stack_layers(layer_grads, item_index):
    return jnp.stack([layer_grads[layer_index][item_index] for layer_index in range(LAYERS)])


def body(
    inputs,
    block_table,
    ln1_gain,
    ln1_bias,
    qkv_weight,
    query_bias,
    value_bias,
    out_weight,
    out_bias,
    ln2_gain,
    ln2_bias,
    up_weight,
    up_bias,
    down_weight,
    down_bias,
    cotangent,
):
    shards = (
        ln1_gain,
        ln1_bias,
        qkv_weight,
        query_bias,
        value_bias,
        out_weight,
        out_bias,
        ln2_gain,
        ln2_bias,
        up_weight,
        up_bias,
        down_weight,
        down_bias,
    )
    block_rows = inputs.shape[1] // 2
    own_index = lax.axis_index("ctx")
    own_blocks = lax.dynamic_slice_in_dim(block_table, own_index, 1, 0).reshape(2)
    offsets = jnp.arange(block_rows, dtype=jnp.int32)
    own_pos = (own_blocks[:, None] * block_rows + offsets[None, :]).reshape(-1)
    every_pos = (block_table.reshape(-1)[:, None] * block_rows + offsets[None, :]).reshape(-1)
    allowed = own_pos[:, None] >= every_pos[None, :]
    allowed_back = every_pos[:, None] >= own_pos[None, :]
    state = inputs.astype(jnp.float32)
    saved_layers = []
    for layer_index in range(LAYERS):
        gathered = gather_forward(shards, layer_index)
        state, saved_state = layer_forward(state, gathered, allowed)
        saved_layers.append(saved_state)
    outputs = state.astype(jnp.bfloat16)
    gradient = cotangent.astype(jnp.float32)
    layer_grads = [None] * LAYERS
    for layer_index in reversed(range(LAYERS)):
        gathered = gather_backward(shards, layer_index)
        gradient, grads = layer_backward(
            gradient, gathered, saved_layers[layer_index], allowed, allowed_back
        )
        layer_grads[layer_index] = reduce_grads(grads)
    return (
        outputs,
        gradient,
        stack_layers(layer_grads, 0),
        stack_layers(layer_grads, 1),
        stack_layers(layer_grads, 2),
        stack_layers(layer_grads, 3),
        stack_layers(layer_grads, 4),
        stack_layers(layer_grads, 5),
        stack_layers(layer_grads, 6),
        stack_layers(layer_grads, 7),
        stack_layers(layer_grads, 8),
        stack_layers(layer_grads, 9),
        stack_layers(layer_grads, 10),
        stack_layers(layer_grads, 11),
        stack_layers(layer_grads, 12),
    )


def solution(mesh):
    in_specs = (
        P("wt", "ctx", None),
        P(),
        P(None, "wt"),
        P(None, "wt"),
        P(None, "wt", None),
        P(None, "wt"),
        P(None, "wt"),
        P(None, "wt", None),
        P(None, "wt"),
        P(None, "wt"),
        P(None, "wt"),
        P(None, "wt", None),
        P(None, "wt"),
        P(None, "wt", None),
        P(None, "wt"),
        P("wt", "ctx", None),
    )
    out_specs = (
        P("wt", "ctx", None),
        P("wt", "ctx", None),
        P(None, "wt"),
        P(None, "wt"),
        P(None, "wt", None),
        P(None, "wt"),
        P(None, "wt"),
        P(None, "wt", None),
        P(None, "wt"),
        P(None, "wt"),
        P(None, "wt"),
        P(None, "wt", None),
        P(None, "wt"),
        P(None, "wt", None),
        P(None, "wt"),
    )
    return jax.shard_map(body, mesh=mesh, in_specs=in_specs, out_specs=out_specs, check_vma=False)
```

profile of v0, /device:TPU:0, one launch (start us, length us, event | category | flops | bytes accessed | tf_op | source)
XLA Modules:
  0.0 2460.3 jit_solution(14960729174822869737)
XLA Ops:
  28.8 23.1 all-reduce.37
  53.6 30.3 %all-gather.57.cloned.1.call-done = bf16[1,768,2304]{2,1,0:T(8,128)(2,1)} async-done(((bf16[1,192,2304]{2,1,0:T(8,128)(2,1)}), bf16[1,768,2304]{2,1,0:T(8,128)(2,1)}) %all-gather.57.cloned.1.call-update) | async-done | bytes 3538960 | tf_op jit(solution)/shard_map/all_gather | solution.py:55
  102.1 13.0 all-gather.10
  116.9 13.4 all-gather.45.cloned.1.call-done
  130.3 44.7 %all-gather.47.cloned.1.call-done = bf16[1,3584,768]{2,1,0:T(8,128)(2,1)} async-done(((bf16[1,448,768]{2,1,0:T(8,128)(2,1)}), bf16[1,3584,768]{2,1,0:T(8,128)(2,1)}) %all-gather.47.cloned.1.call-update) | async-done | bytes 5505040 | tf_op jit(solution)/shard_map/all_gather | solution.py:163
  175.1 80.8 %while.96 = (s32[]{:T(128)}, bf16[1,448,768]{1,2,0:T(8,128)(2,1)S(1)}, f32[1,448,12]{1,0,2:T(1,128)S(1)}, bf16[1,448,768]{2,1,0:T(8,128)(2,1)S(1)}, bf16[1,3584,...) while((s32[]{:T(128)}, ...), condition=%wide.region_5.6_spmd.clone, body=%wide.region_2.5_spmd.clone.sunk | while | flops 425492032 | bytes 21387944 | solution.py:194
  259.0 39.0 %all-gather.61.cloned.1.call-done = bf16[1,768,3072]{2,1,0:T(8,128)(2,1)} async-done(((bf16[1,192,3072]{2,1,0:T(8,128)(2,1)}), bf16[1,768,3072]{2,1,0:T(8,128)(2,1)}) %all-gather.61.cloned.1.call-update) | async-done | bytes 4718608 | tf_op jit(solution)/shard_map/all_gather | solution.py:62
  298.0 7.1 fusion.164
  305.2 82.7 %all-gather.63.cloned.1.call-done = bf16[1,3072,768]{2,1,0:T(8,128)(2,1)} async-done(((bf16[1,768,768]{2,1,0:T(8,128)(2,1)}), bf16[1,3072,768]{2,1,0:T(8,128)(2,1)}) %all-gather.63.cloned.1.call-update) | async-done | bytes 4718608 | tf_op jit(solution)/shard_map/all_gather | solution.py:64
  388.0 7.9 fusion.279
  396.2 61.8 %all-gather.65.cloned.1.call-done = bf16[1,768,2304]{2,1,0:T(8,128)(2,1)} async-done(((bf16[1,192,2304]{2,1,0:T(8,128)(2,1)}), bf16[1,768,2304]{2,1,0:T(8,128)(2,1)}) %all-gather.65.cloned.1.call-update) | async-done | bytes 3538960 | tf_op jit(solution)/shard_map/all_gather | solution.py:55
  467.8 13.0 all-gather.23
  481.5 22.8 all-gather.49.cloned.1.call-done
  504.3 44.1 %all-gather.51.cloned.1.call-done = bf16[1,3584,768]{2,1,0:T(8,128)(2,1)} async-done(((bf16[1,448,768]{2,1,0:T(8,128)(2,1)}), bf16[1,3584,768]{2,1,0:T(8,128)(2,1)}) %all-gather.51.cloned.1.call-update) | async-done | bytes 5505040 | tf_op jit(solution)/shard_map/all_gather | solution.py:163
  548.5 81.8 %while.97 = (s32[]{:T(128)}, bf16[1,448,768]{1,2,0:T(8,128)(2,1)S(1)}, f32[1,448,12]{1,0,2:T(1,128)S(1)}, bf16[1,448,768]{2,1,0:T(8,128)(2,1)}, bf16[1,3584,768]...) while((s32[]{:T(128)}, ...), condition=%wide.region_13.14_spmd.clone, body=%wide.region_10.13_spmd.clone.sunk | while | flops 425492032 | bytes 21385640 | solution.py:194
  635.2 35.9 %all-gather.69.cloned.1.call-done = bf16[1,768,3072]{2,1,0:T(8,128)(2,1)} async-done(((bf16[1,192,3072]{2,1,0:T(8,128)(2,1)}), bf16[1,768,3072]{2,1,0:T(8,128)(2,1)}) %all-gather.69.cloned.1.call-update) | async-done | bytes 4718608 | tf_op jit(solution)/shard_map/all_gather | solution.py:62
  671.1 7.2 fusion.156
  678.3 82.7 %all-gather.71.cloned.1.call-done = bf16[1,3072,768]{2,1,0:T(8,128)(2,1)} async-done(((bf16[1,768,768]{2,1,0:T(8,128)(2,1)}), bf16[1,3072,768]{2,1,0:T(8,128)(2,1)}) %all-gather.71.cloned.1.call-update) | async-done | bytes 4718608 | tf_op jit(solution)/shard_map/all_gather | solution.py:64
  761.0 10.0 convert_reduce_fusion
  781.3 119.9 %while.98 = (s32[]{:T(128)}, bf16[1,448,768]{1,2,0:T(8,128)(2,1)S(1)}, f32[1,448,12]{1,0,2:T(1,128)}, bf16[1,448,768]{2,1,0:T(8,128)(2,1)}, bf16[1,3584,768]{2,1...) while((s32[]{:T(128)}, ...), condition=%wide.region_20.21_spmd.clone, body=%wide.region_18.0_spmd.clone.sunk | while | flops 631041600 | bytes 35265744 | solution.py:303
  902.8 17.4 all_gather.159
  924.8 17.6 all_gather.157
  948.8 173.4 %while.99 = (s32[]{:T(128)}, bf16[1,448,768]{1,2,0:T(8,128)(2,1)}, bf16[1,448,768]{1,2,0:T(8,128)(2,1)}, bf16[1,3584,768]{2,1,0:T(8,128)(2,1)}, bf16[1,448,768]{...) while((s32[]{:T(128)}, bf16[1,448,768]{1,2,0:T(8,128)(2,1)}, ...), condition=%wide.region_22.23_spmd.clone, body=%wide.region_21.22_spmd.clone.sunk | while | flops 834957312 | bytes 49227992 | solution.py:346
  1130.9 11.5 convert_reduce_fusion.1
  1157.9 7.1 fusion.255
  1166.0 9.7 fusion.232
  1177.1 6.4 fusion.213
  1184.9 7.0 fusion.260
  1192.8 15.6 all_gather.161
  1212.0 9.6 fusion.227
  1222.3 105.5 %while.100 = (s32[]{:T(128)}, bf16[1,448,768]{1,2,0:T(8,128)(2,1)S(1)}, f32[1,448,12]{1,0,2:T(1,128)S(1)}, bf16[1,448,768]{2,1,0:T(8,128)(2,1)}, bf16[1,3584,768...) while((s32[]{:T(128)}, ...), condition=%wide.region_29.30_spmd.clone, body=%wide.region_27.0_spmd.clone.sunk | while | flops 631041600 | bytes 35258300 | solution.py:303
  1328.0 15.2 all_gather.163
  1348.7 158.2 %while.101 = (s32[]{:T(128)}, bf16[1,448,768]{1,2,0:T(8,128)(2,1)}, bf16[1,448,768]{1,2,0:T(8,128)(2,1)}, bf16[1,3584,768]{2,1,0:T(8,128)(2,1)}, bf16[1,448,768]...) while((s32[]{:T(128)}, bf16[1,448,768]{1,2,0:T(8,128)(2,1)}, ...), condition=%wide.region_31.32_spmd.clone, body=%wide.region_30.0_spmd.clone.sunk | while | flops 834957312 | bytes 49225688 | solution.py:346
  1395.2 6.2 fusion.355
  1434.4 6.2 fusion.355
  1447.6 6.2 fusion.355
  1460.8 6.8 fusion.355
  1500.6 6.2 fusion.355
  1506.9 6.6 fusion.212
  1533.6 85.3 %reduce-scatter.23.cloned.1.call-done = f32[768,768]{1,0:T(8,128)} async-done(((f32[3072,768]{1,0:T(8,128)}), f32[768,768]{1,0:T(8,128)}) %reduce-scatter.23.cloned.1.call-update) | async-done | bytes 2359312 | tf_op jit(solution)/shard_map/reduce_scatter | solution.py:100
  1618.9 126.7 %reduce-scatter.11.cloned.1.call-done = f32[192,2304]{1,0:T(8,128)} async-done(((f32[768,2304]{1,0:T(8,128)}), f32[192,2304]{1,0:T(8,128)}) %reduce-scatter.11.cloned.1.call-update) | async-done | bytes 1769488 | tf_op jit(solution)/shard_map/reduce_scatter | solution.py:91
  1745.6 164.2 %reduce-scatter.17.cloned.1.call-done = f32[192,3072]{1,0:T(8,128)} async-done(((f32[768,3072]{1,0:T(8,128)}), f32[192,3072]{1,0:T(8,128)}) %reduce-scatter.17.cloned.1.call-update) | async-done | bytes 2359312 | tf_op jit(solution)/shard_map/reduce_scatter | solution.py:98
  1909.8 164.5 %reduce-scatter.21.cloned.1.call-done = f32[768,768]{1,0:T(8,128)} async-done(((f32[3072,768]{1,0:T(8,128)}), f32[768,768]{1,0:T(8,128)}) %reduce-scatter.21.cloned.1.call-update) | async-done | bytes 2359312 | tf_op jit(solution)/shard_map/reduce_scatter | solution.py:100
  2074.3 126.5 %reduce-scatter.9.cloned.1.call-done = f32[192,2304]{1,0:T(8,128)} async-done(((f32[768,2304]{1,0:T(8,128)}), f32[192,2304]{1,0:T(8,128)}) %reduce-scatter.9.cloned.1.call-update) | async-done | bytes 1769488 | tf_op jit(solution)/shard_map/reduce_scatter | solution.py:91
  2202.3 8.4 add_convert_fusion
  2212.4 31.0 %all-reduce.43.cloned.1.call-done = (f32[768]{0:T(1024)}, f32[768]{0:T(1024)}, f32[768]{0:T(1024)}, f32[768]{0:T(1024)}, f32[768]{0:T(1024)}, /*index=5*/f32[768...) async-done(((f32[768]{0:T(1024)}, f32[768]{0:T(1024)}, ...) | async-done | bytes 73744
  2257.0 24.8 %all-reduce.34 = (f32[1,192]{1,0:T(1,128)S(1)}, f32[1,192]{1,0:T(1,128)S(1)}, f32[1,192]{1,0:T(1,128)S(1)}, f32[1,192]{1,0:T(1,128)S(1)}, f32[1,192]{1,0:T(1,128...) all-reduce(f32[1,192]{1,0:T(1,128)S(1)} %bitcast.512, ...), channel_id=1, replica_groups=mesh['ctx'=8,'wt'=4] {'ctx'}, use_global_device_ids=true, to_apply=%region_39.40 | all-reduce | flops 4608 | bytes 36864 | tf_op jit(solution)/shard_map/psum | solution.py:103
  2284.8 156.8 %all-reduce.41.cloned.1.call-done = (f32[1,192,2304]{2,1,0:T(8,128)}, f32[1,192,2304]{2,1,0:T(8,128)}, f32[1,192,768]{2,1,0:T(8,128)}, f32[1,192,768]{2,1,0:T(8,...) async-done(((f32[1,192,2304]{2,1,0:T(8,128)}, f32[1,192,2304]{2,1,0:T(8,128)}, ...) | async-done | bytes 14155792 | tf_op jit(solution)/shard_map/psum | solution.py:103
  (889 shorter events, 857.4 us)
Async XLA Ops:
  7.3 76.6 %all-gather.57.cloned.1.call-start = ((), (), s32[]{:S(2)}) async-start(), calls=%async_computation.22 | async-start | bytes 4423680 | tf_op jit(solution)/shard_map/all_gather | solution.py:55
  10.2 120.1 %all-gather.45.cloned.1.call-start = ((), (), s32[]{:S(2)}) async-start(), calls=%async_computation.8 | async-start | bytes 6193152 | tf_op jit(solution)/shard_map/all_gather | solution.py:162
  89.2 85.9 %all-gather.47.cloned.1.call-start = ((), (), s32[]{:S(2)}) async-start(), calls=%async_computation.9 | async-start | bytes 6193152 | tf_op jit(solution)/shard_map/all_gather | solution.py:163
  89.9 166.1 %all-gather.59.cloned.1.call-start = ((), (), s32[]{:S(2)}) async-start(), calls=%async_computation.23 | async-start | bytes 1474560 | tf_op jit(solution)/shard_map/all_gather | solution.py:58
  90.8 207.2 %all-gather.61.cloned.1.call-start = ((), (), s32[]{:S(2)}) async-start(), calls=%async_computation.24 | async-start | bytes 5898240 | tf_op jit(solution)/shard_map/all_gather | solution.py:62
  94.1 293.8 %all-gather.63.cloned.1.call-start = ((), (), s32[]{:S(2)}) async-start(), calls=%async_computation.25 | async-start | bytes 5898240 | tf_op jit(solution)/shard_map/all_gather | solution.py:64
  97.6 360.4 %all-gather.65.cloned.1.call-start = ((), (), s32[]{:S(2)}) async-start(), calls=%async_computation.26 | async-start | bytes 4423680 | tf_op jit(solution)/shard_map/all_gather | solution.py:55
  98.3 406.0 %all-gather.49.cloned.1.call-start = ((), (), s32[]{:S(2)}) async-start(), calls=%async_computation.10 | async-start | bytes 6193152 | tf_op jit(solution)/shard_map/all_gather | solution.py:162
  255.9 49.2 %copy-start.16 = (bf16[1,448,768]{2,1,0:T(8,128)(2,1)}, bf16[1,448,768]{2,1,0:T(8,128)(2,1)S(1)}, u32[]{:S(2)}) copy-start(bf16[1,448,768]{2,1,0:T(8,128)(2,1)S(1)} %get-tuple-element.2081) | copy-start | bytes 2064388
  255.9 49.2 %copy-start.29 = (bf16[1,448,768]{1,2,0:T(8,128)(2,1)}, bf16[1,448,768]{1,2,0:T(8,128)(2,1)S(1)}, u32[]{:S(2)}) copy-start(bf16[1,448,768]{1,2,0:T(8,128)(2,1)S(1)} %get-tuple-element.915) | copy-start | bytes 2064388
  258.7 46.5 %copy-start.21 = (f32[1,448,768]{2,1,0:T(8,128)}, f32[1,448,768]{2,1,0:T(8,128)S(1)}, u32[]{:S(2)}) copy-start(f32[1,448,768]{2,1,0:T(8,128)S(1)} %get-tuple-element.1335) | copy-start | bytes 4128772
  259.0 128.9 %copy-start.87 = (f32[1,3072]{1,0:T(1,128)S(1)}, f32[1,3072]{1,0:T(1,128)}, u32[]{:S(2)}) copy-start(f32[1,3072]{1,0:T(1,128)} %convert_element_type.309) | copy-start | bytes 36868
  259.0 128.9 %copy-start.107 = (f32[768]{0:T(1024)S(1)}, f32[768]{0:T(1024)}, u32[]{:S(2)}) copy-start(f32[768]{0:T(1024)} %convert_element_type.327) | copy-start | bytes 9220
  387.9 70.0 %copy-start.80 = (f32[768]{0:T(1024)S(1)}, f32[768]{0:T(1024)}, u32[]{:S(2)}) copy-start(f32[768]{0:T(1024)} %convert_element_type.328) | copy-start | bytes 9220
  387.9 70.0 %copy-start.91 = (f32[2304]{0:T(1024)S(1)}, f32[2304]{0:T(1024)}, u32[]{:S(2)}) copy-start(f32[2304]{0:T(1024)} %get-tuple-element.1328) | copy-start | bytes 27652
  387.9 70.0 %copy-start.104 = (f32[768]{0:T(1024)S(1)}, f32[768]{0:T(1024)}, u32[]{:S(2)}) copy-start(f32[768]{0:T(1024)} %convert_element_type.329) | copy-start | bytes 9220
  395.9 66.0 %copy-start.62 = (f32[448]{0:T(512)}, f32[448]{0:T(512)S(1)}, u32[]{:S(2)}) copy-start(f32[448]{0:T(512)S(1)} %broadcast_multiply_fusion.1) | copy-start | bytes 5380
  396.2 65.7 %copy-start.74 = (f32[448]{0:T(512)}, f32[448]{0:T(512)S(1)}, u32[]{:S(2)}) copy-start(f32[448]{0:T(512)S(1)} %multiply_reduce_fusion.3) | copy-start | bytes 5380
  396.2 65.7 %copy-start.96 = (f32[448]{0:T(512)}, f32[448]{0:T(512)S(1)}, u32[]{:S(2)}) copy-start(f32[448]{0:T(512)S(1)} %fusion.244) | copy-start | bytes 5380
  463.3 85.2 %copy-start.44 = (s32[448]{0:T(512)S(1)}, s32[448]{0:T(512)}, u32[]{:S(2)}) copy-start(s32[448]{0:T(512)} %copy-done.43) | copy-start | bytes 5380
  463.3 85.1 %all-gather.51.cloned.1.call-start = ((), (), s32[]{:S(2)}) async-start(), calls=%async_computation.11 | async-start | bytes 6193152 | tf_op jit(solution)/shard_map/all_gather | solution.py:163
  464.1 166.3 %all-gather.67.cloned.1.call-start = ((), (), s32[]{:S(2)}) async-start(), calls=%async_computation.27 | async-start | bytes 1474560 | tf_op jit(solution)/shard_map/all_gather | solution.py:58
  464.7 206.4 %all-gather.69.cloned.1.call-start = ((), (), s32[]{:S(2)}) async-start(), calls=%async_computation.28 | async-start | bytes 5898240 | tf_op jit(solution)/shard_map/all_gather | solution.py:62
  465.4 295.5 %all-gather.71.cloned.1.call-start = ((), (), s32[]{:S(2)}) async-start(), calls=%async_computation.29 | async-start | bytes 5898240 | tf_op jit(solution)/shard_map/all_gather | solution.py:64
  466.0 480.9 %all-gather.53.cloned.1.call-start = ((), (), s32[]{:S(2)}) async-start(), calls=%async_computation.12 | async-start | bytes 6193152 | tf_op jit(solution)/shard_map/all_gather | solution.py:305
  481.5 465.4 %all-gather.73.cloned.1.call-start = ((), (), s32[]{:S(2)}) async-start(), calls=%async_computation.30 | async-start | bytes 6193152 | tf_op jit(solution)/shard_map/all_gather | solution.py:306
  630.4 47.9 %copy-start.14 = (bf16[1,448,768]{1,2,0:T(8,128)(2,1)}, bf16[1,448,768]{1,2,0:T(8,128)(2,1)S(1)}, u32[]{:S(2)}) copy-start(bf16[1,448,768]{1,2,0:T(8,128)(2,1)S(1)} %get-tuple-element.916) | copy-start | bytes 2064388
  633.1 524.7 %copy-start.2 = (f32[1,448,768]{2,1,0:T(8,128)}, f32[1,448,768]{2,1,0:T(8,128)S(1)}, u32[]{:S(2)}) copy-start(f32[1,448,768]{2,1,0:T(8,128)S(1)} %get-tuple-element.1339) | copy-start | bytes 4128772
  779.1 567.6 %all-gather.55.cloned.1.call-start = ((), (), s32[]{:S(2)}) async-start(), calls=%async_computation.13 | async-start | bytes 6193152 | tf_op jit(solution)/shard_map/all_gather | solution.py:305
  779.7 567.1 %all-gather.75.cloned.1.call-start = ((), (), s32[]{:S(2)}) async-start(), calls=%async_computation.31 | async-start | bytes 6193152 | tf_op jit(solution)/shard_map/all_gather | solution.py:306
  901.2 221.0 %copy-start.24 = (bf16[1,448,768]{1,2,0:T(8,128)(2,1)}, bf16[1,448,768]{1,2,0:T(8,128)(2,1)S(1)}, u32[]{:S(2)}) copy-start(bf16[1,448,768]{1,2,0:T(8,128)(2,1)S(1)} %get-tuple-element.918) | copy-start | bytes 2064388
  1150.6 383.0 %reduce-scatter.15.cloned.1.call-start = ((), (), s32[]{:S(2)}) async-start(), calls=%async_computation.17 | async-start | bytes 2949120 | tf_op jit(solution)/shard_map/reduce_scatter | solution.py:94
  1154.0 379.6 %reduce-scatter.13.cloned.1.call-start = ((), (), s32[]{:S(2)}) async-start(), calls=%async_computation.16 | async-start | bytes 2949120 | tf_op jit(solution)/shard_map/reduce_scatter | solution.py:94
  1157.8 375.8 %reduce-scatter.19.cloned.1.call-start = ((), (), s32[]{:S(2)}) async-start(), calls=%async_computation.19 | async-start | bytes 11796480 | tf_op jit(solution)/shard_map/reduce_scatter | solution.py:98
  1165.0 454.0 %reduce-scatter.23.cloned.1.call-start = ((), (), s32[]{:S(2)}) async-start(), calls=%async_computation.21 | async-start | bytes 11796480 | tf_op jit(solution)/shard_map/reduce_scatter | solution.py:100
  1175.8 569.9 %reduce-scatter.11.cloned.1.call-start = ((), (), s32[]{:S(2)}) async-start(), calls=%async_computation.15 | async-start | bytes 8847360 | tf_op jit(solution)/shard_map/reduce_scatter | solution.py:91
  1183.6 726.2 %reduce-scatter.17.cloned.1.call-start = ((), (), s32[]{:S(2)}) async-start(), calls=%async_computation.18 | async-start | bytes 11796480 | tf_op jit(solution)/shard_map/reduce_scatter | solution.py:98
  1191.9 882.4 %reduce-scatter.21.cloned.1.call-start = ((), (), s32[]{:S(2)}) async-start(), calls=%async_computation.20 | async-start | bytes 11796480 | tf_op jit(solution)/shard_map/reduce_scatter | solution.py:100
  1221.6 979.2 %reduce-scatter.9.cloned.1.call-start = ((), (), s32[]{:S(2)}) async-start(), calls=%async_computation.14 | async-start | bytes 8847360 | tf_op jit(solution)/shard_map/reduce_scatter | solution.py:91
  1327.8 179.1 %copy-start.28 = (bf16[1,448,768]{1,2,0:T(8,128)(2,1)}, bf16[1,448,768]{1,2,0:T(8,128)(2,1)S(1)}, u32[]{:S(2)}) copy-start(bf16[1,448,768]{1,2,0:T(8,128)(2,1)S(1)} %get-tuple-element.923) | copy-start | bytes 2064388
  1348.6 158.2 %copy-start.13 = (bf16[1,448,768]{2,1,0:T(8,128)(2,1)S(1)}, bf16[1,448,768]{2,1,0:T(8,128)(2,1)}, u32[]{:S(2)}) copy-start(bf16[1,448,768]{2,1,0:T(8,128)(2,1)} %param.28) | copy-start | bytes 2064388
  1348.6 158.2 %copy-start.52 = (f32[768]{0:T(1024)S(1)}, f32[768]{0:T(1024)}, u32[]{:S(2)}) copy-start(f32[768]{0:T(1024)} %copy-done.51) | copy-start | bytes 9220
  1348.6 158.2 %copy-start.54 = (f32[448]{0:T(512)S(1)}, f32[448]{0:T(512)}, u32[]{:S(2)}) copy-start(f32[448]{0:T(512)} %copy-done.53) | copy-start | bytes 5380
  1348.6 158.2 %copy-start.56 = (f32[448]{0:T(512)S(1)}, f32[448]{0:T(512)}, u32[]{:S(2)}) copy-start(f32[448]{0:T(512)} %copy-done.55) | copy-start | bytes 5380
  1348.6 158.2 %copy-start.102 = (f32[768]{0:T(1024)S(1)}, f32[768]{0:T(1024)}, u32[]{:S(2)}) copy-start(f32[768]{0:T(1024)} %copy-done.101) | copy-start | bytes 9220
  1513.5 729.9 %all-reduce.43.cloned.1.call-start = ((), (), s32[]{:S(2)}) async-start(), calls=%async_computation.33 | async-start | bytes 180224
  1529.3 671.5 %copy-start.10 = (f32[448,768]{1,0:T(8,128)}, f32[448,768]{1,0:T(8,128)S(1)}, u32[]{:S(2)}) copy-start(f32[448,768]{1,0:T(8,128)S(1)} %get-tuple-element.1344) | copy-start | bytes 4128772
  1533.5 908.1 %all-reduce.41.cloned.1.call-start = ((), (), s32[]{:S(2)}) async-start(), calls=%async_computation.32 | async-start | bytes 28311552 | tf_op jit(solution)/shard_map/psum | solution.py:103
  (139 other events, 923.5 us)
Sparse Core Ops, SparseCore 0:
  10.3 73.5 all-gather.56
  89.3 40.9 all-gather.44
  132.8 42.2 all-gather.46
  177.0 30.4 all-gather.58
  209.5 88.5 all-gather.60
  300.0 87.8 all-gather.62
  389.5 68.4 all-gather.64
  463.5 40.7 all-gather.48
  506.2 42.2 all-gather.50
  549.9 30.3 all-gather.66
  582.4 88.5 all-gather.68
  673.0 87.8 all-gather.70
  762.8 40.6 all-gather.52
  805.8 42.2 all-gather.72
  849.8 42.2 all-gather.54
  1150.7 40.1 all-gather.74
  1193.6 48.0 reduce-scatter.14
  1243.8 47.5 reduce-scatter.12
  1293.8 160.7 reduce-scatter.18
  1456.8 162.1 reduce-scatter.22
  1621.2 124.3 reduce-scatter.10
  1748.0 161.7 reduce-scatter.16
  1912.1 162.1 reduce-scatter.20
  2076.5 124.3 reduce-scatter.8
  2205.8 37.5 all-reduce.42
  2248.7 192.8 all-reduce.40
where the time goes:
time: 2480 us; the launch traced here: 2460 us
  waiting for transfers between devices  1320 us (53%)
  matrix products  797 us (32%)
  blocking collectives  140 us (6%)
  local copies, waits for them, and re-layouts  117 us (5%)
  other arithmetic  67.5 us (3%)
    reduce_scatter x2, waiting for transfers between devices, reduce_grads(): lax.psum_scatter(grads[2], 'wt', scatter_dimension=0, tiled=True)  253 us
    reduce_scatter x2, waiting for transfers between devices, reduce_grads(): lax.psum_scatter(grads[11], 'wt', scatter_dimension=0, tiled=True)  250 us
    dot_general x72, matrix products, head_scores(): jnp.einsum('sqd,skd->sqk', query_h, key_h, preferred_element_type=jnp.flo...  222 us
    all_gather x2, waiting for transfers between devices, gather_forward(): lax.all_gather(shards[11][layer_index], 'wt', axis=0, tiled=True)  165 us
    reduce_scatter x2, waiting for transfers between devices, reduce_grads(): lax.psum_scatter(grads[9], 'wt', scatter_dimension=0, tiled=True)  164 us
    psum x1, waiting for transfers between devices, reduce_grads(): lax.psum((owned[0], owned[1], owned[2], owned[3], owned[4], owned[5], own...  157 us
    dot_general x24, matrix products, key_loop(): jnp.einsum('sqk,sqd->skd', grad_scores, query_h, preferred_element_type=j...  148 us
    dot_general x24, matrix products, key_loop(): jnp.einsum('sqk,sqd->skd', probs.astype(jnp.bfloat16), grad_out_h, prefer...  95.1 us
  transfers between devices with their start and end apart: 26, of which 17 were waited for; matrix products, arithmetic and copies ran while one was open for 38% of the time, Pallas kernels for 0%

commit v1 on v0

v1 whole, which is shorter than its diff:
```python
import functools

import jax
import jax.numpy as jnp
from jax import lax
from jax.experimental import pallas as pl
from jax.experimental.pallas import tpu as pltpu
from jax.sharding import PartitionSpec as P

HEAD_DIM = 64
LAYERS = 2
GROUPS = 4

epsilon = 1e-05
gelu_coeff = 0.7978845608028654
BF = jnp.bfloat16
F32 = jnp.float32


def gelu_tanh(values):
    return (
        0.5 * values * (1.0 + jnp.tanh(gelu_coeff * (values + 0.044715 * values * values * values)))
    )


def dot_nt(a, b):
    return lax.dot_general(a, b, (((1,), (1,)), ((), ())), preferred_element_type=F32)


def dot_nn(a, b):
    return lax.dot_general(a, b, (((1,), (0,)), ((), ())), preferred_element_type=F32)


def dot_tn(a, b):
    return lax.dot_general(a, b, (((0,), (0,)), ((), ())), preferred_element_type=F32)


def whole(shape):
    return pl.BlockSpec(shape, lambda *_: (0,) * len(shape))


def norm_parts(values):
    mean = jnp.mean(values, axis=-1, keepdims=True)
    centred = values - mean
    var = jnp.mean(centred * centred, axis=-1, keepdims=True)
    scale = lax.rsqrt(var + epsilon)
    return centred * scale, scale


def norm_back(grad, unit, scale, gain):
    inner = grad * gain
    a = jnp.mean(inner, axis=-1, keepdims=True)
    b = jnp.mean(inner * unit, axis=-1, keepdims=True)
    return (
        scale * (inner - a - unit * b),
        jnp.sum(grad * unit, axis=0, keepdims=True),
        jnp.sum(grad, axis=0, keepdims=True),
    )


def split_refs(refs, *counts):
    out, at = [], 0
    for count in counts:
        out.append(refs[at : at + count])
        at += count
    return out


def mix_kernel(qkv_rows, group_ids, state_ref, gain_ref, shift_ref, w_ref, bias_ref, *refs):
    out_refs, (normed_ref, proj_ref) = split_refs(refs, GROUPS, 2)
    inner = w_ref.shape[0] // GROUPS
    unit, _ = norm_parts(state_ref[...])
    normed = (unit * gain_ref[...] + shift_ref[...]).astype(BF)
    normed_ref[...] = normed
    for k in range(GROUPS):
        g = group_ids[k]
        w = jnp.concatenate([w_ref[g * inner + e, :qkv_rows, :] for e in range(inner)], 0)
        out_refs[k][...] = (dot_nt(normed, w) + bias_ref[g]).astype(BF)
    proj = jnp.concatenate([w_ref[c, qkv_rows:, :] for c in range(w_ref.shape[0])], 0)
    proj = proj.astype(F32).T.astype(BF)
    gw = proj_ref.shape[1]
    for g in range(GROUPS):
        proj_ref[g] = proj[g * gw : (g + 1) * gw]


def mix(group_ids, state, gain, shift, w, bias):
    rows, width = state.shape
    cols = bias.shape[2]
    inner = w.shape[0] // GROUPS
    return pl.pallas_call(
        functools.partial(mix_kernel, cols // inner),
        out_shape=[jax.ShapeDtypeStruct((rows, cols), BF)] * GROUPS
        + [
            jax.ShapeDtypeStruct((rows, width), BF),
            jax.ShapeDtypeStruct((GROUPS, width // GROUPS, width), BF),
        ],
        grid_spec=pltpu.PrefetchScalarGridSpec(
            num_scalar_prefetch=1,
            grid=(1,),
            in_specs=[whole(state.shape), whole(gain.shape), whole(shift.shape), whole(w.shape), whole(bias.shape)],
            out_specs=[whole((rows, cols))] * GROUPS
            + [whole((rows, width)), whole((GROUPS, width // GROUPS, width))],
        ),
        compiler_params=pltpu.CompilerParams(vmem_limit_bytes=40 << 20),
        cost_estimate=pl.CostEstimate(
            flops=2 * rows * width * cols * GROUPS, bytes_accessed=2 * w.size, transcendentals=0
        ),
        name="mix",
    )(group_ids, state, gain, shift, w, bias)


def mix_back_kernel(
    qkv_rows, group_ids, grad_ref, state_ref, gain_ref, normed_ref, w_ref, dproj_ref, *refs
):
    gm_refs, (dw_ref, out_ref, dgain_ref, dshift_ref, dbias_ref) = split_refs(refs, GROUPS, 5)
    inner = w_ref.shape[0] // GROUPS
    rows = state_ref.shape[0]
    normed = normed_ref[...]
    ones = jnp.ones((8, rows), BF)
    total = None
    for k in range(GROUPS):
        g = group_ids[k]
        gm = gm_refs[k][...]
        w = jnp.concatenate([w_ref[g * inner + e, :qkv_rows, :] for e in range(inner)], 0)
        part = dot_nn(gm, w)
        total = part if total is None else total + part
        dw = dot_tn(gm, normed).astype(BF)
        for e in range(inner):
            dw_ref[g * inner + e, :qkv_rows, :] = dw[e * qkv_rows : (e + 1) * qkv_rows]
        dbias_ref[g] = dot_nn(ones, gm)
    dproj = jnp.concatenate([dproj_ref[g] for g in range(GROUPS)], 0)
    dproj = dproj.astype(F32).T.astype(BF)
    part = dproj.shape[0] // dw_ref.shape[0]
    for c in range(dw_ref.shape[0]):
        dw_ref[c, qkv_rows:, :] = dproj[c * part : (c + 1) * part]
    unit, scale = norm_parts(state_ref[...])
    back, dgain, dshift = norm_back(total, unit, scale, gain_ref[...])
    out_ref[...] = grad_ref[...] + back
    dgain_ref[...] = dgain
    dshift_ref[...] = dshift


def mix_back(group_ids, grad_after, state, gain, normed, w, dproj, gms):
    rows, width = state.shape
    cols = gms[0].shape[1]
    n = w.shape[0]
    inner = n // GROUPS
    vec = jax.ShapeDtypeStruct((1, width), F32)
    return pl.pallas_call(
        functools.partial(mix_back_kernel, cols // inner),
        out_shape=[
            jax.ShapeDtypeStruct(w.shape, BF),
            jax.ShapeDtypeStruct((rows, width), F32),
            vec,
            vec,
            jax.ShapeDtypeStruct((GROUPS, 8, cols), F32),
        ],
        grid_spec=pltpu.PrefetchScalarGridSpec(
            num_scalar_prefetch=1,
            grid=(1,),
            in_specs=[whole(x.shape) for x in (grad_after, state, gain, normed, w, dproj, *gms)],
            out_specs=[
                whole(w.shape),
                whole((rows, width)),
                whole((1, width)),
                whole((1, width)),
                whole((GROUPS, 8, cols)),
            ],
        ),
        compiler_params=pltpu.CompilerParams(vmem_limit_bytes=52 << 20),
        cost_estimate=pl.CostEstimate(
            flops=4 * rows * width * cols * GROUPS, bytes_accessed=4 * w.size, transcendentals=0
        ),
        name="mix_back",
    )(group_ids, grad_after, state, gain, normed, w, dproj, *gms)


def turn_weights_kernel(got_ref, attn_ref, feed_ref):
    m = got_ref.shape[0]
    attn_rows, width = attn_ref.shape
    part = width // m
    turned = jnp.concatenate([got_ref[i, :part, :] for i in range(m)], 0)
    turned = turned.astype(F32).T.astype(BF)
    attn_ref[...] = turned[:attn_rows]
    up = feed_ref.shape[0] // 2
    feed_ref[:up, :] = turned[attn_rows : attn_rows + up]
    down = up // m
    for i in range(m):
        feed_ref[up + i * down : up + (i + 1) * down, :] = got_ref[i, part : part + down, :]


def turn_feed_kernel(part_ref, out_ref):
    m, _, cols = out_ref.shape
    two, width = part_ref.shape
    rows, down = width // m, two // (2 * m)
    up = part_ref[: two // 2, :].astype(F32).T.astype(BF)
    for i in range(m):
        out_ref[i, :rows, :] = up[i * rows : (i + 1) * rows]
        low = part_ref[two // 2 + i * down : two // 2 + (i + 1) * down, :]
        for c in range(width // cols):
            out_ref[i, rows + c * down : rows + (c + 1) * down, :] = low[:, c * cols : (c + 1) * cols]


def turn_attn_kernel(part_ref, out_ref):
    m, rows, _ = out_ref.shape
    turned = part_ref[...].astype(F32).T.astype(BF)
    for i in range(m):
        out_ref[i] = turned[i * rows : (i + 1) * rows]


def turn(kernel, x, *shapes):
    out = [jax.ShapeDtypeStruct(shape, BF) for shape in shapes]
    return pl.pallas_call(
        kernel,
        out_shape=out if len(out) > 1 else out[0],
        compiler_params=pltpu.CompilerParams(vmem_limit_bytes=24 << 20),
        cost_estimate=pl.CostEstimate(flops=0, bytes_accessed=4 * x.size, transcendentals=0),
        name="turn",
    )(x)


def mlp_kernel(group_ids, state_ref, proj_ref, bproj_ref, gain_ref, shift_ref, w_ref, bup_ref, bdown_ref, *refs):
    att_refs, (after_ref, normed_ref, out_ref) = split_refs(refs, GROUPS, 3)
    c = pl.program_id(0)

    @pl.when(c == 0)
    def _():
        after = state_ref[...] + bproj_ref[...]
        for k in range(GROUPS):
            after = after + dot_nn(att_refs[k][...], proj_ref[group_ids[k]])
        after_ref[...] = after
        unit, _ = norm_parts(after)
        normed_ref[...] = (unit * gain_ref[...] + shift_ref[...]).astype(BF)
        out_ref[...] = after + bdown_ref[...]

    part = w_ref.shape[1] // 2
    hidden = gelu_tanh(dot_nt(normed_ref[...], w_ref[0, :part, :]) + bup_ref[0])
    out_ref[...] += dot_nn(hidden.astype(BF), w_ref[0, part:, :])


def mlp(group_ids, state, proj, bproj, gain, shift, w, bup, bdown, atts):
    rows, width = state.shape
    n, two, _ = w.shape
    wide = jax.ShapeDtypeStruct((rows, width), F32)
    return pl.pallas_call(
        mlp_kernel,
        out_shape=[wide, jax.ShapeDtypeStruct((rows, width), BF), wide],
        grid_spec=pltpu.PrefetchScalarGridSpec(
            num_scalar_prefetch=1,
            grid=(n,),
            in_specs=[whole(x.shape) for x in (state, proj, bproj, gain, shift)]
            + [
                pl.BlockSpec((1, two, width), lambda c, *_: (c, 0, 0)),
                pl.BlockSpec((1, 1, two // 2), lambda c, *_: (c, 0, 0)),
                whole(bdown.shape),
            ]
            + [whole(x.shape) for x in atts],
            out_specs=[whole((rows, width))] * 3,
        ),
        compiler_params=pltpu.CompilerParams(vmem_limit_bytes=40 << 20),
        cost_estimate=pl.CostEstimate(
            flops=2 * rows * (w.size + proj.size), bytes_accessed=2 * w.size, transcendentals=0
        ),
        name="mlp",
    )(group_ids, state, proj, bproj, gain, shift, w, bup, bdown, *atts)


def mlp_back_kernel(
    group_ids, grad_ref, after_ref, normed_ref, gain_ref, proj_ref, w_ref, bup_ref, *refs
):
    att_refs, datt_refs, outs, (dx_ref,) = split_refs(refs, GROUPS, GROUPS, 8, 1)
    dw_ref, dproj_ref, gafter_ref, dgain_ref, dshift_ref, dbup_ref, dbdown_ref, dbproj_ref = outs
    c = pl.program_id(0)
    rows, width = grad_ref.shape
    part = w_ref.shape[1] // 2
    grad = grad_ref[...].astype(BF)
    normed = normed_ref[...]
    up, down = w_ref[0, :part, :], w_ref[0, part:, :]
    bias = jnp.broadcast_to(bup_ref[0], (8, part)).T[:, :1]

    @pl.when(c == 0)
    def _():
        dx_ref[...] = jnp.zeros_like(dx_ref)
        dbdown_ref[...] = jnp.sum(grad.astype(F32), axis=0, keepdims=True)

    hid = dot_nt(up, normed) + bias
    square = hid * hid
    th = jnp.tanh(gelu_coeff * (hid + 0.044715 * hid * square))
    value = (0.5 * hid * (1.0 + th)).astype(BF)
    slope = 0.5 * (1.0 + th) + 0.5 * hid * (1.0 - th * th) * gelu_coeff * (
        1.0 + 3 * 0.044715 * square
    )
    ghid = (dot_nt(down, grad) * slope).astype(BF)
    dbup_ref[0] = dot_nt(jnp.ones((8, rows), BF), ghid)
    dw_ref[0, :part, :] = dot_nn(ghid, normed).astype(BF)
    dw_ref[0, part:, :] = dot_nn(value, grad).astype(BF)
    dx_ref[...] += dot_tn(ghid, up)

    @pl.when(c == pl.num_programs(0) - 1)
    def _():
        unit, scale = norm_parts(after_ref[...])
        back, dgain, dshift = norm_back(dx_ref[...], unit, scale, gain_ref[...])
        gafter = grad_ref[...] + back
        gafter_ref[...] = gafter
        dgain_ref[...] = dgain
        dshift_ref[...] = dshift
        gatt = gafter.astype(BF)
        dbproj_ref[...] = jnp.sum(gatt.astype(F32), axis=0, keepdims=True)
        for k in range(GROUPS):
            g = group_ids[k]
            datt_refs[k][...] = dot_nt(gatt, proj_ref[g]).astype(BF)
            dproj_ref[g] = dot_tn(att_refs[k][...], gatt).astype(BF)


def mlp_back(group_ids, grad, after, normed, gain, proj, w, bup, atts):
    rows, width = grad.shape
    n, two, _ = w.shape
    gw = width // GROUPS
    vec = jax.ShapeDtypeStruct((1, width), F32)
    step_w = pl.BlockSpec((1, two, width), lambda c, *_: (c, 0, 0))
    return pl.pallas_call(
        mlp_back_kernel,
        out_shape=[jax.ShapeDtypeStruct((rows, gw), BF)] * GROUPS
        + [
            jax.ShapeDtypeStruct(w.shape, BF),
            jax.ShapeDtypeStruct(proj.shape, BF),
            jax.ShapeDtypeStruct((rows, width), F32),
            vec,
            vec,
            jax.ShapeDtypeStruct((n, 8, two // 2), F32),
            vec,
            vec,
        ],
        grid_spec=pltpu.PrefetchScalarGridSpec(
            num_scalar_prefetch=1,
            grid=(n,),
            in_specs=[whole(x.shape) for x in (grad, after, normed, gain, proj)]
            + [step_w, pl.BlockSpec((1, 1, two // 2), lambda c, *_: (c, 0, 0))]
            + [whole(x.shape) for x in atts],
            out_specs=[whole((rows, gw))] * GROUPS
            + [
                step_w,
                whole(proj.shape),
                whole((rows, width)),
                whole((1, width)),
                whole((1, width)),
                pl.BlockSpec((1, 8, two // 2), lambda c, *_: (c, 0, 0)),
                whole((1, width)),
                whole((1, width)),
            ],
            scratch_shapes=[pltpu.VMEM((rows, width), F32)],
        ),
        compiler_params=pltpu.CompilerParams(vmem_limit_bytes=48 << 20),
        cost_estimate=pl.CostEstimate(
            flops=5 * rows * w.size + 4 * rows * proj.size, bytes_accessed=4 * w.size, transcendentals=0
        ),
        name="mlp_back",
    )(group_ids, grad, after, normed, gain, proj, w, bup, *atts)


def head_masks(rows, width):
    lane = lax.broadcasted_iota(jnp.int32, (rows, width), 1)
    return [
        (lane >= h * HEAD_DIM) & (lane < (h + 1) * HEAD_DIM) for h in range(width // HEAD_DIM)
    ]


def only_head(block, masks):
    wide = block.astype(F32)
    return [jnp.where(mask, wide, 0.0).astype(BF) for mask in masks]


def causal_tile(blk):
    key_at = lax.broadcasted_iota(jnp.int32, (blk, blk), 0)
    query_at = lax.broadcasted_iota(jnp.int32, (blk, blk), 1)
    return key_at <= query_at


def query_part(ref, rows, width):
    low = width // 128 * 128
    high = -(-2 * width // 128) * 128
    window = ref[rows, low:high].astype(F32)
    if width > low:
        window = pltpu.roll(window, high - width, 1)
    return (window[:, :width] * (HEAD_DIM ** (-0.5))).astype(BF)


def attend_kernel(q_id, k_loc, *refs):
    mixed_refs, o_refs, (lse_ref, q_ref, k_ref, vt_ref, acc_ref) = split_refs(
        refs, len(refs) - GROUPS - 5, GROUPS, 5
    )
    q_blocks, blk, width = q_ref.shape
    heads = width // HEAD_DIM

    for r, ref in enumerate(mixed_refs):
        for b in range(2):
            rows = slice(b * blk, (b + 1) * blk)
            k_ref[2 * r + b] = ref[rows, :width]
            vt_ref[2 * r + b] = ref[rows, 2 * width :].astype(F32).T.astype(BF)
            if r < GROUPS:
                q_ref[2 * r + b] = query_part(ref, rows, width)
    masks = head_masks(blk, width)

    def per_query(qb):
        q_blk = q_ref[qb]
        q_h = only_head(q_blk, masks)
        own = q_id[qb]
        loc = k_loc[own]
        keys = k_ref[loc]
        tri = causal_tile(blk)
        stats = []
        for h in range(heads):
            rows = slice(h * HEAD_DIM, (h + 1) * HEAD_DIM)
            s = jnp.where(tri, dot_nt(keys, q_h[h]), -1e30)
            top = jnp.max(s, axis=0, keepdims=True)
            p = jnp.exp(s - top)
            stats.append((top, jnp.sum(p, axis=0, keepdims=True)))
            acc_ref[rows, :] = dot_nn(vt_ref[loc, rows, :], p.astype(BF))

        def step(i, carry):
            loc = k_loc[i]
            keys = k_ref[loc]
            out = []
            for h in range(heads):
                rows = slice(h * HEAD_DIM, (h + 1) * HEAD_DIM)
                top, total = carry[h]
                s = dot_nt(keys, q_h[h])
                new = jnp.maximum(top, jnp.max(s, axis=0, keepdims=True))
                alpha = jnp.exp(top - new)
                p = jnp.exp(s - new)
                out.append((new, total * alpha + jnp.sum(p, axis=0, keepdims=True)))
                acc_ref[rows, :] = acc_ref[rows, :] * alpha + dot_nn(
                    vt_ref[loc, rows, :], p.astype(BF)
                )
            return tuple(out)

        stats = lax.fori_loop(0, own, step, tuple(stats))
        for h in range(heads):
            rows = slice(h * HEAD_DIM, (h + 1) * HEAD_DIM)
            top, total = stats[h]
            acc_ref[rows, :] = acc_ref[rows, :] / total
            lse_ref[qb, h : h + 1, :] = top + jnp.log(total)
        return acc_ref[...].T.astype(BF)

    for k in range(GROUPS):

        def pair(b, _, k=k):
            start = pl.multiple_of(b * blk, 32)
            o_refs[k][pl.ds(start, blk), :] = per_query(2 * k + b)
            return 0

        lax.fori_loop(0, 2, pair, 0)


def attend(q_id, k_loc, mixed):
    rows, cols = mixed[0].shape
    blk, width = rows // 2, cols // 3
    q_blocks, k_blocks = 2 * GROUPS, 2 * len(mixed)
    return pl.pallas_call(
        attend_kernel,
        out_shape=[jax.ShapeDtypeStruct((rows, width), BF)] * GROUPS
        + [jax.ShapeDtypeStruct((q_blocks, 8, blk), F32)],
        grid_spec=pltpu.PrefetchScalarGridSpec(
            num_scalar_prefetch=2,
            grid=(1,),
            in_specs=[whole(x.shape) for x in mixed],
            out_specs=[whole((rows, width))] * GROUPS + [whole((q_blocks, 8, blk))],
            scratch_shapes=[
                pltpu.VMEM((q_blocks, blk, width), BF),
                pltpu.VMEM((k_blocks, blk, width), BF),
                pltpu.VMEM((k_blocks, width, blk), BF),
                pltpu.VMEM((width, blk), F32),
            ],
        ),
        compiler_params=pltpu.CompilerParams(vmem_limit_bytes=48 << 20),
        cost_estimate=pl.CostEstimate(
            flops=4 * q_blocks * k_blocks * blk * blk * width,
            bytes_accessed=2 * len(mixed) * rows * cols,
            transcendentals=q_blocks * k_blocks * blk * blk * 2,
        ),
        name="attend",
    )(q_id, k_loc, *mixed)


def attend_back_kernel(q_id, k_loc, *refs):
    count = (len(refs) - 2 * GROUPS - 9) // 2
    mixed_refs, o_refs, do_refs, (lse_ref,), dm_refs, scratch = split_refs(
        refs, count, GROUPS, GROUPS, 1, count, 8
    )
    q_ref, k_ref, v_ref, kt_ref, dq_ref, dka_ref, dva_ref, dqt_ref = scratch
    q_blocks, blk, width = q_ref.shape
    heads = width // HEAD_DIM
    for r, ref in enumerate(mixed_refs):
        for b in range(2):
            rows = slice(b * blk, (b + 1) * blk)
            at = 2 * r + b
            keys = ref[rows, :width]
            k_ref[at] = keys
            kt_ref[at] = keys.astype(F32).T.astype(BF)
            v_ref[at] = ref[rows, 2 * width :]
            if r < GROUPS:
                q_ref[at] = query_part(ref, rows, width)

    def clear(b, _):
        dka_ref[b] = jnp.zeros((blk, width), F32)
        dva_ref[b] = jnp.zeros((blk, width), F32)
        return 0

    lax.fori_loop(0, k_ref.shape[0], clear, 0)
    masks = head_masks(blk, width)

    def per_query(qb, do_blk, o_blk):
        q_blk = q_ref[qb]
        q_h = only_head(q_blk, masks)
        do_h = only_head(do_blk, masks)
        both = (do_blk.astype(F32) * o_blk.astype(F32)).T
        delta = [
            jnp.sum(both[h * HEAD_DIM : (h + 1) * HEAD_DIM], axis=0, keepdims=True)
            for h in range(heads)
        ]
        lse = [lse_ref[qb, h : h + 1, :] for h in range(heads)]
        own = q_id[qb]

        def tile(loc, tri, first):
            keys = k_ref[loc]
            values = v_ref[loc]
            dk = dka_ref[loc]
            dv = dva_ref[loc]
            for h in range(heads):
                rows = slice(h * HEAD_DIM, (h + 1) * HEAD_DIM)
                p = jnp.exp(dot_nt(keys, q_h[h]) - lse[h])
                if tri is not None:
                    p = jnp.where(tri, p, 0.0)
                dp = dot_nt(values, do_h[h])
                ds = (p * (dp - delta[h])).astype(BF)
                dv = dv + dot_nn(p.astype(BF), do_h[h])
                dk = dk + dot_nn(ds, q_h[h])
                dq = dot_nn(kt_ref[loc, rows, :], ds)
                dqt_ref[rows, :] = dq if first else dqt_ref[rows, :] + dq
            dka_ref[loc] = dk
            dva_ref[loc] = dv

        tile(k_loc[own], causal_tile(blk), True)

        def step(i, _):
            tile(k_loc[i], None, False)
            return 0

        lax.fori_loop(0, own, step, 0)
        dq_ref[qb] = (dqt_ref[...] * (HEAD_DIM ** (-0.5))).T

    for k in range(GROUPS):

        def pair(b, _, k=k):
            rows = pl.ds(pl.multiple_of(b * blk, 32), blk)
            per_query(2 * k + b, do_refs[k][rows, :], o_refs[k][rows, :])
            return 0

        lax.fori_loop(0, 2, pair, 0)

    for r, ref in enumerate(dm_refs):

        def finish(b, _, r=r, ref=ref):
            at = 2 * r + b
            dq = dq_ref[at] if r < GROUPS else jnp.zeros((blk, width), F32)
            joined = jnp.concatenate([dka_ref[at], dq, dva_ref[at]], 1)
            ref[pl.ds(pl.multiple_of(b * blk, 32), blk), :] = joined.astype(BF)
            return 0

        lax.fori_loop(0, 2, finish, 0)


def attend_back(q_id, k_loc, mixed, o, do, lse):
    rows, cols = mixed[0].shape
    blk, width = rows // 2, cols // 3
    q_blocks, k_blocks = 2 * GROUPS, 2 * len(mixed)
    return pl.pallas_call(
        attend_back_kernel,
        out_shape=[jax.ShapeDtypeStruct((rows, cols), BF)] * len(mixed),
        grid_spec=pltpu.PrefetchScalarGridSpec(
            num_scalar_prefetch=2,
            grid=(1,),
            in_specs=[whole(x.shape) for x in (*mixed, *o, *do, lse)],
            out_specs=[whole((rows, cols))] * len(mixed),
            scratch_shapes=[
                pltpu.VMEM((q_blocks, blk, width), BF),
                pltpu.VMEM((k_blocks, blk, width), BF),
                pltpu.VMEM((k_blocks, blk, width), BF),
                pltpu.VMEM((k_blocks, width, blk), BF),
                pltpu.VMEM((q_blocks, blk, width), F32),
                pltpu.VMEM((k_blocks, blk, width), F32),
                pltpu.VMEM((k_blocks, blk, width), F32),
                pltpu.VMEM((width, blk), F32),
            ],
        ),
        compiler_params=pltpu.CompilerParams(vmem_limit_bytes=56 << 20),
        cost_estimate=pl.CostEstimate(
            flops=10 * q_blocks * k_blocks * blk * blk * width,
            bytes_accessed=4 * len(mixed) * rows * cols,
            transcendentals=q_blocks * k_blocks * blk * blk * 2,
        ),
        name="attend_back",
    )(q_id, k_loc, *mixed, *o, *do, lse)


def swap(x, axis_name, size, k):
    return lax.ppermute(x, axis_name, [(i, i ^ k) for i in range(size)])


def pick(x, at):
    return lax.dynamic_index_in_dim(x, at, 0, keepdims=False)


class Place:
    def __init__(self, n, m):
        self.n, self.m = n, m
        self.inner = n // GROUPS
        self.idx = lax.axis_index("ctx")
        self.outer_at = self.idx // self.inner
        self.inner_at = self.idx % self.inner
        self.w = lax.axis_index("wt")

    def exchange(self, parts):
        return [parts[0]] + [
            swap(parts[k], "ctx", self.n, k * self.inner) for k in range(1, GROUPS)
        ]

    def scatter_ctx(self, x):
        return lax.psum_scatter(x, "ctx", scatter_dimension=0, tiled=True)

    def gather_ctx(self, x):
        return lax.all_gather(x, "ctx", axis=0, tiled=False)

    def scatter_wt(self, x):
        total = pick(x, self.w).astype(F32)
        for k in range(1, self.m):
            total = total + swap(pick(x, self.w ^ k), "wt", self.m, k).astype(F32)
        return total

    def total(self, x):
        for axis_name, size in (("ctx", self.n), ("wt", self.m)):
            k = 1
            while k < size:
                x = x + swap(x, axis_name, size, k)
                k *= 2
        return x


def split_columns(shard, at, count, groups):
    rows, cols = shard.shape
    c = cols // (groups * count)
    cut = shard.reshape(rows, groups, count, c)
    return lax.dynamic_index_in_dim(cut, at, 2, keepdims=False).reshape(rows, groups * c)


def qkv_piece(shard, place):
    rows, cols = shard.shape
    cut = shard.reshape(rows, 3, GROUPS, cols // (3 * GROUPS))
    own = lax.dynamic_index_in_dim(cut, place.outer_at, 2, keepdims=False)
    own = jnp.concatenate([own[:, 1], own[:, 0], own[:, 2]], 1)
    part = own.shape[1] // place.inner
    return lax.dynamic_slice_in_dim(own, place.inner_at * part, part, 1)


def after(x, done):
    return lax.optimization_barrier((x, done))[0]


def pack_layer(place, matrices, layer):
    qkv_weight, out_weight, up_weight, down_weight = matrices
    n, m = place.n, place.m
    width, ff = out_weight.shape[2], up_weight.shape[2]
    columns = jnp.concatenate(
        [
            qkv_piece(qkv_weight[layer], place),
            split_columns(out_weight[layer], place.idx, n, 1),
            split_columns(up_weight[layer], place.idx, n, m),
        ],
        1,
    )
    pad = -columns.shape[1] % width
    assert pad == 0 or columns.shape[1] < width
    if pad:
        columns = jnp.pad(columns, ((0, 0), (0, pad)))
    down = pick(down_weight[layer].reshape(n, ff // (n * m), width), place.idx)
    return jnp.concatenate([columns, down], 0)


def pack_small(small, width):
    flat = [s.reshape(-1) for s in small]
    size = sum(f.shape[0] for f in flat)
    extra = -(-size // (width * 16)) * 16
    flat.append(jnp.zeros((extra * width - size,), BF))
    return jnp.concatenate(flat).reshape(extra, width)


def unpack_small(place, got, small):
    got = got.reshape(place.m, -1)
    out, at = [], 0
    for s in small:
        count, c = s.shape
        part = got[:, at : at + count * c].reshape(place.m, count, c)
        out.append(part.transpose(1, 0, 2).reshape(count, place.m * c).astype(F32))
        at += count * c
    return out


def gather_layer(place, got, ff):
    width = got.shape[2]
    attn_rows = 4 * width // place.n
    attn, feed = turn(
        turn_weights_kernel, got, (attn_rows, width), (2 * ff // place.n, width)
    )
    attn = place.gather_ctx(attn)
    return attn, place.gather_ctx(after(feed, attn))


def scatter_part(place, dw, ready, kernel, rows):
    n, two, width = dw.shape
    dw = dw.reshape(n * two, width)
    if ready is not None:
        dw = after(dw, ready)
    part = place.scatter_ctx(dw)
    return turn(kernel, part, (place.m, rows, two * width // (place.m * rows)))


def unpack_feed(place, own, ff, width):
    n, m = place.n, place.m
    rows = width // m
    up, down = own[:, :rows], own[:, rows:]
    up = up.reshape(n, rows, m, ff // (n * m)).transpose(1, 2, 0, 3).reshape(rows, ff)
    down = down.reshape(n, -1, ff // (n * m), down.shape[2]).transpose(0, 2, 1, 3)
    return up.astype(F32), down.reshape(ff // m, width).astype(F32)


def unpack_both(place, joined, ff, width):
    cut = width // place.m
    return unpack_attn(place, joined[:, :cut], width) + unpack_feed(place, joined[:, cut:], ff, width)


def unpack_attn(place, own, width):
    n, m = place.n, place.m
    rows = 3 * width // n
    gw = width // GROUPS
    qkv, proj = own[:, :, :rows], own[:, :, rows:]
    qkv = qkv.reshape(GROUPS, place.inner, width // m, rows).transpose(2, 0, 1, 3)
    qkv = qkv.reshape(width // m, GROUPS, 3, gw)
    qkv = jnp.concatenate([qkv[:, :, i].reshape(width // m, width) for i in (1, 0, 2)], 1)
    proj = proj.transpose(1, 0, 2).reshape(width // m, width)
    return qkv.astype(F32), proj.astype(F32)


def reduce_small(place, smalls):
    sizes = [v.shape[0] for v in smalls[0]]
    packed = jnp.concatenate([v for layer in smalls for v in layer]).reshape(-1, 128)
    packed = place.total(packed).reshape(len(smalls), -1)
    out, at = [], 0
    for size in sizes:
        part = packed[:, at : at + size].reshape(len(smalls), place.m, size // place.m)
        out.append(lax.dynamic_index_in_dim(part, place.w, 1, keepdims=False))
        at += size
    return out


def body(
    n, m, inputs, block_table, ln1_gain, ln1_bias, qkv_weight, query_bias, value_bias, out_weight,
    out_bias, ln2_gain, ln2_bias, up_weight, up_bias, down_weight, down_bias, cotangent,
):
    place = Place(n, m)
    rows, width = inputs.shape[1:]
    ff = up_weight.shape[2]
    gw = width // GROUPS
    group_ids = jnp.stack([place.outer_at ^ k for k in range(GROUPS)]).astype(jnp.int32)
    key_ids = jnp.concatenate(
        [
            pick(block_table, place.idx ^ (k * place.inner + j))
            for j in range(place.inner)
            for k in range(GROUPS)
        ]
    ).astype(jnp.int32)
    q_id = key_ids[: 2 * GROUPS]
    at = jnp.arange(2 * n, dtype=jnp.int32)
    k_loc = jnp.sum(jnp.where(key_ids[None, :] == at[:, None], at[None, :], 0), axis=1).astype(jnp.int32)

    small = (ln1_gain, ln1_bias, query_bias, value_bias, out_bias, ln2_gain, ln2_bias, up_bias, down_bias)
    matrices = (qkv_weight, out_weight, up_weight, down_weight)
    first = jnp.concatenate([pack_layer(place, matrices, 0), pack_small(small, width)], 0)
    got = lax.all_gather(first, "wt", axis=0, tiled=False)
    big_rows = width // m + ff // (n * m)
    vectors = unpack_small(place, got[:, big_rows:], small)
    weights = [gather_layer(place, got, ff)]
    params = []
    for layer in range(LAYERS):
        v = [x[layer].reshape(1, -1) for x in vectors]
        bias = jnp.concatenate(
            [jnp.zeros((GROUPS, 1, gw), F32), v[2].reshape(GROUPS, 1, gw), v[3].reshape(GROUPS, 1, gw)], 2
        )
        bup = v[7].reshape(m, n, ff // (n * m)).transpose(1, 0, 2).reshape(n, 1, ff // n)
        params.append((v, bias, bup))

    state = inputs[0].astype(F32)
    saved = []
    for layer in range(LAYERS):
        attn, feed = weights[layer]
        v, bias, bup = params[layer]
        *mixed, normed, proj = mix(group_ids, state, v[0], v[1], attn, bias)
        mixed = place.exchange(mixed)
        if layer + 1 < LAYERS:
            send = after(pack_layer(place, matrices, layer + 1), mixed[1])
            coming = lax.all_gather(send, "wt", axis=0, tiled=False)
        mixed = mixed + [
            swap(x, "ctx", n, j) for j in range(1, place.inner) for x in mixed
        ]
        *o, lse = attend(q_id, k_loc, mixed)
        if layer + 1 < LAYERS:
            weights.append(gather_layer(place, after(coming, o[0]), ff))
        atts = place.exchange(o)
        mid, normed_two, new = mlp(
            group_ids, state, proj, v[4], v[5], v[6], feed, bup, v[8], atts
        )
        saved.append((state, normed, mixed, o, lse, atts, mid, normed_two, proj))
        state = new
    outputs = state.astype(BF)[None]
    gradient = cotangent[0].astype(F32)
    shards, smalls, ready = [None] * LAYERS, [None] * LAYERS, None
    for layer in reversed(range(LAYERS)):
        attn, feed = weights[layer]
        v, bias, bup = params[layer]
        before, normed, mixed, o, lse, atts, mid, normed_two, proj = saved[layer]
        *datts, dfeed, dproj, gafter, dgain2, dshift2, dbup, dbdown, dbproj = mlp_back(
            group_ids, gradient, mid, normed_two, v[5], proj, feed, bup, atts
        )
        part_feed = scatter_part(place, dfeed, ready, turn_feed_kernel, 2 * width // m)
        do = place.exchange(datts)
        dm = list(attend_back(q_id, k_loc, mixed, o, do, lse))
        dm[0] = after(dm[0], part_feed)
        own_feed = place.scatter_wt(part_feed).astype(BF)
        own = []
        for k in range(GROUPS):
            if place.inner == 1:
                own.append(dm[k])
                continue
            total = dm[k].astype(F32)
            for j in range(1, place.inner):
                total = total + swap(dm[j * GROUPS + k], "ctx", n, j).astype(F32)
            own.append(total.astype(BF))
        gms = place.exchange(own)
        dmix, gradient, dgain1, dshift1, dbias = mix_back(
            group_ids, gafter, before, v[0], normed, attn, dproj, gms
        )
        if layer + 1 < LAYERS:
            joined = place.gather_ctx(after(pending, part_feed))
            shards[layer + 1] = unpack_both(place, joined, ff, width)
            dmix = after(dmix, joined)
        part_attn = scatter_part(place, dmix, part_feed, turn_attn_kernel, width // m)
        own_attn = place.scatter_wt(part_attn).astype(BF)
        pending = jnp.concatenate([own_attn, own_feed], 0)
        ready = part_attn
        if layer == 0:
            own_feed = place.gather_ctx(own_feed)
            own_attn = place.gather_ctx(after(own_attn, own_feed))
            shards[layer] = unpack_attn(place, own_attn, width) + unpack_feed(place, own_feed, ff, width)
        dbup = dbup[:, 0].reshape(n, m, ff // (n * m)).transpose(1, 0, 2)
        smalls[layer] = [
            x.reshape(-1)
            for x in (
                dgain1, dshift1, dbias[:, 0, gw : 2 * gw], dbias[:, 0, 2 * gw :], dbproj,
                dgain2, dshift2, dbup, dbdown,
            )
        ]
    vec = reduce_small(place, smalls)
    mixw, projw, up, down = [jnp.stack([s[i] for s in shards]) for i in range(4)]
    return (
        outputs, gradient[None], vec[0], vec[1], mixw, vec[2], vec[3], projw, vec[4],
        vec[5], vec[6], up, vec[7], down, vec[8],
    )


def solution(mesh):
    row, vec, mat = P("wt", "ctx", None), P(None, "wt"), P(None, "wt", None)
    in_specs = (row, P(), vec, vec, mat, vec, vec, mat, vec, vec, vec, mat, vec, mat, vec, row)
    out_specs = (row, row, vec, vec, mat, vec, vec, mat, vec, vec, vec, mat, vec, mat, vec)
    return jax.shard_map(
        functools.partial(body, mesh.shape["ctx"], mesh.shape["wt"]),
        mesh=mesh,
        in_specs=in_specs,
        out_specs=out_specs,
        check_vma=False,
    )
```

time: 2480 us -> 1050 us (0.42)
  waiting for transfers between devices: 1320 us -> 465 us
  matrix products: 797 us -> 0 us
  Pallas kernels: 0 us -> 339 us
  blocking collectives: 140 us -> 0 us
  starting transfers between devices: 1.69 us -> 69.6 us
  other arithmetic: 67.5 us -> 25.4 us
    dot_general x216 -> x0, matrix products: 797 us -> none  [the longest x72 222 us: head_scores(): jnp.einsum('sqd,skd->sqk', query_h, key_h, preferred_element_type=jnp.flo...]
    reduce_scatter x8 -> x4, waiting for transfers between devices: 667 us -> 58.1 us  [scatter_ctx(): return lax.psum_scatter(x, 'ctx', scatter_dimension=0, tiled=True)]
    pallas_call x0 -> x18, Pallas kernels: none -> 339 us  [the longest x2 142 us: attend_back(): pl.pallas_call(attend_back_kernel, out_shape=[jax.ShapeDtypeStruct((rows,...]
    all_gather x16 -> x9, waiting for transfers between devices: 457 us -> 175 us  [the longest x7 130 us: gather_ctx(): return lax.all_gather(x, 'ctx', axis=0, tiled=False)]
    ppermute x0 -> x57, waiting for transfers between devices: none -> 231 us  [swap(): return lax.ppermute(x, axis_name, [(i, i ^ k) for i in range(size)])]
    psum x1 -> x0, waiting for transfers between devices: 157 us -> none  [reduce_grads(): lax.psum((owned[0], owned[1], owned[2], owned[3], owned[4], owned[5], own...]
    all_gather x6 -> x0, blocking collectives: 91.9 us -> none  [the longest x2 33.2 us: layer_backward(): lax.all_gather(lse_all, 'ctx', axis=1, tiled=True)]
    ppermute x0 -> x57, starting transfers between devices: none -> 68.6 us  [swap(): return lax.ppermute(x, axis_name, [(i, i ^ k) for i in range(size)])]
  transfers between devices with their start and end apart: 26 -> 70, of which waited for: 17 -> 43; matrix products, arithmetic and copies ran while one was open for 38% -> 7% of each run, Pallas kernels for 0% -> 27%
where the time goes in v1:
time: 1050 us; the launch traced here: 1040 us
  waiting for transfers between devices  465 us (44%)
  Pallas kernels  339 us (32%)
  local copies, waits for them, and re-layouts  129 us (12%)
  starting transfers between devices  69.6 us (7%)
  other arithmetic  25.4 us (2%)
  between operations  15.8 us (2%)
    ppermute x57, waiting for transfers between devices, swap(): return lax.ppermute(x, axis_name, [(i, i ^ k) for i in range(size)])  231 us
    pallas_call x2, Pallas kernels, attend_back(): pl.pallas_call(attend_back_kernel, out_shape=[jax.ShapeDtypeStruct((rows,...  142 us
    all_gather x7, waiting for transfers between devices, gather_ctx(): return lax.all_gather(x, 'ctx', axis=0, tiled=False)  130 us
    pallas_call x2, Pallas kernels, attend(): pl.pallas_call(attend_kernel, out_shape=[jax.ShapeDtypeStruct((rows, widt...  82.1 us
    ppermute x57, starting transfers between devices, swap(): return lax.ppermute(x, axis_name, [(i, i ^ k) for i in range(size)])  68.6 us
    reduce_scatter x4, waiting for transfers between devices, scatter_ctx(): return lax.psum_scatter(x, 'ctx', scatter_dimension=0, tiled=True)  58.1 us
    pallas_call x2, Pallas kernels, mlp_back(): pl.pallas_call(mlp_back_kernel, out_shape=[jax.ShapeDtypeStruct((rows, gw...  54.6 us
    unnamed x250, local copies, waits for them, and re-layouts  51.7 us
  transfers between devices with their start and end apart: 70, of which 43 were waited for; matrix products, arithmetic and copies ran while one was open for 7% of the time, Pallas kernels for 27%

profile of v1, /device:TPU:0, one launch (start us, length us, event | category | flops | bytes accessed | tf_op | source)
XLA Modules:
  0.0 1043.7 jit_solution(1533461243079845009)
XLA Ops:
  37.4 44.7 %all-gather.19.cloned.1.call-done = bf16[1216,768]{1,0:T(8,128)(2,1)} async-done(((bf16[304,768]{1,0:T(8,128)(2,1)}), bf16[1216,768]{1,0:T(8,128)(2,1)}) %all-gather.19.cloned.1.call-update) | async-done | bytes 1867792 | tf_op jit(solution)/shard_map/all_gather | solution.py:788
  90.8 32.4 %all-gather.21.cloned.1.call-done = bf16[3072,768]{1,0:T(8,128)(2,1)} async-done(((bf16[384,768]{1,0:T(8,128)(2,1)}), bf16[3072,768]{1,0:T(8,128)(2,1)}) %all-gather.21.cloned.1.call-update) | async-done | bytes 4718608 | tf_op jit(solution)/shard_map/all_gather | solution.py:632
  125.5 3.8 mix.2
  134.2 3.9 reshape_squeeze.54
  150.0 23.4 %collective-permute-done.1.refs_2_ = bf16[448,576]{1,0:T(8,128)(2,1)S(1)} collective-permute-done((bf16[448,576]{1,0:T(8,128)(2,1)}, bf16[448,576]{1,0:T(8,128)(2,1)S(1)}, u32[]{:S(2)}, u32[]{:S(2)}) %collective-permute-start.1) | collective-permute-done | bytes 516128 | tf_op jit(solution)/shard_map/ppermute | solution.py:607
  176.3 41.9 %attend.2 = (bf16[448,192]{1,0:T(8,128)(2,1)S(1)}, bf16[448,192]{1,0:T(8,128)(2,1)S(1)}, bf16[448,192]{1,0:T(8,128)(2,1)S(1)}, bf16[448,192]{1,0:T(8,128)(2,1)S(1)}, f32[8,8,224]{2,1,0:T(8,128)S(1)}) custom-call(s32[8]{0:T(128)S(1)} %pad_add_fusion.1.q_id, s32[16]{0:T(128)S(1)} %select_reduce_fusion.k_loc, bf16[448,576]{1,0:T(8,128)(2,1)S(1)} %get-tuple-element.113.refs_0_, ...), custom_call_target="tpu_custom_call" | custom-call | flops 4932501504 | bytes 4128768 | tf_op jit(solution)/shard_map/attend/pallas_call | solution.py:459
  224.2 38.4 %all-gather.27.cloned.1.call-done = bf16[3072,768]{1,0:T(8,128)(2,1)} async-done(((bf16[384,768]{1,0:T(8,128)(2,1)}), bf16[3072,768]{1,0:T(8,128)(2,1)}) %all-gather.27.cloned.1.call-update) | async-done | bytes 4718608 | tf_op jit(solution)/shard_map/all_gather | solution.py:632
  268.2 4.2 collective-permute-done.7.refs_1_
  273.2 5.1 collective-permute-done.8.refs_2_
  279.7 45.8 %all-gather.23.cloned.1.call-done = bf16[6144,768]{1,0:T(8,128)(2,1)} async-done(((bf16[768,768]{1,0:T(8,128)(2,1)}), bf16[6144,768]{1,0:T(8,128)(2,1)}) %all-gather.23.cloned.1.call-update) | async-done | bytes 9437200 | tf_op jit(solution)/shard_map/all_gather | solution.py:632
  330.5 13.2 %mlp.2 = (f32[448,768]{1,0:T(8,128)S(1)}, bf16[448,768]{1,0:T(8,128)(2,1)S(1)}, f32[448,768]{1,0:T(8,128)S(1)}) custom-call(s32[4]{0:T(128)S(1)} %pad_add_fusion.group_ids, f32[448,768]{1,0:T(8,128)S(1)} %bitcast_convert_fusion.1.state_ref, bf16[4,192,768]{2,1,0:T(8,128)(2,1)S(1)} %copy-done.14, f32[1,768]{1,0:T(1,128)S(1)} %slice.283.bproj_ref, ...), custom_call_target="tpu_custom_call" | custom-call | flops 4756340736 | bytes 9437184 | tf_op jit(solution)/shard_map/mlp/pallas_call | solution.py:245
  356.1 21.4 %collective-permute-done.10.refs_1_ = bf16[448,576]{1,0:T(8,128)(2,1)S(1)} collective-permute-done((bf16[448,576]{1,0:T(8,128)(2,1)S(1)}, bf16[448,576]{1,0:T(8,128)(2,1)S(1)}, u32[]{:S(2)}, u32[]{:S(2)}) %collective-permute-start.10) | collective-permute-done | bytes 516128 | tf_op jit(solution)/shard_map/ppermute | solution.py:607
  377.5 5.0 collective-permute-done.11.refs_2_
  382.5 19.1 %collective-permute-done.12.refs_3_ = bf16[448,576]{1,0:T(8,128)(2,1)S(1)} collective-permute-done((bf16[448,576]{1,0:T(8,128)(2,1)S(1)}, bf16[448,576]{1,0:T(8,128)(2,1)S(1)}, u32[]{:S(2)}, u32[]{:S(2)}) %collective-permute-start.12) | collective-permute-done | bytes 516128 | tf_op jit(solution)/shard_map/ppermute | solution.py:607
  403.5 40.1 %attend.3 = (bf16[448,192]{1,0:T(8,128)(2,1)S(1)}, bf16[448,192]{1,0:T(8,128)(2,1)S(1)}, bf16[448,192]{1,0:T(8,128)(2,1)S(1)}, bf16[448,192]{1,0:T(8,128)(2,1)S(1)}, f32[8,8,224]{2,1,0:T(8,128)S(1)}) custom-call(s32[8]{0:T(128)S(1)} %pad_add_fusion.1.q_id, s32[16]{0:T(128)S(1)} %select_reduce_fusion.k_loc, bf16[448,576]{1,0:T(8,128)(2,1)S(1)} %get-tuple-element.128.refs_0_, ...), custom_call_target="tpu_custom_call" | custom-call | flops 4932501504 | bytes 4128768 | tf_op jit(solution)/shard_map/attend/pallas_call | solution.py:459
  452.5 5.9 collective-permute-done.18.refs_2_
  459.3 12.7 %mlp.3 = (f32[448,768]{1,0:T(8,128)S(1)}, bf16[448,768]{1,0:T(8,128)(2,1)S(1)}, f32[448,768]{1,0:T(8,128)S(1)}) custom-call(s32[4]{0:T(128)S(1)} %pad_add_fusion.group_ids, f32[448,768]{1,0:T(8,128)S(1)} %get-tuple-element.121.state_ref, bf16[4,192,768]{2,1,0:T(8,128)(2,1)S(1)} %get-tuple-element.125.proj_ref, f32[1,768]{1,0:T(1,128)S(1)} %slice.309.bproj_ref, ...), custom_call_target="tpu_custom_call" | custom-call | flops 4756340736 | bytes 9437184 | tf_op jit(solution)/shard_map/mlp/pallas_call | solution.py:245
  474.2 27.1 %mlp_back.2 = (bf16[448,192]{1,0:T(8,128)(2,1)S(1)}, bf16[448,192]{1,0:T(8,128)(2,1)S(1)}, bf16[448,192]{1,0:T(8,128)(2,1)S(1)}, bf16[448,192]{1,0:T(8,128)(2,1)...) custom-call(s32[4]{0:T(128)S(1)} %pad_add_fusion.group_ids, ...), custom_call_target="tpu_custom_call" | custom-call | flops 11626610688 | bytes 18874368 | tf_op jit(solution)/shard_map/mlp_back/pallas_call | solution.py:321
  506.6 5.1 collective-permute-done.20.refs_13_
  511.7 4.4 collective-permute-done.21.refs_14_
  516.9 71.1 %attend_back.2 = (bf16[448,576]{1,0:T(8,128)(2,1)}, bf16[448,576]{1,0:T(8,128)(2,1)}, bf16[448,576]{1,0:T(8,128)(2,1)}, bf16[448,576]{1,0:T(8,128)(2,1)}, bf16[4...) custom-call(s32[8]{0:T(128)} %copy-done.12, ...), custom_call_target="tpu_custom_call" | custom-call | flops 12331253760 | bytes 8257536 | tf_op jit(solution)/shard_map/attend_back/pallas_call | solution.py:577
  600.4 7.8 collective-permute-done.25.refs_1_
  608.3 13.2 %collective-permute-done.27.refs_2_ = bf16[448,576]{1,0:T(8,128)(2,1)} collective-permute-done((bf16[448,576]{1,0:T(8,128)(2,1)}, bf16[448,576]{1,0:T(8,128)(2,1)}, u32[]{:S(2)}, u32[]{:S(2)}) %collective-permute-start.27) | collective-permute-done | bytes 516128 | tf_op jit(solution)/shard_map/ppermute | solution.py:607
  621.5 11.8 %mix_back.2 = (bf16[8,384,768]{2,1,0:T(8,128)(2,1)}, f32[448,768]{1,0:T(8,128)}, f32[1,768]{1,0:T(1,128)S(1)}, f32[1,768]{1,0:T(1,128)S(1)}, f32[4,8,576]{2,1,0:T(8,128)S(1)}) custom-call(s32[4]{0:T(128)S(1)} %pad_add_fusion.group_ids, f32[448,768]{1,0:T(8,128)} %get-tuple-element.139.grad_ref, f32[448,768]{1,0:T(8,128)} %copy-done.5, ...), custom_call_target="tpu_custom_call" | custom-call | flops 3170893824 | bytes 9437184 | tf_op jit(solution)/shard_map/mix_back/pallas_call | solution.py:149
  636.0 27.5 %mlp_back.3 = (bf16[448,192]{1,0:T(8,128)(2,1)S(1)}, bf16[448,192]{1,0:T(8,128)(2,1)S(1)}, bf16[448,192]{1,0:T(8,128)(2,1)S(1)}, bf16[448,192]{1,0:T(8,128)(2,1)...) custom-call(s32[4]{0:T(128)S(1)} %pad_add_fusion.group_ids, ...), custom_call_target="tpu_custom_call" | custom-call | flops 11626610688 | bytes 18874368 | tf_op jit(solution)/shard_map/mlp_back/pallas_call | solution.py:321
  666.6 20.6 %reduce-scatter.7.cloned.1.call-done.part_ref = bf16[384,768]{1,0:T(8,128)(2,1)} async-done(((bf16[3072,768]{1,0:T(8,128)(2,1)}), bf16[384,768]{1,0:T(8,128)(2,1)}) %reduce-scatter.7.cloned.1.call-update) | async-done | bytes 589840 | tf_op jit(solution)/shard_map/reduce_scatter | solution.py:629
  688.7 3.4 collective-permute-start.50
  693.2 3.4 collective-permute-start.47
  696.6 4.1 collective-permute-done.50
  700.7 13.2 %collective-permute-start.45 = (bf16[192,384]{1,0:T(8,128)(2,1)S(1)}, bf16[192,384]{1,0:T(8,128)(2,1)S(1)}, u32[]{:S(2)}, u32[]{:S(2)}) collective-permute-start(bf16[192,384]{1,0:T(8,128)(2,1)S(1)} %get-tuple-element.250), channel_id=1, source_target_pairs={{0,1},{1,0},{2,3},{3,2},{4,5},{5,4},{6,7},{7,6},{8,9},{9,8},{10,11... | collective-permute-start | bytes 442376 | tf_op jit(solution)/shard_map/ppermute | solution.py:607
  713.9 11.0 %collective-permute-done.49 = bf16[384,384]{1,0:T(8,128)(2,1)} collective-permute-done((bf16[384,384]{1,0:T(8,128)(2,1)S(1)}, bf16[384,384]{1,0:T(8,128)(2,1)}, u32[]{:S(2)}, u32[]{:S(2)}) %collective-permute-start.49) | collective-permute-done | bytes 294944 | tf_op jit(solution)/shard_map/ppermute | solution.py:607
  726.1 3.9 collective-permute-done.46
  731.0 36.6 %reduce-scatter.9.cloned.1.call-done.part_ref = bf16[768,768]{1,0:T(8,128)(2,1)} async-done(((bf16[6144,768]{1,0:T(8,128)(2,1)}), bf16[768,768]{1,0:T(8,128)(2,1)}) %reduce-scatter.9.cloned.1.call-update) | async-done | bytes 1179664 | tf_op jit(solution)/shard_map/reduce_scatter | solution.py:629
  773.3 5.0 collective-permute-done.30.refs_13_
  778.3 3.4 collective-permute-done.31.refs_14_
  781.8 4.5 collective-permute-done.32.refs_15_
  787.0 70.6 %attend_back.3 = (bf16[448,576]{1,0:T(8,128)(2,1)}, bf16[448,576]{1,0:T(8,128)(2,1)}, bf16[448,576]{1,0:T(8,128)(2,1)}, bf16[448,576]{1,0:T(8,128)(2,1)}, bf16[4...) custom-call(s32[8]{0:T(128)} %copy-done.12, ...), custom_call_target="tpu_custom_call" | custom-call | flops 12331253760 | bytes 8257536 | tf_op jit(solution)/shard_map/attend_back/pallas_call | solution.py:577
  865.1 11.7 %collective-permute-done.35.refs_1_ = bf16[448,576]{1,0:T(8,128)(2,1)S(1)} collective-permute-done((bf16[448,576]{1,0:T(8,128)(2,1)S(1)}, bf16[448,576]{1,0:T(8,128)(2,1)S(1)}, u32[]{:S(2)}, u32[]{:S(2)}) %collective-permute-start.35) | collective-permute-done | bytes 516128 | tf_op jit(solution)/shard_map/ppermute | solution.py:607
  876.9 12.8 %collective-permute-done.37.refs_2_ = bf16[448,576]{1,0:T(8,128)(2,1)S(1)} collective-permute-done((bf16[448,576]{1,0:T(8,128)(2,1)S(1)}, bf16[448,576]{1,0:T(8,128)(2,1)S(1)}, u32[]{:S(2)}, u32[]{:S(2)}) %collective-permute-start.37) | collective-permute-done | bytes 516128 | tf_op jit(solution)/shard_map/ppermute | solution.py:607
  890.5 11.5 %mix_back.3 = (bf16[8,384,768]{2,1,0:T(8,128)(2,1)}, f32[448,768]{1,0:T(8,128)}, f32[1,768]{1,0:T(1,128)S(1)}, f32[1,768]{1,0:T(1,128)S(1)}, f32[4,8,576]{2,1,0:T(8,128)S(1)}) custom-call(s32[4]{0:T(128)S(1)} %pad_add_fusion.group_ids, f32[448,768]{1,0:T(8,128)} %get-tuple-element.160.grad_ref, f32[448,768]{1,0:T(8,128)} %copy-done, ...), custom_call_target="tpu_custom_call" | custom-call | flops 3170893824 | bytes 9437184 | tf_op jit(solution)/shard_map/mix_back/pallas_call | solution.py:149
  908.9 7.4 collective-permute-done.56
  916.3 15.9 %collective-permute-done.55 = bf16[384,384]{1,0:T(8,128)(2,1)} collective-permute-done((bf16[384,384]{1,0:T(8,128)(2,1)S(1)}, bf16[384,384]{1,0:T(8,128)(2,1)}, u32[]{:S(2)}, u32[]{:S(2)}) %collective-permute-start.55) | collective-permute-done | bytes 294944 | tf_op jit(solution)/shard_map/ppermute | solution.py:607
  937.6 3.5 collective-permute-done.41
  946.6 3.4 collective-permute-done.43
  958.9 3.4 collective-permute-start.53
  963.6 4.0 collective-permute-done.53
  967.6 7.4 collective-permute-done.52
  975.7 13.2 %all-gather.33.cloned.1.call-done = bf16[3072,384]{1,0:T(8,128)(2,1)} async-done(((bf16[384,384]{1,0:T(8,128)(2,1)}), bf16[3072,384]{1,0:T(8,128)(2,1)}) %all-gather.33.cloned.1.call-update) | async-done | bytes 2359312 | tf_op jit(solution)/shard_map/all_gather | solution.py:632
  (564 shorter events, 225.0 us)
Async XLA Ops:
  7.2 74.9 %all-gather.19.cloned.1.call-start = ((), (), s32[]{:S(2)}) async-start(), calls=%async_computation.8 | async-start | bytes 2334720 | tf_op jit(solution)/shard_map/all_gather | solution.py:788
  37.3 85.8 %all-gather.21.cloned.1.call-start = ((), (), s32[]{:S(2)}) async-start(), calls=%async_computation.9 | async-start | bytes 5308416 | tf_op jit(solution)/shard_map/all_gather | solution.py:632
  85.2 135.1 %all-gather.25.cloned.1.call-start = ((), (), s32[]{:S(2)}) async-start(), calls=%async_computation.11 | async-start | bytes 2211840 | tf_op jit(solution)/shard_map/all_gather | solution.py:810
  131.0 15.5 %collective-permute-start = (bf16[448,576]{1,0:T(8,128)(2,1)}, bf16[448,576]{1,0:T(8,128)(2,1)}, u32[]{:S(2)}, u32[]{:S(2)}) collective-permute-start(bf16[448,576]{1,0:T(8,128)(2,1)} %get-tuple-element.114), channel_id=1, source_target_pairs={{0,8},{4,12},{8,0},{12,4},{16,24},{20,28},{24,16},{28,20},{1,9},{5... | collective-permute-start | bytes 1548296 | tf_op jit(solution)/shard_map/ppermute | solution.py:607
  146.4 116.2 %all-gather.27.cloned.1.call-start = ((), (), s32[]{:S(2)}) async-start(), calls=%async_computation.12 | async-start | bytes 5308416 | tf_op jit(solution)/shard_map/all_gather | solution.py:632
  146.5 26.9 %collective-permute-start.1 = (bf16[448,576]{1,0:T(8,128)(2,1)}, bf16[448,576]{1,0:T(8,128)(2,1)S(1)}, u32[]{:S(2)}, u32[]{:S(2)}) collective-permute-start(bf16[448,576]{1,0:T(8,128)(2,1)} %get-tuple-element.115), channel_id=1, source_target_pairs={{0,16},{4,20},{8,24},{12,28},{16,0},{20,4},{24,8},{28,12},{1,17},{... | collective-permute-start | bytes 1548296 | tf_op jit(solution)/shard_map/ppermute | solution.py:607
  147.8 25.6 %collective-permute-start.2 = (bf16[448,576]{1,0:T(8,128)(2,1)}, bf16[448,576]{1,0:T(8,128)(2,1)S(1)}, u32[]{:S(2)}, u32[]{:S(2)}) collective-permute-start(bf16[448,576]{1,0:T(8,128)(2,1)} %copy-done.29), channel_id=1, source_target_pairs={{0,24},{4,28},{8,16},{12,20},{16,8},{20,12},{24,0},{28,4},{1,25},{... | collective-permute-start | bytes 1548296 | tf_op jit(solution)/shard_map/ppermute | solution.py:607
  149.5 25.0 %collective-permute-start.3 = (bf16[448,576]{1,0:T(8,128)(2,1)S(1)}, bf16[448,576]{1,0:T(8,128)(2,1)}, u32[]{:S(2)}, u32[]{:S(2)}) collective-permute-start(bf16[448,576]{1,0:T(8,128)(2,1)S(1)} %get-tuple-element.113.refs_0_), channel_id=1, source_target_pairs={{0,4},{4,0},{8,12},{12,8},{16,20},{20,16},{24,28},{28,24},{1,5},{5... | collective-permute-start | bytes 1548296 | tf_op jit(solution)/shard_map/ppermute | solution.py:607
  149.5 25.0 %collective-permute-start.4 = (bf16[448,576]{1,0:T(8,128)(2,1)}, bf16[448,576]{1,0:T(8,128)(2,1)}, u32[]{:S(2)}, u32[]{:S(2)}) collective-permute-start(bf16[448,576]{1,0:T(8,128)(2,1)} %collective-permute-done.refs_1_), channel_id=1, source_target_pairs={{0,4},{4,0},{8,12},{12,8},{16,20},{20,16},{24,28},{28,24},{1,5},{5... | collective-permute-start | bytes 1548296 | tf_op jit(solution)/shard_map/ppermute | solution.py:607
  223.6 101.9 %all-gather.23.cloned.1.call-start = ((), (), s32[]{:S(2)}) async-start(), calls=%async_computation.10 | async-start | bytes 10616832 | tf_op jit(solution)/shard_map/all_gather | solution.py:632
  224.2 234.2 %all-gather.29.cloned.1.call-start = ((), (), s32[]{:S(2)}) async-start(), calls=%async_computation.13 | async-start | bytes 10616832 | tf_op jit(solution)/shard_map/all_gather | solution.py:632
  262.7 335.0 %reduce-scatter.5.cloned.1.call-start = ((), (), s32[]{:S(2)}) async-start(), calls=%async_computation.4 | async-start | bytes 10616832 | tf_op jit(solution)/shard_map/reduce_scatter | solution.py:629
  265.5 12.8 %collective-permute-start.8 = (bf16[448,192]{1,0:T(8,128)(2,1)S(1)}, bf16[448,192]{1,0:T(8,128)(2,1)S(1)}, u32[]{:S(2)}, u32[]{:S(2)}) collective-permute-start(bf16[448,192]{1,0:T(8,128)(2,1)S(1)} %copy-done.32), channel_id=1, source_target_pairs={{0,16},{4,20},{8,24},{12,28},{16,0},{20,4},{24,8},{28,12},{1,17},{... | collective-permute-start | bytes 516104 | tf_op jit(solution)/shard_map/ppermute | solution.py:607
  266.0 12.9 %collective-permute-start.9 = (bf16[448,192]{1,0:T(8,128)(2,1)S(1)}, bf16[448,192]{1,0:T(8,128)(2,1)S(1)}, u32[]{:S(2)}, u32[]{:S(2)}) collective-permute-start(bf16[448,192]{1,0:T(8,128)(2,1)S(1)} %copy-done.34), channel_id=1, source_target_pairs={{0,24},{4,28},{8,16},{12,20},{16,8},{20,12},{24,0},{28,4},{1,25},{... | collective-permute-start | bytes 516104 | tf_op jit(solution)/shard_map/ppermute | solution.py:607
  352.6 24.9 %collective-permute-start.10 = (bf16[448,576]{1,0:T(8,128)(2,1)S(1)}, bf16[448,576]{1,0:T(8,128)(2,1)S(1)}, u32[]{:S(2)}, u32[]{:S(2)}) collective-permute-start(bf16[448,576]{1,0:T(8,128)(2,1)S(1)} %get-tuple-element.129), channel_id=1, source_target_pairs={{0,8},{4,12},{8,0},{12,4},{16,24},{20,28},{24,16},{28,20},{1,9},{5... | collective-permute-start | bytes 1548296 | tf_op jit(solution)/shard_map/ppermute | solution.py:607
  354.0 28.4 %collective-permute-start.11 = (bf16[448,576]{1,0:T(8,128)(2,1)S(1)}, bf16[448,576]{1,0:T(8,128)(2,1)S(1)}, u32[]{:S(2)}, u32[]{:S(2)}) collective-permute-start(bf16[448,576]{1,0:T(8,128)(2,1)S(1)} %get-tuple-element.130), channel_id=1, source_target_pairs={{0,16},{4,20},{8,24},{12,28},{16,0},{20,4},{24,8},{28,12},{1,17},{... | collective-permute-start | bytes 1548296 | tf_op jit(solution)/shard_map/ppermute | solution.py:607
  354.7 46.8 %collective-permute-start.12 = (bf16[448,576]{1,0:T(8,128)(2,1)S(1)}, bf16[448,576]{1,0:T(8,128)(2,1)S(1)}, u32[]{:S(2)}, u32[]{:S(2)}) collective-permute-start(bf16[448,576]{1,0:T(8,128)(2,1)S(1)} %get-tuple-element.131), channel_id=1, source_target_pairs={{0,24},{4,28},{8,16},{12,20},{16,8},{20,12},{24,0},{28,4},{1,25},{... | collective-permute-start | bytes 1548296 | tf_op jit(solution)/shard_map/ppermute | solution.py:607
  356.1 45.5 %collective-permute-start.13 = (bf16[448,576]{1,0:T(8,128)(2,1)S(1)}, bf16[448,576]{1,0:T(8,128)(2,1)S(1)}, u32[]{:S(2)}, u32[]{:S(2)}) collective-permute-start(bf16[448,576]{1,0:T(8,128)(2,1)S(1)} %get-tuple-element.128.refs_0_), channel_id=1, source_target_pairs={{0,4},{4,0},{8,12},{12,8},{16,20},{20,16},{24,28},{28,24},{1,5},{5... | collective-permute-start | bytes 1548296 | tf_op jit(solution)/shard_map/ppermute | solution.py:607
  377.5 24.1 %collective-permute-start.14 = (bf16[448,576]{1,0:T(8,128)(2,1)S(1)}, bf16[448,576]{1,0:T(8,128)(2,1)S(1)}, u32[]{:S(2)}, u32[]{:S(2)}) collective-permute-start(bf16[448,576]{1,0:T(8,128)(2,1)S(1)} %collective-permute-done.10.refs_1_), channel_id=1, source_target_pairs={{0,4},{4,0},{8,12},{12,8},{16,20},{20,16},{24,28},{28,24},{1,5},{5... | collective-permute-start | bytes 1548296 | tf_op jit(solution)/shard_map/ppermute | solution.py:607
  382.5 19.1 %collective-permute-start.15 = (bf16[448,576]{1,0:T(8,128)(2,1)S(1)}, bf16[448,576]{1,0:T(8,128)(2,1)S(1)}, u32[]{:S(2)}, u32[]{:S(2)}) collective-permute-start(bf16[448,576]{1,0:T(8,128)(2,1)S(1)} %collective-permute-done.11.refs_2_), channel_id=1, source_target_pairs={{0,4},{4,0},{8,12},{12,8},{16,20},{20,16},{24,28},{28,24},{1,5},{5... | collective-permute-start | bytes 1548296 | tf_op jit(solution)/shard_map/ppermute | solution.py:607
  445.3 13.0 %collective-permute-start.18 = (bf16[448,192]{1,0:T(8,128)(2,1)S(1)}, bf16[448,192]{1,0:T(8,128)(2,1)}, u32[]{:S(2)}, u32[]{:S(2)}) collective-permute-start(bf16[448,192]{1,0:T(8,128)(2,1)S(1)} %get-tuple-element.134.refs_10_), channel_id=1, source_target_pairs={{0,16},{4,20},{8,24},{12,28},{16,0},{20,4},{24,8},{28,12},{1,17},{... | collective-permute-start | bytes 516104 | tf_op jit(solution)/shard_map/ppermute | solution.py:607
  447.6 10.7 %collective-permute-start.19 = (bf16[448,192]{1,0:T(8,128)(2,1)S(1)}, bf16[448,192]{1,0:T(8,128)(2,1)}, u32[]{:S(2)}, u32[]{:S(2)}) collective-permute-start(bf16[448,192]{1,0:T(8,128)(2,1)S(1)} %get-tuple-element.135.refs_11_), channel_id=1, source_target_pairs={{0,24},{4,28},{8,16},{12,20},{16,8},{20,12},{24,0},{28,4},{1,25},{... | collective-permute-start | bytes 516104 | tf_op jit(solution)/shard_map/ppermute | solution.py:607
  503.0 184.2 %reduce-scatter.7.cloned.1.call-start = ((), (), s32[]{:S(2)}) async-start(), calls=%async_computation.5 | async-start | bytes 5308416 | tf_op jit(solution)/shard_map/reduce_scatter | solution.py:629
  504.6 11.5 %collective-permute-start.21 = (bf16[448,192]{1,0:T(8,128)(2,1)S(1)}, bf16[448,192]{1,0:T(8,128)(2,1)S(1)}, u32[]{:S(2)}, u32[]{:S(2)}) collective-permute-start(bf16[448,192]{1,0:T(8,128)(2,1)S(1)} %get-tuple-element.144), channel_id=1, source_target_pairs={{0,16},{4,20},{8,24},{12,28},{16,0},{20,4},{24,8},{28,12},{1,17},{... | collective-permute-start | bytes 516104 | tf_op jit(solution)/shard_map/ppermute | solution.py:607
  505.2 10.8 %collective-permute-start.22 = (bf16[448,192]{1,0:T(8,128)(2,1)S(1)}, bf16[448,192]{1,0:T(8,128)(2,1)S(1)}, u32[]{:S(2)}, u32[]{:S(2)}) collective-permute-start(bf16[448,192]{1,0:T(8,128)(2,1)S(1)} %get-tuple-element.145), channel_id=1, source_target_pairs={{0,24},{4,28},{8,16},{12,20},{16,8},{20,12},{24,0},{28,4},{1,25},{... | collective-permute-start | bytes 516104 | tf_op jit(solution)/shard_map/ppermute | solution.py:607
  592.2 16.0 %collective-permute-start.25 = (bf16[448,576]{1,0:T(8,128)(2,1)}, bf16[448,576]{1,0:T(8,128)(2,1)S(1)}, u32[]{:S(2)}, u32[]{:S(2)}) collective-permute-start(bf16[448,576]{1,0:T(8,128)(2,1)} %add_convert_fusion.6), channel_id=1, source_target_pairs={{0,8},{4,12},{8,0},{12,4},{16,24},{20,28},{24,16},{28,20},{1,9},{5... | collective-permute-start | bytes 1548296 | tf_op jit(solution)/shard_map/ppermute | solution.py:607
  594.2 27.3 %collective-permute-start.27 = (bf16[448,576]{1,0:T(8,128)(2,1)}, bf16[448,576]{1,0:T(8,128)(2,1)}, u32[]{:S(2)}, u32[]{:S(2)}) collective-permute-start(bf16[448,576]{1,0:T(8,128)(2,1)} %add_convert_fusion.5), channel_id=1, source_target_pairs={{0,16},{4,20},{8,24},{12,28},{16,0},{20,4},{24,8},{28,12},{1,17},{... | collective-permute-start | bytes 1548296 | tf_op jit(solution)/shard_map/ppermute | solution.py:607
  596.5 25.0 %collective-permute-start.29 = (bf16[448,576]{1,0:T(8,128)(2,1)}, bf16[448,576]{1,0:T(8,128)(2,1)}, u32[]{:S(2)}, u32[]{:S(2)}) collective-permute-start(bf16[448,576]{1,0:T(8,128)(2,1)} %add_convert_fusion.4), channel_id=1, source_target_pairs={{0,24},{4,28},{8,16},{12,20},{16,8},{20,12},{24,0},{28,4},{1,25},{... | collective-permute-start | bytes 1548296 | tf_op jit(solution)/shard_map/ppermute | solution.py:607
  633.3 134.3 %reduce-scatter.9.cloned.1.call-start = ((), (), s32[]{:S(2)}) async-start(), calls=%async_computation.6 | async-start | bytes 10616832 | tf_op jit(solution)/shard_map/reduce_scatter | solution.py:629
  688.6 213.4 %all-gather.31.cloned.1.call-start = ((), (), s32[]{:S(2)}) async-start(), calls=%async_computation.14 | async-start | bytes 3981312 | tf_op jit(solution)/shard_map/all_gather | solution.py:632
  688.7 12.0 %collective-permute-start.50 = (bf16[384,384]{1,0:T(8,128)(2,1)S(1)}, bf16[384,384]{1,0:T(8,128)(2,1)}, u32[]{:S(2)}, u32[]{:S(2)}) collective-permute-start(bf16[384,384]{1,0:T(8,128)(2,1)S(1)} %get-tuple-element.245), channel_id=1, source_target_pairs={{0,3},{1,2},{2,1},{3,0},{4,7},{5,6},{6,5},{7,4},{8,11},{9,10},{10,... | collective-permute-start | bytes 884744 | tf_op jit(solution)/shard_map/ppermute | solution.py:607
  692.1 32.7 %collective-permute-start.49 = (bf16[384,384]{1,0:T(8,128)(2,1)S(1)}, bf16[384,384]{1,0:T(8,128)(2,1)}, u32[]{:S(2)}, u32[]{:S(2)}) collective-permute-start(bf16[384,384]{1,0:T(8,128)(2,1)S(1)} %get-tuple-element.246), channel_id=1, source_target_pairs={{0,2},{1,3},{2,0},{3,1},{4,6},{5,7},{6,4},{7,5},{8,10},{9,11},{10,... | collective-permute-start | bytes 884744 | tf_op jit(solution)/shard_map/ppermute | solution.py:607
  692.1 32.7 %collective-permute-start.48 = (bf16[384,384]{1,0:T(8,128)(2,1)S(1)}, bf16[384,384]{1,0:T(8,128)(2,1)}, u32[]{:S(2)}, u32[]{:S(2)}) collective-permute-start(bf16[384,384]{1,0:T(8,128)(2,1)S(1)} %get-tuple-element.244), channel_id=1, source_target_pairs={{0,1},{1,0},{2,3},{3,2},{4,5},{5,4},{6,7},{7,6},{8,9},{9,8},{10,11... | collective-permute-start | bytes 884744 | tf_op jit(solution)/shard_map/ppermute | solution.py:607
  693.2 32.9 %collective-permute-start.47 = (bf16[192,384]{1,0:T(8,128)(2,1)S(1)}, bf16[192,384]{1,0:T(8,128)(2,1)S(1)}, u32[]{:S(2)}, u32[]{:S(2)}) collective-permute-start(bf16[192,384]{1,0:T(8,128)(2,1)S(1)} %get-tuple-element.251), channel_id=1, source_target_pairs={{0,3},{1,2},{2,1},{3,0},{4,7},{5,6},{6,5},{7,4},{8,11},{9,10},{10,... | collective-permute-start | bytes 442376 | tf_op jit(solution)/shard_map/ppermute | solution.py:607
  696.6 33.4 %collective-permute-start.46 = (bf16[192,384]{1,0:T(8,128)(2,1)S(1)}, bf16[192,384]{1,0:T(8,128)(2,1)S(1)}, u32[]{:S(2)}, u32[]{:S(2)}) collective-permute-start(bf16[192,384]{1,0:T(8,128)(2,1)S(1)} %get-tuple-element.252), channel_id=1, source_target_pairs={{0,2},{1,3},{2,0},{3,1},{4,6},{5,7},{6,4},{7,5},{8,10},{9,11},{10,... | collective-permute-start | bytes 442376 | tf_op jit(solution)/shard_map/ppermute | solution.py:607
  700.7 29.4 %collective-permute-start.45 = (bf16[192,384]{1,0:T(8,128)(2,1)S(1)}, bf16[192,384]{1,0:T(8,128)(2,1)S(1)}, u32[]{:S(2)}, u32[]{:S(2)}) collective-permute-start(bf16[192,384]{1,0:T(8,128)(2,1)S(1)} %get-tuple-element.250), channel_id=1, source_target_pairs={{0,1},{1,0},{2,3},{3,2},{4,5},{5,4},{6,7},{7,6},{8,9},{9,8},{10,11... | collective-permute-start | bytes 442376 | tf_op jit(solution)/shard_map/ppermute | solution.py:607
  769.2 188.4 %reduce-scatter.11.cloned.1.call-start = ((), (), s32[]{:S(2)}) async-start(), calls=%async_computation.7 | async-start | bytes 5308416 | tf_op jit(solution)/shard_map/reduce_scatter | solution.py:629
  771.8 14.4 %collective-permute-start.32 = (bf16[448,192]{1,0:T(8,128)(2,1)S(1)}, bf16[448,192]{1,0:T(8,128)(2,1)S(1)}, u32[]{:S(2)}, u32[]{:S(2)}) collective-permute-start(bf16[448,192]{1,0:T(8,128)(2,1)S(1)} %get-tuple-element.166), channel_id=1, source_target_pairs={{0,24},{4,28},{8,16},{12,20},{16,8},{20,12},{24,0},{28,4},{1,25},{... | collective-permute-start | bytes 516104 | tf_op jit(solution)/shard_map/ppermute | solution.py:607
  861.0 15.9 %collective-permute-start.35 = (bf16[448,576]{1,0:T(8,128)(2,1)S(1)}, bf16[448,576]{1,0:T(8,128)(2,1)S(1)}, u32[]{:S(2)}, u32[]{:S(2)}) collective-permute-start(bf16[448,576]{1,0:T(8,128)(2,1)S(1)} %add_convert_fusion.2), channel_id=1, source_target_pairs={{0,8},{4,12},{8,0},{12,4},{16,24},{20,28},{24,16},{28,20},{1,9},{5... | collective-permute-start | bytes 1548296 | tf_op jit(solution)/shard_map/ppermute | solution.py:607
  862.0 27.7 %collective-permute-start.37 = (bf16[448,576]{1,0:T(8,128)(2,1)S(1)}, bf16[448,576]{1,0:T(8,128)(2,1)S(1)}, u32[]{:S(2)}, u32[]{:S(2)}) collective-permute-start(bf16[448,576]{1,0:T(8,128)(2,1)S(1)} %add_convert_fusion.1), channel_id=1, source_target_pairs={{0,16},{4,20},{8,24},{12,28},{16,0},{20,4},{24,8},{28,12},{1,17},{... | collective-permute-start | bytes 1548296 | tf_op jit(solution)/shard_map/ppermute | solution.py:607
  864.5 25.1 %collective-permute-start.39 = (bf16[448,576]{1,0:T(8,128)(2,1)S(1)}, bf16[448,576]{1,0:T(8,128)(2,1)S(1)}, u32[]{:S(2)}, u32[]{:S(2)}) collective-permute-start(bf16[448,576]{1,0:T(8,128)(2,1)S(1)} %add_convert_fusion), channel_id=1, source_target_pairs={{0,24},{4,28},{8,16},{12,20},{16,8},{20,12},{24,0},{28,4},{1,25},{... | collective-permute-start | bytes 1548296 | tf_op jit(solution)/shard_map/ppermute | solution.py:607
  902.0 86.9 %all-gather.33.cloned.1.call-start = ((), (), s32[]{:S(2)}) async-start(), calls=%async_computation.15 | async-start | bytes 2654208 | tf_op jit(solution)/shard_map/all_gather | solution.py:632
  904.1 12.2 %collective-permute-start.56 = (bf16[384,384]{1,0:T(8,128)(2,1)}, bf16[384,384]{1,0:T(8,128)(2,1)}, u32[]{:S(2)}, u32[]{:S(2)}) collective-permute-start(bf16[384,384]{1,0:T(8,128)(2,1)} %get-tuple-element.239), channel_id=1, source_target_pairs={{0,3},{1,2},{2,1},{3,0},{4,7},{5,6},{6,5},{7,4},{8,11},{9,10},{10,... | collective-permute-start | bytes 884744 | tf_op jit(solution)/shard_map/ppermute | solution.py:607
  907.2 25.0 %collective-permute-start.55 = (bf16[384,384]{1,0:T(8,128)(2,1)S(1)}, bf16[384,384]{1,0:T(8,128)(2,1)}, u32[]{:S(2)}, u32[]{:S(2)}) collective-permute-start(bf16[384,384]{1,0:T(8,128)(2,1)S(1)} %get-tuple-element.240), channel_id=1, source_target_pairs={{0,2},{1,3},{2,0},{3,1},{4,6},{5,7},{6,4},{7,5},{8,10},{9,11},{10,... | collective-permute-start | bytes 884744 | tf_op jit(solution)/shard_map/ppermute | solution.py:607
  907.2 25.0 %collective-permute-start.54 = (bf16[384,384]{1,0:T(8,128)(2,1)S(1)}, bf16[384,384]{1,0:T(8,128)(2,1)}, u32[]{:S(2)}, u32[]{:S(2)}) collective-permute-start(bf16[384,384]{1,0:T(8,128)(2,1)S(1)} %get-tuple-element.238), channel_id=1, source_target_pairs={{0,1},{1,0},{2,3},{3,2},{4,5},{5,4},{6,7},{7,6},{8,9},{9,8},{10,11... | collective-permute-start | bytes 884744 | tf_op jit(solution)/shard_map/ppermute | solution.py:607
  934.2 95.2 %all-gather.35.cloned.1.call-start = ((), (), s32[]{:S(2)}) async-start(), calls=%async_computation.16 | async-start | bytes 1327104 | tf_op jit(solution)/shard_map/all_gather | solution.py:632
  962.3 12.7 %collective-permute-start.52 = (bf16[192,384]{1,0:T(8,128)(2,1)S(1)}, bf16[192,384]{1,0:T(8,128)(2,1)S(1)}, u32[]{:S(2)}, u32[]{:S(2)}) collective-permute-start(bf16[192,384]{1,0:T(8,128)(2,1)S(1)} %get-tuple-element.249), channel_id=1, source_target_pairs={{0,2},{1,3},{2,0},{3,1},{4,6},{5,7},{6,4},{7,5},{8,10},{9,11},{10,... | collective-permute-start | bytes 442376 | tf_op jit(solution)/shard_map/ppermute | solution.py:607
  962.3 12.7 %collective-permute-start.51 = (bf16[192,384]{1,0:T(8,128)(2,1)S(1)}, bf16[192,384]{1,0:T(8,128)(2,1)S(1)}, u32[]{:S(2)}, u32[]{:S(2)}) collective-permute-start(bf16[192,384]{1,0:T(8,128)(2,1)S(1)} %get-tuple-element.247), channel_id=1, source_target_pairs={{0,1},{1,0},{2,3},{3,2},{4,5},{5,4},{6,7},{7,6},{8,9},{9,8},{10,11... | collective-permute-start | bytes 442376 | tf_op jit(solution)/shard_map/ppermute | solution.py:607
  (127 other events, 2187.8 us)
Sparse Core Ops, SparseCore 0:
  37.4 44.6 all-gather.18
  85.4 37.7 all-gather.20
  146.6 40.3 all-gather.24
  223.7 38.9 all-gather.26
  264.9 60.5 all-gather.22
  327.8 80.7 all-gather.28
  503.1 76.6 reduce-scatter.4
  633.5 53.7 reduce-scatter.6
  691.1 76.4 reduce-scatter.8
  769.5 37.1 all-gather.30
  902.1 55.3 reduce-scatter.10
  959.9 28.9 all-gather.32
  990.8 24.0 all-gather.34

commit v2 on v1

--- a/solution.py
+++ b/solution.py
@@ -169,24 +169,52 @@
         ),
         compiler_params=pltpu.CompilerParams(vmem_limit_bytes=52 << 20),
         cost_estimate=pl.CostEstimate(
-            flops=4 * rows * width * cols * GROUPS, bytes_accessed=4 * w.size, transcendentals=0
+            flops=12 * rows * width * cols * GROUPS, bytes_accessed=4 * w.size, transcendentals=0
         ),
         name="mix_back",
     )(group_ids, grad_after, state, gain, normed, w, dproj, *gms)
 
 
-def turn_weights_kernel(got_ref, attn_ref, feed_ref):
-    m = got_ref.shape[0]
+def turn_weights_kernel(w_at, *refs):
+    parts, (attn_ref, feed_ref, rows_ref) = split_refs(refs, len(refs) - 3, 3)
+    m = len(parts)
     attn_rows, width = attn_ref.shape
     part = width // m
-    turned = jnp.concatenate([got_ref[i, :part, :] for i in range(m)], 0)
+    up = feed_ref.shape[0] // 2
+    down = up // m
+    for k, ref in enumerate(parts):
+        rows_ref[w_at[0] ^ k] = ref[: part + down, :]
+    turned = jnp.concatenate([rows_ref[i, :part, :] for i in range(m)], 0)
     turned = turned.astype(F32).T.astype(BF)
     attn_ref[...] = turned[:attn_rows]
-    up = feed_ref.shape[0] // 2
     feed_ref[:up, :] = turned[attn_rows : attn_rows + up]
-    down = up // m
     for i in range(m):
-        feed_ref[up + i * down : up + (i + 1) * down, :] = got_ref[i, part : part + down, :]
+        feed_ref[up + i * down : up + (i + 1) * down, :] = rows_ref[i, part : part + down, :]
+
+
+def turn_weights(w_at, parts, attn_rows, feed_rows):
+    m = len(parts)
+    width = parts[0].shape[1]
+    rows = width // m + feed_rows // (2 * m)
+    return pl.pallas_call(
+        turn_weights_kernel,
+        out_shape=[
+            jax.ShapeDtypeStruct((attn_rows, width), BF),
+            jax.ShapeDtypeStruct((feed_rows, width), BF),
+        ],
+        grid_spec=pltpu.PrefetchScalarGridSpec(
+            num_scalar_prefetch=1,
+            grid=(1,),
+            in_specs=[whole(x.shape) for x in parts],
+            out_specs=[whole((attn_rows, width)), whole((feed_rows, width))],
+            scratch_shapes=[pltpu.VMEM((m, rows, width), BF)],
+        ),
+        compiler_params=pltpu.CompilerParams(vmem_limit_bytes=24 << 20),
+        cost_estimate=pl.CostEstimate(
+            flops=0, bytes_accessed=4 * m * rows * width, transcendentals=0
+        ),
+        name="turn_weights",
+    )(w_at, *parts)
 
 
 def turn_feed_kernel(part_ref, out_ref):
@@ -259,7 +287,7 @@
         ),
         compiler_params=pltpu.CompilerParams(vmem_limit_bytes=40 << 20),
         cost_estimate=pl.CostEstimate(
-            flops=2 * rows * (w.size + proj.size), bytes_accessed=2 * w.size, transcendentals=0
+            flops=6 * rows * (w.size + proj.size), bytes_accessed=2 * w.size, transcendentals=0
         ),
         name="mlp",
     )(group_ids, state, proj, bproj, gain, shift, w, bup, bdown, *atts)
@@ -352,7 +380,7 @@
         ),
         compiler_params=pltpu.CompilerParams(vmem_limit_bytes=48 << 20),
         cost_estimate=pl.CostEstimate(
-            flops=5 * rows * w.size + 4 * rows * proj.size, bytes_accessed=4 * w.size, transcendentals=0
+            flops=15 * rows * w.size + 12 * rows * proj.size, bytes_accessed=4 * w.size, transcendentals=0
         ),
         name="mlp_back",
     )(group_ids, grad, after, normed, gain, proj, w, bup, *atts)
@@ -474,7 +502,7 @@
         ),
         compiler_params=pltpu.CompilerParams(vmem_limit_bytes=48 << 20),
         cost_estimate=pl.CostEstimate(
-            flops=4 * q_blocks * k_blocks * blk * blk * width,
+            flops=40 * q_blocks * k_blocks * blk * blk * width,
             bytes_accessed=2 * len(mixed) * rows * cols,
             transcendentals=q_blocks * k_blocks * blk * blk * 2,
         ),
@@ -595,7 +623,7 @@
         ),
         compiler_params=pltpu.CompilerParams(vmem_limit_bytes=56 << 20),
         cost_estimate=pl.CostEstimate(
-            flops=10 * q_blocks * k_blocks * blk * blk * width,
+            flops=70 * q_blocks * k_blocks * blk * blk * width,
             bytes_accessed=4 * len(mixed) * rows * cols,
             transcendentals=q_blocks * k_blocks * blk * blk * 2,
         ),
@@ -694,7 +722,8 @@
     return jnp.concatenate(flat).reshape(extra, width)
 
 
-def unpack_small(place, got, small):
+def unpack_small(place, parts, small):
+    got = jnp.stack([pick(jnp.stack(parts), place.w ^ i) for i in range(place.m)])
     got = got.reshape(place.m, -1)
     out, at = [], 0
     for s in small:
@@ -705,23 +734,17 @@
     return out
 
 
-def gather_layer(place, got, ff):
-    width = got.shape[2]
-    attn_rows = 4 * width // place.n
-    attn, feed = turn(
-        turn_weights_kernel, got, (attn_rows, width), (2 * ff // place.n, width)
-    )
-    attn = place.gather_ctx(attn)
-    return attn, place.gather_ctx(after(feed, attn))
-
-
-def scatter_part(place, dw, ready, kernel, rows):
-    n, two, width = dw.shape
-    dw = dw.reshape(n * two, width)
-    if ready is not None:
-        dw = after(dw, ready)
-    part = place.scatter_ctx(dw)
-    return turn(kernel, part, (place.m, rows, two * width // (place.m * rows)))
+def spread_wt(place, x):
+    return [x] + [swap(x, "wt", place.m, k) for k in range(1, place.m)]
+
+
+def scatter_part(place, dw):
+    return place.scatter_ctx(dw.reshape(-1, dw.shape[2]))
+
+
+def own_part(place, part, kernel, rows):
+    turned = turn(kernel, part, (place.m, rows, part.size // (place.m * rows)))
+    return place.scatter_wt(turned).astype(BF)
 
 
 def unpack_feed(place, own, ff, width):
@@ -731,11 +754,6 @@
     up = up.reshape(n, rows, m, ff // (n * m)).transpose(1, 2, 0, 3).reshape(rows, ff)
     down = down.reshape(n, -1, ff // (n * m), down.shape[2]).transpose(0, 2, 1, 3)
     return up.astype(F32), down.reshape(ff // m, width).astype(F32)
-
-
-def unpack_both(place, joined, ff, width):
-    cut = width // place.m
-    return unpack_attn(place, joined[:, :cut], width) + unpack_feed(place, joined[:, cut:], ff, width)
 
 
 def unpack_attn(place, own, width):
@@ -784,11 +802,15 @@
 
     small = (ln1_gain, ln1_bias, query_bias, value_bias, out_bias, ln2_gain, ln2_bias, up_bias, down_bias)
     matrices = (qkv_weight, out_weight, up_weight, down_weight)
+    w_at = place.w.astype(jnp.int32).reshape(1)
+    attn_rows, feed_rows = 4 * width // n, 2 * ff // n
+    big_rows = width // m + ff // (n * m)
     first = jnp.concatenate([pack_layer(place, matrices, 0), pack_small(small, width)], 0)
-    got = lax.all_gather(first, "wt", axis=0, tiled=False)
-    big_rows = width // m + ff // (n * m)
-    vectors = unpack_small(place, got[:, big_rows:], small)
-    weights = [gather_layer(place, got, ff)]
+    parts = spread_wt(place, first)
+    vectors = unpack_small(place, [p[big_rows:] for p in parts], small)
+    attn, feed = turn_weights(w_at, parts, attn_rows, feed_rows)
+    attn = place.gather_ctx(attn)
+    weights = [(attn, place.gather_ctx(after(feed, attn)))]
     params = []
     for layer in range(LAYERS):
         v = [x[layer].reshape(1, -1) for x in vectors]
@@ -806,14 +828,16 @@
         *mixed, normed, proj = mix(group_ids, state, v[0], v[1], attn, bias)
         mixed = place.exchange(mixed)
         if layer + 1 < LAYERS:
-            send = after(pack_layer(place, matrices, layer + 1), mixed[1])
-            coming = lax.all_gather(send, "wt", axis=0, tiled=False)
+            send = after(pack_layer(place, matrices, layer + 1), parts[1])
+            parts = spread_wt(place, send)
         mixed = mixed + [
             swap(x, "ctx", n, j) for j in range(1, place.inner) for x in mixed
         ]
         *o, lse = attend(q_id, k_loc, mixed)
         if layer + 1 < LAYERS:
-            weights.append(gather_layer(place, after(coming, o[0]), ff))
+            next_attn, next_feed = turn_weights(w_at, parts, attn_rows, feed_rows)
+            next_attn = place.gather_ctx(after(next_attn, (feed, mixed)))
+            weights.append((next_attn, place.gather_ctx(after(next_feed, (next_attn, o[0])))))
         atts = place.exchange(o)
         mid, normed_two, new = mlp(
             group_ids, state, proj, v[4], v[5], v[6], feed, bup, v[8], atts
@@ -822,7 +846,7 @@
         state = new
     outputs = state.astype(BF)[None]
     gradient = cotangent[0].astype(F32)
-    shards, smalls, ready = [None] * LAYERS, [None] * LAYERS, None
+    shards, smalls, pending = [None] * LAYERS, [None] * LAYERS, []
     for layer in reversed(range(LAYERS)):
         attn, feed = weights[layer]
         v, bias, bup = params[layer]
@@ -830,11 +854,17 @@
         *datts, dfeed, dproj, gafter, dgain2, dshift2, dbup, dbdown, dbproj = mlp_back(
             group_ids, gradient, mid, normed_two, v[5], proj, feed, bup, atts
         )
-        part_feed = scatter_part(place, dfeed, ready, turn_feed_kernel, 2 * width // m)
+        part_feed = scatter_part(place, dfeed)
         do = place.exchange(datts)
-        dm = list(attend_back(q_id, k_loc, mixed, o, do, lse))
-        dm[0] = after(dm[0], part_feed)
-        own_feed = place.scatter_wt(part_feed).astype(BF)
+        dm = attend_back(q_id, k_loc, mixed, o, do, lse)
+        dm = list(dm)
+        if layer > 0:
+            dm[0] = after(dm[0], part_feed)
+        if layer + 1 < LAYERS:
+            part_attn = after(part_attn, dm[1])
+            pending.append(own_part(place, part_attn, turn_attn_kernel, width // m))
+        part_feed = after(part_feed, dm[1])
+        pending.append(own_part(place, part_feed, turn_feed_kernel, 2 * width // m))
         own = []
         for k in range(GROUPS):
             if place.inner == 1:
@@ -848,18 +878,10 @@
         dmix, gradient, dgain1, dshift1, dbias = mix_back(
             group_ids, gafter, before, v[0], normed, attn, dproj, gms
         )
-        if layer + 1 < LAYERS:
-            joined = place.gather_ctx(after(pending, part_feed))
-            shards[layer + 1] = unpack_both(place, joined, ff, width)
+        if layer == 0:
+            joined = place.gather_ctx(jnp.concatenate(pending, 0))
             dmix = after(dmix, joined)
-        part_attn = scatter_part(place, dmix, part_feed, turn_attn_kernel, width // m)
-        own_attn = place.scatter_wt(part_attn).astype(BF)
-        pending = jnp.concatenate([own_attn, own_feed], 0)
-        ready = part_attn
-        if layer == 0:
-            own_feed = place.gather_ctx(own_feed)
-            own_attn = place.gather_ctx(after(own_attn, own_feed))
-            shards[layer] = unpack_attn(place, own_attn, width) + unpack_feed(place, own_feed, ff, width)
+        part_attn = scatter_part(place, dmix)
         dbup = dbup[:, 0].reshape(n, m, ff // (n * m)).transpose(1, 0, 2)
         smalls[layer] = [
             x.reshape(-1)
@@ -868,6 +890,15 @@
                 dgain2, dshift2, dbup, dbdown,
             )
         ]
+    own_attn = place.gather_ctx(own_part(place, part_attn, turn_attn_kernel, width // m))
+    counts, at, owns = [p.shape[0] for p in pending], 0, []
+    for count in counts:
+        owns.append(joined[:, at : at + count])
+        at += count
+    for layer in range(LAYERS):
+        own_feed = owns[2 * (LAYERS - 1 - layer)]
+        part = own_attn if layer == 0 else owns[2 * (LAYERS - 1 - layer) + 1]
+        shards[layer] = unpack_attn(place, part, width) + unpack_feed(place, own_feed, ff, width)
     vec = reduce_small(place, smalls)
     mixw, projw, up, down = [jnp.stack([s[i] for s in shards]) for i in range(4)]
     return (

time: 1050 us -> 959 us (0.913)
  waiting for transfers between devices: 465 us -> 366 us
  starting transfers between devices: 69.6 us -> 86.4 us
    all_gather x7 -> x6, waiting for transfers between devices: 130 us -> 49.9 us  [gather_ctx(): return lax.all_gather(x, 'ctx', axis=0, tiled=False)]
    all_gather x2 -> x0, waiting for transfers between devices: 44.7 us -> none  [the longest x1 44.7 us: body(): got = lax.all_gather(first, 'wt', axis=0, tiled=False)]
    ppermute x57 -> x63, waiting for transfers between devices: 231 us -> 260 us  [swap(): return lax.ppermute(x, axis_name, [(i, i ^ k) for i in range(size)])]
    ppermute x57 -> x63, starting transfers between devices: 68.6 us -> 85.3 us  [swap(): return lax.ppermute(x, axis_name, [(i, i ^ k) for i in range(size)])]
    unnamed x250 -> x255, local copies, waits for them, and re-layouts: 51.7 us -> 46 us
  transfers between devices with their start and end apart: 70 -> 73, of which waited for: 43 -> 36; matrix products, arithmetic and copies ran while one was open for 7% -> 7% of each run, Pallas kernels for 27% -> 30%
where the time goes in v2:
time: 959 us; the launch traced here: 949 us
  waiting for transfers between devices  366 us (38%)
  Pallas kernels  337 us (35%)
  local copies, waits for them, and re-layouts  121 us (13%)
  starting transfers between devices  86.4 us (9%)
  other arithmetic  22.2 us (2%)
  between operations  16 us (2%)
    ppermute x63, waiting for transfers between devices, swap(): return lax.ppermute(x, axis_name, [(i, i ^ k) for i in range(size)])  260 us
    pallas_call x2, Pallas kernels, attend_back(): pl.pallas_call(attend_back_kernel, out_shape=[jax.ShapeDtypeStruct((rows,...  142 us
    ppermute x63, starting transfers between devices, swap(): return lax.ppermute(x, axis_name, [(i, i ^ k) for i in range(size)])  85.3 us
    pallas_call x2, Pallas kernels, attend(): pl.pallas_call(attend_kernel, out_shape=[jax.ShapeDtypeStruct((rows, widt...  81 us
    reduce_scatter x4, waiting for transfers between devices, scatter_ctx(): return lax.psum_scatter(x, 'ctx', scatter_dimension=0, tiled=True)  55.7 us
    pallas_call x2, Pallas kernels, mlp_back(): pl.pallas_call(mlp_back_kernel, out_shape=[jax.ShapeDtypeStruct((rows, gw...  53.8 us
    all_gather x6, waiting for transfers between devices, gather_ctx(): return lax.all_gather(x, 'ctx', axis=0, tiled=False)  49.9 us
    unnamed x255, local copies, waits for them, and re-layouts  46 us
  transfers between devices with their start and end apart: 73, of which 36 were waited for; matrix products, arithmetic and copies ran while one was open for 7% of the time, Pallas kernels for 30%

profile of v2, /device:TPU:0, one launch (start us, length us, event | category | flops | bytes accessed | tf_op | source)
XLA Modules:
  0.0 948.8 jit_solution(11188462813719720522)
XLA Ops:
  16.9 3.3 fusion.27
  35.7 5.1 collective-permute-start.2
  41.5 11.0 %collective-permute-done.2.refs_3_ = bf16[304,768]{1,0:T(8,128)(2,1)S(1)} collective-permute-done((bf16[304,768]{1,0:T(8,128)(2,1)S(1)}, bf16[304,768]{1,0:T(8,128)(2,1)S(1)}, u32[]{:S(2)}, u32[]{:S(2)}) %collective-permute-start.2) | collective-permute-done | bytes 466976 | tf_op jit(solution)/shard_map/ppermute | solution.py:635
  52.5 28.2 %collective-permute-done.1.refs_2_ = bf16[304,768]{1,0:T(8,128)(2,1)S(1)} collective-permute-done((bf16[304,768]{1,0:T(8,128)(2,1)S(1)}, bf16[304,768]{1,0:T(8,128)(2,1)S(1)}, u32[]{:S(2)}, u32[]{:S(2)}) %collective-permute-start.1) | collective-permute-done | bytes 466976 | tf_op jit(solution)/shard_map/ppermute | solution.py:635
  82.5 39.1 %all-gather.13.cloned.1.call-done = bf16[3072,768]{1,0:T(8,128)(2,1)} async-done(((bf16[384,768]{1,0:T(8,128)(2,1)}), bf16[3072,768]{1,0:T(8,128)(2,1)}) %all-gather.13.cloned.1.call-update) | async-done | bytes 4718608 | tf_op jit(solution)/shard_map/all_gather | solution.py:660
  137.5 3.1 mix.2
  148.3 16.9 %collective-permute-done.13.refs_1_ = bf16[288,768]{1,0:T(8,128)(2,1)S(1)} collective-permute-done((bf16[288,768]{1,0:T(8,128)(2,1)S(1)}, bf16[288,768]{1,0:T(8,128)(2,1)S(1)}, u32[]{:S(2)}, u32[]{:S(2)}) %collective-permute-start.13) | collective-permute-done | bytes 442400 | tf_op jit(solution)/shard_map/ppermute | solution.py:635
  167.4 18.0 %collective-permute-done.5.refs_3_ = bf16[448,576]{1,0:T(8,128)(2,1)S(1)} collective-permute-done((bf16[448,576]{1,0:T(8,128)(2,1)S(1)}, bf16[448,576]{1,0:T(8,128)(2,1)S(1)}, u32[]{:S(2)}, u32[]{:S(2)}) %collective-permute-start.5) | collective-permute-done | bytes 516128 | tf_op jit(solution)/shard_map/ppermute | solution.py:635
  186.2 3.3 collective-permute-start.15
  189.5 11.2 %collective-permute-done.15.refs_3_ = bf16[288,768]{1,0:T(8,128)(2,1)S(1)} collective-permute-done((bf16[288,768]{1,0:T(8,128)(2,1)S(1)}, bf16[288,768]{1,0:T(8,128)(2,1)S(1)}, u32[]{:S(2)}, u32[]{:S(2)}) %collective-permute-start.15) | collective-permute-done | bytes 442400 | tf_op jit(solution)/shard_map/ppermute | solution.py:635
  213.8 40.1 %attend.2 = (bf16[448,192]{1,0:T(8,128)(2,1)S(1)}, bf16[448,192]{1,0:T(8,128)(2,1)S(1)}, bf16[448,192]{1,0:T(8,128)(2,1)S(1)}, bf16[448,192]{1,0:T(8,128)(2,1)S(1)}, f32[8,8,224]{2,1,0:T(8,128)S(1)}) custom-call(s32[8]{0:T(128)S(1)} %pad_add_fusion.1.q_id, s32[16]{0:T(128)S(1)} %select_reduce_fusion.k_loc, bf16[448,576]{1,0:T(8,128)(2,1)S(1)} %get-tuple-element.110.refs_0_, ...), custom_call_target="tpu_custom_call" | custom-call | flops 49325015040 | bytes 4128768 | tf_op jit(solution)/shard_map/attend/pallas_call | solution.py:487
  260.6 4.3 collective-permute-done.10.refs_1_
  264.9 3.9 collective-permute-done.11.refs_2_
  271.2 12.9 %mlp.2 = (f32[448,768]{1,0:T(8,128)S(1)}, bf16[448,768]{1,0:T(8,128)(2,1)S(1)}, f32[448,768]{1,0:T(8,128)S(1)}) custom-call(s32[4]{0:T(128)S(1)} %pad_add_fusion.group_ids, f32[448,768]{1,0:T(8,128)S(1)} %bitcast_convert_fusion.1.state_ref, bf16[4,192,768]{2,1,0:T(8,128)(2,1)S(1)} %copy-done.14, f32[1,768]{1,0:T(1,128)S(1)} %slice.294.bproj_ref, ...), custom_call_target="tpu_custom_call" | custom-call | flops 14269022208 | bytes 9437184 | tf_op jit(solution)/shard_map/mlp/pallas_call | solution.py:273
  285.0 3.2 mix.3
  292.5 21.6 %collective-permute-done.16.refs_1_ = bf16[448,576]{1,0:T(8,128)(2,1)S(1)} collective-permute-done((bf16[448,576]{1,0:T(8,128)(2,1)S(1)}, bf16[448,576]{1,0:T(8,128)(2,1)S(1)}, u32[]{:S(2)}, u32[]{:S(2)}) %collective-permute-start.16) | collective-permute-done | bytes 516128 | tf_op jit(solution)/shard_map/ppermute | solution.py:635
  316.4 20.5 %collective-permute-done.18.refs_3_ = bf16[448,576]{1,0:T(8,128)(2,1)S(1)} collective-permute-done((bf16[448,576]{1,0:T(8,128)(2,1)S(1)}, bf16[448,576]{1,0:T(8,128)(2,1)S(1)}, u32[]{:S(2)}, u32[]{:S(2)}) %collective-permute-start.18) | collective-permute-done | bytes 516128 | tf_op jit(solution)/shard_map/ppermute | solution.py:635
  338.9 40.8 %attend.3 = (bf16[448,192]{1,0:T(8,128)(2,1)S(1)}, bf16[448,192]{1,0:T(8,128)(2,1)}, bf16[448,192]{1,0:T(8,128)(2,1)}, bf16[448,192]{1,0:T(8,128)(2,1)}, f32[8,8,224]{2,1,0:T(8,128)S(1)}) custom-call(s32[8]{0:T(128)S(1)} %pad_add_fusion.1.q_id, s32[16]{0:T(128)S(1)} %select_reduce_fusion.k_loc, bf16[448,576]{1,0:T(8,128)(2,1)S(1)} %get-tuple-element.125.refs_0_, ...), custom_call_target="tpu_custom_call" | custom-call | flops 49325015040 | bytes 4128768 | tf_op jit(solution)/shard_map/attend/pallas_call | solution.py:487
  385.6 3.5 collective-permute-done.23.refs_1_
  389.1 4.8 collective-permute-done.24.refs_2_
  394.9 12.7 %mlp.3 = (f32[448,768]{1,0:T(8,128)S(1)}, bf16[448,768]{1,0:T(8,128)(2,1)S(1)}, f32[448,768]{1,0:T(8,128)S(1)}) custom-call(s32[4]{0:T(128)S(1)} %pad_add_fusion.group_ids, f32[448,768]{1,0:T(8,128)S(1)} %get-tuple-element.118.state_ref, bf16[4,192,768]{2,1,0:T(8,128)(2,1)S(1)} %get-tuple-element.122.proj_ref, f32[1,768]{1,0:T(1,128)S(1)} %slice.320.bproj_ref, ...), custom_call_target="tpu_custom_call" | custom-call | flops 14269022208 | bytes 9437184 | tf_op jit(solution)/shard_map/mlp/pallas_call | solution.py:273
  409.7 26.9 %mlp_back.2 = (bf16[448,192]{1,0:T(8,128)(2,1)S(1)}, bf16[448,192]{1,0:T(8,128)(2,1)S(1)}, bf16[448,192]{1,0:T(8,128)(2,1)S(1)}, bf16[448,192]{1,0:T(8,128)(2,1)...) custom-call(s32[4]{0:T(128)S(1)} %pad_add_fusion.group_ids, ...), custom_call_target="tpu_custom_call" | custom-call | flops 34879832064 | bytes 18874368 | tf_op jit(solution)/shard_map/mlp_back/pallas_call | solution.py:349
  441.8 5.1 collective-permute-done.26.refs_13_
  446.9 3.9 collective-permute-done.27.refs_14_
  451.6 71.1 %attend_back.2 = (bf16[448,576]{1,0:T(8,128)(2,1)}, bf16[448,576]{1,0:T(8,128)(2,1)}, bf16[448,576]{1,0:T(8,128)(2,1)}, bf16[448,576]{1,0:T(8,128)(2,1)}, bf16[4...) custom-call(s32[8]{0:T(128)} %copy-done.12, ...), custom_call_target="tpu_custom_call" | custom-call | flops 86318776320 | bytes 8257536 | tf_op jit(solution)/shard_map/attend_back/pallas_call | solution.py:605
  532.6 10.4 %collective-permute-done.31.refs_1_ = bf16[448,576]{1,0:T(8,128)(2,1)S(1)} collective-permute-done((bf16[448,576]{1,0:T(8,128)(2,1)}, bf16[448,576]{1,0:T(8,128)(2,1)S(1)}, u32[]{:S(2)}, u32[]{:S(2)}) %collective-permute-start.31) | collective-permute-done | bytes 516128 | tf_op jit(solution)/shard_map/ppermute | solution.py:635
  543.0 12.9 %collective-permute-done.33.refs_2_ = bf16[448,576]{1,0:T(8,128)(2,1)S(1)} collective-permute-done((bf16[448,576]{1,0:T(8,128)(2,1)}, bf16[448,576]{1,0:T(8,128)(2,1)S(1)}, u32[]{:S(2)}, u32[]{:S(2)}) %collective-permute-start.33) | collective-permute-done | bytes 516128 | tf_op jit(solution)/shard_map/ppermute | solution.py:635
  556.8 11.7 %mix_back.2 = (bf16[8,384,768]{2,1,0:T(8,128)(2,1)}, f32[448,768]{1,0:T(8,128)}, f32[1,768]{1,0:T(1,128)S(1)}, f32[1,768]{1,0:T(1,128)S(1)}, f32[4,8,576]{2,1,0:T(8,128)S(1)}) custom-call(s32[4]{0:T(128)S(1)} %pad_add_fusion.group_ids, f32[448,768]{1,0:T(8,128)} %get-tuple-element.136.grad_ref, f32[448,768]{1,0:T(8,128)} %copy-done.3, ...), custom_call_target="tpu_custom_call" | custom-call | flops 9512681472 | bytes 9437184 | tf_op jit(solution)/shard_map/mix_back/pallas_call | solution.py:149
  571.1 26.9 %mlp_back.3 = (bf16[448,192]{1,0:T(8,128)(2,1)S(1)}, bf16[448,192]{1,0:T(8,128)(2,1)S(1)}, bf16[448,192]{1,0:T(8,128)(2,1)S(1)}, bf16[448,192]{1,0:T(8,128)(2,1)...) custom-call(s32[4]{0:T(128)S(1)} %pad_add_fusion.group_ids, ...), custom_call_target="tpu_custom_call" | custom-call | flops 34879832064 | bytes 18874368 | tf_op jit(solution)/shard_map/mlp_back/pallas_call | solution.py:349
  604.4 3.4 collective-permute-start.53
  607.8 9.3 collective-permute-start.52
  617.1 4.6 collective-permute-start.51
  623.3 70.9 %attend_back.3 = (bf16[448,576]{1,0:T(8,128)(2,1)}, bf16[448,576]{1,0:T(8,128)(2,1)}, bf16[448,576]{1,0:T(8,128)(2,1)}, bf16[448,576]{1,0:T(8,128)(2,1)}, bf16[4...) custom-call(s32[8]{0:T(128)} %copy-done.12, ...), custom_call_target="tpu_custom_call" | custom-call | flops 86318776320 | bytes 8257536 | tf_op jit(solution)/shard_map/attend_back/pallas_call | solution.py:605
  698.4 3.4 collective-permute-start.55
  701.9 19.2 %reduce-scatter.9.cloned.1.call-done.part_ref = bf16[768,768]{1,0:T(8,128)(2,1)} async-done(((bf16[6144,768]{1,0:T(8,128)(2,1)}), bf16[768,768]{1,0:T(8,128)(2,1)}) %reduce-scatter.9.cloned.1.call-update) | async-done | bytes 1179664 | tf_op jit(solution)/shard_map/reduce_scatter | solution.py:657
  730.9 7.1 collective-permute-done.59
  738.0 14.4 %collective-permute-done.58 = bf16[384,384]{1,0:T(8,128)(2,1)S(1)} collective-permute-done((bf16[384,384]{1,0:T(8,128)(2,1)S(1)}, bf16[384,384]{1,0:T(8,128)(2,1)S(1)}, u32[]{:S(2)}, u32[]{:S(2)}) %collective-permute-start.58) | collective-permute-done | bytes 294944 | tf_op jit(solution)/shard_map/ppermute | solution.py:635
  761.1 18.9 %collective-permute-done.41.refs_1_ = bf16[448,576]{1,0:T(8,128)(2,1)S(1)} collective-permute-done((bf16[448,576]{1,0:T(8,128)(2,1)S(1)}, bf16[448,576]{1,0:T(8,128)(2,1)S(1)}, u32[]{:S(2)}, u32[]{:S(2)}) %collective-permute-start.41) | collective-permute-done | bytes 516128 | tf_op jit(solution)/shard_map/ppermute | solution.py:635
  780.0 13.1 %collective-permute-done.43.refs_2_ = bf16[448,576]{1,0:T(8,128)(2,1)S(1)} collective-permute-done((bf16[448,576]{1,0:T(8,128)(2,1)S(1)}, bf16[448,576]{1,0:T(8,128)(2,1)S(1)}, u32[]{:S(2)}, u32[]{:S(2)}) %collective-permute-start.43) | collective-permute-done | bytes 516128 | tf_op jit(solution)/shard_map/ppermute | solution.py:635
  793.9 12.4 %mix_back.3 = (bf16[8,384,768]{2,1,0:T(8,128)(2,1)}, f32[448,768]{1,0:T(8,128)}, f32[1,768]{1,0:T(1,128)S(1)}, f32[1,768]{1,0:T(1,128)S(1)}, f32[4,8,576]{2,1,0:T(8,128)S(1)}) custom-call(s32[4]{0:T(128)S(1)} %pad_add_fusion.group_ids, f32[448,768]{1,0:T(8,128)} %get-tuple-element.157.grad_ref, f32[448,768]{1,0:T(8,128)} %copy-done, ...), custom_call_target="tpu_custom_call" | custom-call | flops 9512681472 | bytes 9437184 | tf_op jit(solution)/shard_map/mix_back/pallas_call | solution.py:149
  806.4 10.7 %all-gather.21.cloned.1.call-done = bf16[7680,384]{1,0:T(8,128)(2,1)} async-done(((bf16[960,384]{1,0:T(8,128)(2,1)}), bf16[7680,384]{1,0:T(8,128)(2,1)}) %all-gather.21.cloned.1.call-update) | async-done | bytes 5898256 | tf_op jit(solution)/shard_map/all_gather | solution.py:660
  825.7 3.1 collective-permute-done.48
  838.9 36.5 %reduce-scatter.11.cloned.1.call-done.part_ref = bf16[384,768]{1,0:T(8,128)(2,1)} async-done(((bf16[3072,768]{1,0:T(8,128)(2,1)}), bf16[384,768]{1,0:T(8,128)(2,1)}) %reduce-scatter.11.cloned.1.call-update) | async-done | bytes 589840 | tf_op jit(solution)/shard_map/reduce_scatter | solution.py:657
  876.8 3.4 collective-permute-start.62
  881.4 4.0 collective-permute-done.62
  885.4 7.4 collective-permute-done.61
  906.7 4.3 fusion.25
  916.9 3.3 convert_element_type.443
  (578 shorter events, 206.9 us)
Async XLA Ops:
  7.2 114.5 %all-gather.13.cloned.1.call-start = ((), (), s32[]{:S(2)}) async-start(), calls=%async_computation.8 | async-start | bytes 5308416 | tf_op jit(solution)/shard_map/all_gather | solution.py:660
  35.7 16.8 %collective-permute-start.2 = (bf16[304,768]{1,0:T(8,128)(2,1)S(1)}, bf16[304,768]{1,0:T(8,128)(2,1)S(1)}, u32[]{:S(2)}, u32[]{:S(2)}) collective-permute-start(bf16[304,768]{1,0:T(8,128)(2,1)S(1)} %pad_maximum_fusion.1.refs_0_), channel_id=1, source_target_pairs={{0,3},{1,2},{2,1},{3,0},{4,7},{5,6},{6,5},{7,4},{8,11},{9,10},{10,... | collective-permute-start | bytes 1400840 | tf_op jit(solution)/shard_map/ppermute | solution.py:635
  40.8 39.9 %collective-permute-start.1 = (bf16[304,768]{1,0:T(8,128)(2,1)S(1)}, bf16[304,768]{1,0:T(8,128)(2,1)S(1)}, u32[]{:S(2)}, u32[]{:S(2)}) collective-permute-start(bf16[304,768]{1,0:T(8,128)(2,1)S(1)} %pad_maximum_fusion.1.refs_0_), channel_id=1, source_target_pairs={{0,2},{1,3},{2,0},{3,1},{4,6},{5,7},{6,4},{7,5},{8,10},{9,11},{10,... | collective-permute-start | bytes 1400840 | tf_op jit(solution)/shard_map/ppermute | solution.py:635
  40.8 39.9 %collective-permute-start = (bf16[304,768]{1,0:T(8,128)(2,1)S(1)}, bf16[304,768]{1,0:T(8,128)(2,1)S(1)}, u32[]{:S(2)}, u32[]{:S(2)}) collective-permute-start(bf16[304,768]{1,0:T(8,128)(2,1)S(1)} %pad_maximum_fusion.1.refs_0_), channel_id=1, source_target_pairs={{0,1},{1,0},{2,3},{3,2},{4,5},{5,4},{6,7},{7,6},{8,9},{9,8},{10,11... | collective-permute-start | bytes 1400840 | tf_op jit(solution)/shard_map/ppermute | solution.py:635
  82.4 123.2 %all-gather.15.cloned.1.call-start = ((), (), s32[]{:S(2)}) async-start(), calls=%async_computation.9 | async-start | bytes 10616832 | tf_op jit(solution)/shard_map/all_gather | solution.py:660
  121.7 133.0 %all-gather.17.cloned.1.call-start = ((), (), s32[]{:S(2)}) async-start(), calls=%async_computation.10 | async-start | bytes 5308416 | tf_op jit(solution)/shard_map/all_gather | solution.py:660
  140.7 24.5 %collective-permute-start.3 = (bf16[448,576]{1,0:T(8,128)(2,1)S(1)}, bf16[448,576]{1,0:T(8,128)(2,1)S(1)}, u32[]{:S(2)}, u32[]{:S(2)}) collective-permute-start(bf16[448,576]{1,0:T(8,128)(2,1)S(1)} %get-tuple-element.111), channel_id=1, source_target_pairs={{0,8},{4,12},{8,0},{12,4},{16,24},{20,28},{24,16},{28,20},{1,9},{5... | collective-permute-start | bytes 1548296 | tf_op jit(solution)/shard_map/ppermute | solution.py:635
  142.2 24.3 %collective-permute-start.4 = (bf16[448,576]{1,0:T(8,128)(2,1)S(1)}, bf16[448,576]{1,0:T(8,128)(2,1)S(1)}, u32[]{:S(2)}, u32[]{:S(2)}) collective-permute-start(bf16[448,576]{1,0:T(8,128)(2,1)S(1)} %get-tuple-element.112), channel_id=1, source_target_pairs={{0,16},{4,20},{8,24},{12,28},{16,0},{20,4},{24,8},{28,12},{1,17},{... | collective-permute-start | bytes 1548296 | tf_op jit(solution)/shard_map/ppermute | solution.py:635
  142.8 42.5 %collective-permute-start.5 = (bf16[448,576]{1,0:T(8,128)(2,1)S(1)}, bf16[448,576]{1,0:T(8,128)(2,1)S(1)}, u32[]{:S(2)}, u32[]{:S(2)}) collective-permute-start(bf16[448,576]{1,0:T(8,128)(2,1)S(1)} %get-tuple-element.113), channel_id=1, source_target_pairs={{0,24},{4,28},{8,16},{12,20},{16,8},{20,12},{24,0},{28,4},{1,25},{... | collective-permute-start | bytes 1548296 | tf_op jit(solution)/shard_map/ppermute | solution.py:635
  144.4 20.8 %collective-permute-start.13 = (bf16[288,768]{1,0:T(8,128)(2,1)S(1)}, bf16[288,768]{1,0:T(8,128)(2,1)S(1)}, u32[]{:S(2)}, u32[]{:S(2)}) collective-permute-start(bf16[288,768]{1,0:T(8,128)(2,1)S(1)} %pad_maximum_fusion.2.refs_0_), channel_id=1, source_target_pairs={{0,1},{1,0},{2,3},{3,2},{4,5},{5,4},{6,7},{7,6},{8,9},{9,8},{10,11... | collective-permute-start | bytes 1327112 | tf_op jit(solution)/shard_map/ppermute | solution.py:635
  145.9 40.3 %collective-permute-start.14 = (bf16[288,768]{1,0:T(8,128)(2,1)S(1)}, bf16[288,768]{1,0:T(8,128)(2,1)S(1)}, u32[]{:S(2)}, u32[]{:S(2)}) collective-permute-start(bf16[288,768]{1,0:T(8,128)(2,1)S(1)} %pad_maximum_fusion.2.refs_0_), channel_id=1, source_target_pairs={{0,2},{1,3},{2,0},{3,1},{4,6},{5,7},{6,4},{7,5},{8,10},{9,11},{10,... | collective-permute-start | bytes 1327112 | tf_op jit(solution)/shard_map/ppermute | solution.py:635
  165.2 37.2 %collective-permute-start.6 = (bf16[448,576]{1,0:T(8,128)(2,1)S(1)}, bf16[448,576]{1,0:T(8,128)(2,1)S(1)}, u32[]{:S(2)}, u32[]{:S(2)}) collective-permute-start(bf16[448,576]{1,0:T(8,128)(2,1)S(1)} %get-tuple-element.110.refs_0_), channel_id=1, source_target_pairs={{0,4},{4,0},{8,12},{12,8},{16,20},{20,16},{24,28},{28,24},{1,5},{5... | collective-permute-start | bytes 1548296 | tf_op jit(solution)/shard_map/ppermute | solution.py:635
  165.2 38.0 %collective-permute-start.7 = (bf16[448,576]{1,0:T(8,128)(2,1)S(1)}, bf16[448,576]{1,0:T(8,128)(2,1)S(1)}, u32[]{:S(2)}, u32[]{:S(2)}) collective-permute-start(bf16[448,576]{1,0:T(8,128)(2,1)S(1)} %collective-permute-done.3.refs_1_), channel_id=1, source_target_pairs={{0,4},{4,0},{8,12},{12,8},{16,20},{20,16},{24,28},{28,24},{1,5},{5... | collective-permute-start | bytes 1548296 | tf_op jit(solution)/shard_map/ppermute | solution.py:635
  166.5 37.5 %collective-permute-start.8 = (bf16[448,576]{1,0:T(8,128)(2,1)S(1)}, bf16[448,576]{1,0:T(8,128)(2,1)S(1)}, u32[]{:S(2)}, u32[]{:S(2)}) collective-permute-start(bf16[448,576]{1,0:T(8,128)(2,1)S(1)} %collective-permute-done.4.refs_2_), channel_id=1, source_target_pairs={{0,4},{4,0},{8,12},{12,8},{16,20},{20,16},{24,28},{28,24},{1,5},{5... | collective-permute-start | bytes 1548296 | tf_op jit(solution)/shard_map/ppermute | solution.py:635
  185.3 19.5 %collective-permute-start.9 = (bf16[448,576]{1,0:T(8,128)(2,1)S(1)}, bf16[448,576]{1,0:T(8,128)(2,1)S(1)}, u32[]{:S(2)}, u32[]{:S(2)}) collective-permute-start(bf16[448,576]{1,0:T(8,128)(2,1)S(1)} %collective-permute-done.5.refs_3_), channel_id=1, source_target_pairs={{0,4},{4,0},{8,12},{12,8},{16,20},{20,16},{24,28},{28,24},{1,5},{5... | collective-permute-start | bytes 1548296 | tf_op jit(solution)/shard_map/ppermute | solution.py:635
  186.2 14.5 %collective-permute-start.15 = (bf16[288,768]{1,0:T(8,128)(2,1)S(1)}, bf16[288,768]{1,0:T(8,128)(2,1)S(1)}, u32[]{:S(2)}, u32[]{:S(2)}) collective-permute-start(bf16[288,768]{1,0:T(8,128)(2,1)S(1)} %pad_maximum_fusion.2.refs_0_), channel_id=1, source_target_pairs={{0,3},{1,2},{2,1},{3,0},{4,7},{5,6},{6,5},{7,4},{8,11},{9,10},{10,... | collective-permute-start | bytes 1327112 | tf_op jit(solution)/shard_map/ppermute | solution.py:635
  205.7 188.2 %all-gather.19.cloned.1.call-start = ((), (), s32[]{:S(2)}) async-start(), calls=%async_computation.11 | async-start | bytes 10616832 | tf_op jit(solution)/shard_map/all_gather | solution.py:660
  254.7 277.8 %reduce-scatter.5.cloned.1.call-start = ((), (), s32[]{:S(2)}) async-start(), calls=%async_computation.4 | async-start | bytes 10616832 | tf_op jit(solution)/shard_map/reduce_scatter | solution.py:657
  289.0 25.1 %collective-permute-start.16 = (bf16[448,576]{1,0:T(8,128)(2,1)S(1)}, bf16[448,576]{1,0:T(8,128)(2,1)S(1)}, u32[]{:S(2)}, u32[]{:S(2)}) collective-permute-start(bf16[448,576]{1,0:T(8,128)(2,1)S(1)} %get-tuple-element.126), channel_id=1, source_target_pairs={{0,8},{4,12},{8,0},{12,4},{16,24},{20,28},{24,16},{28,20},{1,9},{5... | collective-permute-start | bytes 1548296 | tf_op jit(solution)/shard_map/ppermute | solution.py:635
  290.6 25.8 %collective-permute-start.17 = (bf16[448,576]{1,0:T(8,128)(2,1)S(1)}, bf16[448,576]{1,0:T(8,128)(2,1)S(1)}, u32[]{:S(2)}, u32[]{:S(2)}) collective-permute-start(bf16[448,576]{1,0:T(8,128)(2,1)S(1)} %get-tuple-element.127), channel_id=1, source_target_pairs={{0,16},{4,20},{8,24},{12,28},{16,0},{20,4},{24,8},{28,12},{1,17},{... | collective-permute-start | bytes 1548296 | tf_op jit(solution)/shard_map/ppermute | solution.py:635
  291.3 45.7 %collective-permute-start.18 = (bf16[448,576]{1,0:T(8,128)(2,1)S(1)}, bf16[448,576]{1,0:T(8,128)(2,1)S(1)}, u32[]{:S(2)}, u32[]{:S(2)}) collective-permute-start(bf16[448,576]{1,0:T(8,128)(2,1)S(1)} %get-tuple-element.128), channel_id=1, source_target_pairs={{0,24},{4,28},{8,16},{12,20},{16,8},{20,12},{24,0},{28,4},{1,25},{... | collective-permute-start | bytes 1548296 | tf_op jit(solution)/shard_map/ppermute | solution.py:635
  292.5 44.4 %collective-permute-start.19 = (bf16[448,576]{1,0:T(8,128)(2,1)S(1)}, bf16[448,576]{1,0:T(8,128)(2,1)S(1)}, u32[]{:S(2)}, u32[]{:S(2)}) collective-permute-start(bf16[448,576]{1,0:T(8,128)(2,1)S(1)} %get-tuple-element.125.refs_0_), channel_id=1, source_target_pairs={{0,4},{4,0},{8,12},{12,8},{16,20},{20,16},{24,28},{28,24},{1,5},{5... | collective-permute-start | bytes 1548296 | tf_op jit(solution)/shard_map/ppermute | solution.py:635
  314.1 22.8 %collective-permute-start.20 = (bf16[448,576]{1,0:T(8,128)(2,1)S(1)}, bf16[448,576]{1,0:T(8,128)(2,1)S(1)}, u32[]{:S(2)}, u32[]{:S(2)}) collective-permute-start(bf16[448,576]{1,0:T(8,128)(2,1)S(1)} %collective-permute-done.16.refs_1_), channel_id=1, source_target_pairs={{0,4},{4,0},{8,12},{12,8},{16,20},{20,16},{24,28},{28,24},{1,5},{5... | collective-permute-start | bytes 1548296 | tf_op jit(solution)/shard_map/ppermute | solution.py:635
  316.4 20.6 %collective-permute-start.21 = (bf16[448,576]{1,0:T(8,128)(2,1)S(1)}, bf16[448,576]{1,0:T(8,128)(2,1)S(1)}, u32[]{:S(2)}, u32[]{:S(2)}) collective-permute-start(bf16[448,576]{1,0:T(8,128)(2,1)S(1)} %collective-permute-done.17.refs_2_), channel_id=1, source_target_pairs={{0,4},{4,0},{8,12},{12,8},{16,20},{20,16},{24,28},{28,24},{1,5},{5... | collective-permute-start | bytes 1548296 | tf_op jit(solution)/shard_map/ppermute | solution.py:635
  438.3 255.9 %reduce-scatter.7.cloned.1.call-start = ((), (), s32[]{:S(2)}) async-start(), calls=%async_computation.5 | async-start | bytes 5308416 | tf_op jit(solution)/shard_map/reduce_scatter | solution.py:657
  527.0 16.0 %collective-permute-start.31 = (bf16[448,576]{1,0:T(8,128)(2,1)}, bf16[448,576]{1,0:T(8,128)(2,1)S(1)}, u32[]{:S(2)}, u32[]{:S(2)}) collective-permute-start(bf16[448,576]{1,0:T(8,128)(2,1)} %add_convert_fusion.6), channel_id=1, source_target_pairs={{0,8},{4,12},{8,0},{12,4},{16,24},{20,28},{24,16},{28,20},{1,9},{5... | collective-permute-start | bytes 1548296 | tf_op jit(solution)/shard_map/ppermute | solution.py:635
  528.7 27.2 %collective-permute-start.33 = (bf16[448,576]{1,0:T(8,128)(2,1)}, bf16[448,576]{1,0:T(8,128)(2,1)S(1)}, u32[]{:S(2)}, u32[]{:S(2)}) collective-permute-start(bf16[448,576]{1,0:T(8,128)(2,1)} %add_convert_fusion.5), channel_id=1, source_target_pairs={{0,16},{4,20},{8,24},{12,28},{16,0},{20,4},{24,8},{28,12},{1,17},{... | collective-permute-start | bytes 1548296 | tf_op jit(solution)/shard_map/ppermute | solution.py:635
  531.0 24.9 %collective-permute-start.35 = (bf16[448,576]{1,0:T(8,128)(2,1)}, bf16[448,576]{1,0:T(8,128)(2,1)S(1)}, u32[]{:S(2)}, u32[]{:S(2)}) collective-permute-start(bf16[448,576]{1,0:T(8,128)(2,1)} %add_convert_fusion.4), channel_id=1, source_target_pairs={{0,24},{4,28},{8,16},{12,20},{16,8},{20,12},{24,0},{28,4},{1,25},{... | collective-permute-start | bytes 1548296 | tf_op jit(solution)/shard_map/ppermute | solution.py:635
  568.5 152.6 %reduce-scatter.9.cloned.1.call-start = ((), (), s32[]{:S(2)}) async-start(), calls=%async_computation.6 | async-start | bytes 10616832 | tf_op jit(solution)/shard_map/reduce_scatter | solution.py:657
  599.7 217.3 %all-gather.21.cloned.1.call-start = ((), (), s32[]{:S(2)}) async-start(), calls=%async_computation.12 | async-start | bytes 6635520 | tf_op jit(solution)/shard_map/all_gather | solution.py:660
  599.8 17.3 %collective-permute-start.36 = (bf16[448,192]{1,0:T(8,128)(2,1)S(1)}, bf16[448,192]{1,0:T(8,128)(2,1)S(1)}, u32[]{:S(2)}, u32[]{:S(2)}) collective-permute-start(bf16[448,192]{1,0:T(8,128)(2,1)S(1)} %get-tuple-element.161), channel_id=1, source_target_pairs={{0,8},{4,12},{8,0},{12,4},{16,24},{20,28},{24,16},{28,20},{1,9},{5... | collective-permute-start | bytes 516104 | tf_op jit(solution)/shard_map/ppermute | solution.py:635
  601.1 20.6 %collective-permute-start.37 = (bf16[448,192]{1,0:T(8,128)(2,1)S(1)}, bf16[448,192]{1,0:T(8,128)(2,1)S(1)}, u32[]{:S(2)}, u32[]{:S(2)}) collective-permute-start(bf16[448,192]{1,0:T(8,128)(2,1)S(1)} %get-tuple-element.162), channel_id=1, source_target_pairs={{0,16},{4,20},{8,24},{12,28},{16,0},{20,4},{24,8},{28,12},{1,17},{... | collective-permute-start | bytes 516104 | tf_op jit(solution)/shard_map/ppermute | solution.py:635
  601.9 20.7 %collective-permute-start.38 = (bf16[448,192]{1,0:T(8,128)(2,1)S(1)}, bf16[448,192]{1,0:T(8,128)(2,1)S(1)}, u32[]{:S(2)}, u32[]{:S(2)}) collective-permute-start(bf16[448,192]{1,0:T(8,128)(2,1)S(1)} %get-tuple-element.163), channel_id=1, source_target_pairs={{0,24},{4,28},{8,16},{12,20},{16,8},{20,12},{24,0},{28,4},{1,25},{... | collective-permute-start | bytes 516104 | tf_op jit(solution)/shard_map/ppermute | solution.py:635
  604.4 118.3 %collective-permute-start.53 = (bf16[384,384]{1,0:T(8,128)(2,1)}, bf16[384,384]{1,0:T(8,128)(2,1)}, u32[]{:S(2)}, u32[]{:S(2)}) collective-permute-start(bf16[384,384]{1,0:T(8,128)(2,1)} %get-tuple-element.236), channel_id=1, source_target_pairs={{0,3},{1,2},{2,1},{3,0},{4,7},{5,6},{6,5},{7,4},{8,11},{9,10},{10,... | collective-permute-start | bytes 884744 | tf_op jit(solution)/shard_map/ppermute | solution.py:635
  607.8 116.5 %collective-permute-start.52 = (bf16[384,384]{1,0:T(8,128)(2,1)S(1)}, bf16[384,384]{1,0:T(8,128)(2,1)}, u32[]{:S(2)}, u32[]{:S(2)}) collective-permute-start(bf16[384,384]{1,0:T(8,128)(2,1)S(1)} %get-tuple-element.237), channel_id=1, source_target_pairs={{0,2},{1,3},{2,0},{3,1},{4,6},{5,7},{6,4},{7,5},{8,10},{9,11},{10,... | collective-permute-start | bytes 884744 | tf_op jit(solution)/shard_map/ppermute | solution.py:635
  617.1 109.6 %collective-permute-start.51 = (bf16[384,384]{1,0:T(8,128)(2,1)S(1)}, bf16[384,384]{1,0:T(8,128)(2,1)S(1)}, u32[]{:S(2)}, u32[]{:S(2)}) collective-permute-start(bf16[384,384]{1,0:T(8,128)(2,1)S(1)} %get-tuple-element.235), channel_id=1, source_target_pairs={{0,1},{1,0},{2,3},{3,2},{4,5},{5,4},{6,7},{7,6},{8,9},{9,8},{10,11... | collective-permute-start | bytes 884744 | tf_op jit(solution)/shard_map/ppermute | solution.py:635
  696.4 30.4 %collective-permute-start.56 = (bf16[192,384]{1,0:T(8,128)(2,1)}, bf16[192,384]{1,0:T(8,128)(2,1)S(1)}, u32[]{:S(2)}, u32[]{:S(2)}) collective-permute-start(bf16[192,384]{1,0:T(8,128)(2,1)} %get-tuple-element.245), channel_id=1, source_target_pairs={{0,3},{1,2},{2,1},{3,0},{4,7},{5,6},{6,5},{7,4},{8,11},{9,10},{10,... | collective-permute-start | bytes 442376 | tf_op jit(solution)/shard_map/ppermute | solution.py:635
  698.4 31.5 %collective-permute-start.55 = (bf16[192,384]{1,0:T(8,128)(2,1)}, bf16[192,384]{1,0:T(8,128)(2,1)}, u32[]{:S(2)}, u32[]{:S(2)}) collective-permute-start(bf16[192,384]{1,0:T(8,128)(2,1)} %get-tuple-element.246), channel_id=1, source_target_pairs={{0,2},{1,3},{2,0},{3,1},{4,6},{5,7},{6,4},{7,5},{8,10},{9,11},{10,... | collective-permute-start | bytes 442376 | tf_op jit(solution)/shard_map/ppermute | solution.py:635
  724.3 13.7 %collective-permute-start.59 = (bf16[384,384]{1,0:T(8,128)(2,1)S(1)}, bf16[384,384]{1,0:T(8,128)(2,1)S(1)}, u32[]{:S(2)}, u32[]{:S(2)}) collective-permute-start(bf16[384,384]{1,0:T(8,128)(2,1)S(1)} %get-tuple-element.239), channel_id=1, source_target_pairs={{0,3},{1,2},{2,1},{3,0},{4,7},{5,6},{6,5},{7,4},{8,11},{9,10},{10,... | collective-permute-start | bytes 884744 | tf_op jit(solution)/shard_map/ppermute | solution.py:635
  726.7 25.7 %collective-permute-start.58 = (bf16[384,384]{1,0:T(8,128)(2,1)S(1)}, bf16[384,384]{1,0:T(8,128)(2,1)S(1)}, u32[]{:S(2)}, u32[]{:S(2)}) collective-permute-start(bf16[384,384]{1,0:T(8,128)(2,1)S(1)} %get-tuple-element.240), channel_id=1, source_target_pairs={{0,2},{1,3},{2,0},{3,1},{4,6},{5,7},{6,4},{7,5},{8,10},{9,11},{10,... | collective-permute-start | bytes 884744 | tf_op jit(solution)/shard_map/ppermute | solution.py:635
  726.8 25.6 %collective-permute-start.57 = (bf16[384,384]{1,0:T(8,128)(2,1)S(1)}, bf16[384,384]{1,0:T(8,128)(2,1)S(1)}, u32[]{:S(2)}, u32[]{:S(2)}) collective-permute-start(bf16[384,384]{1,0:T(8,128)(2,1)S(1)} %get-tuple-element.238), channel_id=1, source_target_pairs={{0,1},{1,0},{2,3},{3,2},{4,5},{5,4},{6,7},{7,6},{8,9},{9,8},{10,11... | collective-permute-start | bytes 884744 | tf_op jit(solution)/shard_map/ppermute | solution.py:635
  753.6 121.8 %reduce-scatter.11.cloned.1.call-start = ((), (), s32[]{:S(2)}) async-start(), calls=%async_computation.7 | async-start | bytes 5308416 | tf_op jit(solution)/shard_map/reduce_scatter | solution.py:657
  756.2 23.8 %collective-permute-start.41 = (bf16[448,576]{1,0:T(8,128)(2,1)S(1)}, bf16[448,576]{1,0:T(8,128)(2,1)S(1)}, u32[]{:S(2)}, u32[]{:S(2)}) collective-permute-start(bf16[448,576]{1,0:T(8,128)(2,1)S(1)} %add_convert_fusion.2), channel_id=1, source_target_pairs={{0,8},{4,12},{8,0},{12,4},{16,24},{20,28},{24,16},{28,20},{1,9},{5... | collective-permute-start | bytes 1548296 | tf_op jit(solution)/shard_map/ppermute | solution.py:635
  757.8 35.3 %collective-permute-start.43 = (bf16[448,576]{1,0:T(8,128)(2,1)S(1)}, bf16[448,576]{1,0:T(8,128)(2,1)S(1)}, u32[]{:S(2)}, u32[]{:S(2)}) collective-permute-start(bf16[448,576]{1,0:T(8,128)(2,1)S(1)} %add_convert_fusion.1), channel_id=1, source_target_pairs={{0,16},{4,20},{8,24},{12,28},{16,0},{20,4},{24,8},{28,12},{1,17},{... | collective-permute-start | bytes 1548296 | tf_op jit(solution)/shard_map/ppermute | solution.py:635
  759.4 33.7 %collective-permute-start.45 = (bf16[448,576]{1,0:T(8,128)(2,1)S(1)}, bf16[448,576]{1,0:T(8,128)(2,1)S(1)}, u32[]{:S(2)}, u32[]{:S(2)}) collective-permute-start(bf16[448,576]{1,0:T(8,128)(2,1)S(1)} %add_convert_fusion), channel_id=1, source_target_pairs={{0,24},{4,28},{8,16},{12,20},{16,8},{20,12},{24,0},{28,4},{1,25},{... | collective-permute-start | bytes 1548296 | tf_op jit(solution)/shard_map/ppermute | solution.py:635
  817.1 117.4 %all-gather.23.cloned.1.call-start = ((), (), s32[]{:S(2)}) async-start(), calls=%async_computation.13 | async-start | bytes 1327104 | tf_op jit(solution)/shard_map/all_gather | solution.py:660
  880.1 12.6 %collective-permute-start.61 = (bf16[192,384]{1,0:T(8,128)(2,1)S(1)}, bf16[192,384]{1,0:T(8,128)(2,1)S(1)}, u32[]{:S(2)}, u32[]{:S(2)}) collective-permute-start(bf16[192,384]{1,0:T(8,128)(2,1)S(1)} %get-tuple-element.243), channel_id=1, source_target_pairs={{0,2},{1,3},{2,0},{3,1},{4,6},{5,7},{6,4},{7,5},{8,10},{9,11},{10,... | collective-permute-start | bytes 442376 | tf_op jit(solution)/shard_map/ppermute | solution.py:635
  880.1 12.6 %collective-permute-start.60 = (bf16[192,384]{1,0:T(8,128)(2,1)S(1)}, bf16[192,384]{1,0:T(8,128)(2,1)S(1)}, u32[]{:S(2)}, u32[]{:S(2)}) collective-permute-start(bf16[192,384]{1,0:T(8,128)(2,1)S(1)} %get-tuple-element.241), channel_id=1, source_target_pairs={{0,1},{1,0},{2,3},{3,2},{4,5},{5,4},{6,7},{7,6},{8,9},{9,8},{10,11... | collective-permute-start | bytes 442376 | tf_op jit(solution)/shard_map/ppermute | solution.py:635
  (133 other events, 1836.7 us)
Sparse Core Ops, SparseCore 0:
  82.6 39.0 all-gather.12
  124.1 75.7 all-gather.14
  205.8 44.7 all-gather.16
  254.8 87.6 all-gather.18
  437.8 85.0 reduce-scatter.4
  568.6 72.0 reduce-scatter.6
  644.6 76.4 reduce-scatter.8
  753.7 63.3 all-gather.20
  821.4 53.8 reduce-scatter.10
  893.7 23.0 all-gather.22

commit v3 on v2

--- a/solution.py
+++ b/solution.py
@@ -386,22 +386,25 @@
     )(group_ids, grad, after, normed, gain, proj, w, bup, *atts)
 
 
-def head_masks(rows, width):
-    lane = lax.broadcasted_iota(jnp.int32, (rows, width), 1)
-    return [
-        (lane >= h * HEAD_DIM) & (lane < (h + 1) * HEAD_DIM) for h in range(width // HEAD_DIM)
-    ]
-
-
-def only_head(block, masks):
+def padded(blk):
+    return -(-blk // 128) * 128
+
+
+def heads_apart(cat_ref, block):
+    blk, width = block.shape
     wide = block.astype(F32)
-    return [jnp.where(mask, wide, 0.0).astype(BF) for mask in masks]
-
-
-def causal_tile(blk):
-    key_at = lax.broadcasted_iota(jnp.int32, (blk, blk), 0)
-    query_at = lax.broadcasted_iota(jnp.int32, (blk, blk), 1)
-    return key_at <= query_at
+    lane = lax.broadcasted_iota(jnp.int32, (blk, width), 1)
+    for h in range(width // HEAD_DIM):
+        mine = (lane >= h * HEAD_DIM) & (lane < (h + 1) * HEAD_DIM)
+        at = h * padded(blk)
+        cat_ref[at : at + blk, :] = jnp.where(mine, wide, 0.0).astype(BF)
+
+
+def causal_tile(blk, heads):
+    pad = padded(blk)
+    key_at = lax.broadcasted_iota(jnp.int32, (blk, heads * pad), 0)
+    query_at = lax.broadcasted_iota(jnp.int32, (blk, heads * pad), 1)
+    return key_at <= lax.rem(query_at, pad)
 
 
 def query_part(ref, rows, width):
@@ -414,9 +417,10 @@
 
 
 def attend_kernel(q_id, k_loc, *refs):
-    mixed_refs, o_refs, (lse_ref, q_ref, k_ref, vt_ref, acc_ref) = split_refs(
-        refs, len(refs) - GROUPS - 5, GROUPS, 5
+    mixed_refs, o_refs, (lse_ref, *scratch) = split_refs(
+        refs, len(refs) - GROUPS - 8, GROUPS, 8
     )
+    q_ref, k_ref, vt_ref, acc_ref, cat_ref, even_ref, odd_ref = scratch
     q_blocks, blk, width = q_ref.shape
     heads = width // HEAD_DIM
 
@@ -427,48 +431,50 @@
             vt_ref[2 * r + b] = ref[rows, 2 * width :].astype(F32).T.astype(BF)
             if r < GROUPS:
                 q_ref[2 * r + b] = query_part(ref, rows, width)
-    masks = head_masks(blk, width)
+    pad = padded(blk)
+    cat_ref[...] = jnp.zeros_like(cat_ref)
+    head_rows = [slice(h * HEAD_DIM, (h + 1) * HEAD_DIM) for h in range(heads)]
+    head_cols = [slice(h * pad, (h + 1) * pad) for h in range(heads)]
 
     def per_query(qb):
-        q_blk = q_ref[qb]
-        q_h = only_head(q_blk, masks)
+        heads_apart(cat_ref, q_ref[qb])
         own = q_id[qb]
         loc = k_loc[own]
-        keys = k_ref[loc]
-        tri = causal_tile(blk)
-        stats = []
+        even_ref[...] = jnp.where(
+            causal_tile(blk, heads), dot_nt(k_ref[loc], cat_ref[...]), -1e30
+        )
+        acc_ref[...] = jnp.zeros_like(acc_ref)
+
+        def block_at(t):
+            return k_loc[jnp.where(t == 0, own, jnp.minimum(t, own) - 1 + (own == 0))]
+
+        def half(t, here, ahead, carry):
+            top, total = carry
+            ahead[...] = dot_nt(k_ref[block_at(t + 1)], cat_ref[...])
+            s = here[...] + jnp.where(t <= own, 0.0, -1e30)
+            new = jnp.maximum(top, jnp.max(s, axis=0, keepdims=True))
+            alpha = jnp.exp(top - new)
+            p = jnp.exp(s - new)
+            total = total * alpha + jnp.sum(p, axis=0, keepdims=True)
+            p = p.astype(BF)
+            loc = block_at(t)
+            for h in range(heads):
+                acc_ref[head_rows[h], :] = acc_ref[head_rows[h], :] * alpha[
+                    :, head_cols[h]
+                ] + dot_nn(vt_ref[loc, head_rows[h], :], p[:, head_cols[h]])
+            return new, total
+
+        def step(i, carry):
+            carry = half(2 * i, even_ref, odd_ref, carry)
+            return half(2 * i + 1, odd_ref, even_ref, carry)
+
+        row = (1, heads * pad)
+        start = (jnp.full(row, -1e30, F32), jnp.zeros(row, F32))
+        top, total = lax.fori_loop(0, own // 2 + 1, step, start)
         for h in range(heads):
-            rows = slice(h * HEAD_DIM, (h + 1) * HEAD_DIM)
-            s = jnp.where(tri, dot_nt(keys, q_h[h]), -1e30)
-            top = jnp.max(s, axis=0, keepdims=True)
-            p = jnp.exp(s - top)
-            stats.append((top, jnp.sum(p, axis=0, keepdims=True)))
-            acc_ref[rows, :] = dot_nn(vt_ref[loc, rows, :], p.astype(BF))
-
-        def step(i, carry):
-            loc = k_loc[i]
-            keys = k_ref[loc]
-            out = []
-            for h in range(heads):
-                rows = slice(h * HEAD_DIM, (h + 1) * HEAD_DIM)
-                top, total = carry[h]
-                s = dot_nt(keys, q_h[h])
-                new = jnp.maximum(top, jnp.max(s, axis=0, keepdims=True))
-                alpha = jnp.exp(top - new)
-                p = jnp.exp(s - new)
-                out.append((new, total * alpha + jnp.sum(p, axis=0, keepdims=True)))
-                acc_ref[rows, :] = acc_ref[rows, :] * alpha + dot_nn(
-                    vt_ref[loc, rows, :], p.astype(BF)
-                )
-            return tuple(out)
-
-        stats = lax.fori_loop(0, own, step, tuple(stats))
-        for h in range(heads):
-            rows = slice(h * HEAD_DIM, (h + 1) * HEAD_DIM)
-            top, total = stats[h]
-            acc_ref[rows, :] = acc_ref[rows, :] / total
-            lse_ref[qb, h : h + 1, :] = top + jnp.log(total)
-        return acc_ref[...].T.astype(BF)
+            acc_ref[head_rows[h], :] = acc_ref[head_rows[h], :] / total[:, head_cols[h]]
+        lse_ref[qb, :1, :] = top + jnp.log(total)
+        return acc_ref[...].T[:blk].astype(BF)
 
     for k in range(GROUPS):
 
@@ -487,22 +493,26 @@
     return pl.pallas_call(
         attend_kernel,
         out_shape=[jax.ShapeDtypeStruct((rows, width), BF)] * GROUPS
-        + [jax.ShapeDtypeStruct((q_blocks, 8, blk), F32)],
+        + [jax.ShapeDtypeStruct((q_blocks, 8, width // HEAD_DIM * padded(blk)), F32)],
         grid_spec=pltpu.PrefetchScalarGridSpec(
             num_scalar_prefetch=2,
             grid=(1,),
             in_specs=[whole(x.shape) for x in mixed],
-            out_specs=[whole((rows, width))] * GROUPS + [whole((q_blocks, 8, blk))],
+            out_specs=[whole((rows, width))] * GROUPS
+            + [whole((q_blocks, 8, width // HEAD_DIM * padded(blk)))],
             scratch_shapes=[
                 pltpu.VMEM((q_blocks, blk, width), BF),
                 pltpu.VMEM((k_blocks, blk, width), BF),
                 pltpu.VMEM((k_blocks, width, blk), BF),
-                pltpu.VMEM((width, blk), F32),
+                pltpu.VMEM((width, padded(blk)), F32),
+                pltpu.VMEM((width // HEAD_DIM * padded(blk), width), BF),
+                pltpu.VMEM((blk, width // HEAD_DIM * padded(blk)), F32),
+                pltpu.VMEM((blk, width // HEAD_DIM * padded(blk)), F32),
             ],
         ),
         compiler_params=pltpu.CompilerParams(vmem_limit_bytes=48 << 20),
         cost_estimate=pl.CostEstimate(
-            flops=40 * q_blocks * k_blocks * blk * blk * width,
+            flops=28 * q_blocks * k_blocks * blk * blk * width,
             bytes_accessed=2 * len(mixed) * rows * cols,
             transcendentals=q_blocks * k_blocks * blk * blk * 2,
         ),
@@ -510,72 +520,81 @@
     )(q_id, k_loc, *mixed)
 
 
-def attend_back_kernel(q_id, k_loc, *refs):
-    count = (len(refs) - 2 * GROUPS - 9) // 2
+def attend_back_kernel(q_id, key_ids, *refs):
+    count = (len(refs) - 2 * GROUPS - 11) // 2
     mixed_refs, o_refs, do_refs, (lse_ref,), dm_refs, scratch = split_refs(
-        refs, count, GROUPS, GROUPS, 1, count, 8
+        refs, count, GROUPS, GROUPS, 1, count, 10
     )
-    q_ref, k_ref, v_ref, kt_ref, dq_ref, dka_ref, dva_ref, dqt_ref = scratch
+    q_ref, k_ref, v_ref, kt_ref, dq_ref, dka_ref, dva_ref, dqt_ref, cat_ref, dcat_ref = scratch
     q_blocks, blk, width = q_ref.shape
     heads = width // HEAD_DIM
     for r, ref in enumerate(mixed_refs):
         for b in range(2):
             rows = slice(b * blk, (b + 1) * blk)
-            at = 2 * r + b
+            at = key_ids[2 * r + b]
+            in_order = pl.ds(pl.multiple_of(at * blk, 32), blk)
             keys = ref[rows, :width]
-            k_ref[at] = keys
+            k_ref[in_order, :] = keys
             kt_ref[at] = keys.astype(F32).T.astype(BF)
-            v_ref[at] = ref[rows, 2 * width :]
+            v_ref[in_order, :] = ref[rows, 2 * width :]
             if r < GROUPS:
-                q_ref[at] = query_part(ref, rows, width)
+                q_ref[2 * r + b] = query_part(ref, rows, width)
 
     def clear(b, _):
-        dka_ref[b] = jnp.zeros((blk, width), F32)
-        dva_ref[b] = jnp.zeros((blk, width), F32)
+        rows = pl.ds(pl.multiple_of(b * blk, 32), blk)
+        dka_ref[rows, :] = jnp.zeros((blk, width), F32)
+        dva_ref[rows, :] = jnp.zeros((blk, width), F32)
         return 0
 
-    lax.fori_loop(0, k_ref.shape[0], clear, 0)
-    masks = head_masks(blk, width)
+    lax.fori_loop(0, kt_ref.shape[0], clear, 0)
+    pad = padded(blk)
+    cat_ref[...] = jnp.zeros_like(cat_ref)
+    dcat_ref[...] = jnp.zeros_like(dcat_ref)
 
     def per_query(qb, do_blk, o_blk):
-        q_blk = q_ref[qb]
-        q_h = only_head(q_blk, masks)
-        do_h = only_head(do_blk, masks)
-        both = (do_blk.astype(F32) * o_blk.astype(F32)).T
-        delta = [
-            jnp.sum(both[h * HEAD_DIM : (h + 1) * HEAD_DIM], axis=0, keepdims=True)
-            for h in range(heads)
-        ]
-        lse = [lse_ref[qb, h : h + 1, :] for h in range(heads)]
+        heads_apart(cat_ref, q_ref[qb])
+        heads_apart(dcat_ref, do_blk)
+        both = do_blk.astype(F32) * o_blk.astype(F32)
+        both = jnp.concatenate([both, jnp.zeros((pad - blk, width), F32)], 0).T
+        delta = jnp.concatenate(
+            [
+                jnp.sum(both[h * HEAD_DIM : (h + 1) * HEAD_DIM], axis=0, keepdims=True)
+                for h in range(heads)
+            ],
+            1,
+        )
+        lse = lse_ref[qb, :1, :]
         own = q_id[qb]
 
-        def tile(loc, tri, first):
-            keys = k_ref[loc]
-            values = v_ref[loc]
-            dk = dka_ref[loc]
-            dv = dva_ref[loc]
+        dqt_ref[...] = jnp.zeros_like(dqt_ref)
+
+        def two_blocks(t, allowed):
+            rows = pl.ds(pl.multiple_of(t * (2 * blk), 32), 2 * blk)
+            p = jnp.exp(dot_nt(k_ref[rows, :], cat_ref[...]) - lse)
+            if allowed is not None:
+                p = jnp.where(allowed, p, 0.0)
+            dp = dot_nt(v_ref[rows, :], dcat_ref[...])
+            ds = (p * (dp - delta)).astype(BF)
+            dva_ref[rows, :] += dot_nn(p.astype(BF), dcat_ref[...])
+            dka_ref[rows, :] += dot_nn(ds, cat_ref[...])
             for h in range(heads):
-                rows = slice(h * HEAD_DIM, (h + 1) * HEAD_DIM)
-                p = jnp.exp(dot_nt(keys, q_h[h]) - lse[h])
-                if tri is not None:
-                    p = jnp.where(tri, p, 0.0)
-                dp = dot_nt(values, do_h[h])
-                ds = (p * (dp - delta[h])).astype(BF)
-                dv = dv + dot_nn(p.astype(BF), do_h[h])
-                dk = dk + dot_nn(ds, q_h[h])
-                dq = dot_nn(kt_ref[loc, rows, :], ds)
-                dqt_ref[rows, :] = dq if first else dqt_ref[rows, :] + dq
-            dka_ref[loc] = dk
-            dva_ref[loc] = dv
-
-        tile(k_loc[own], causal_tile(blk), True)
-
-        def step(i, _):
-            tile(k_loc[i], None, False)
+                part = slice(h * HEAD_DIM, (h + 1) * HEAD_DIM)
+                cols = slice(h * pad, (h + 1) * pad)
+                dqt_ref[part, :] += dot_nn(kt_ref[2 * t, part, :], ds[:blk, cols]) + dot_nn(
+                    kt_ref[2 * t + 1, part, :], ds[blk:, cols]
+                )
+
+        def step(t, _):
+            two_blocks(t, None)
             return 0
 
-        lax.fori_loop(0, own, step, 0)
-        dq_ref[qb] = (dqt_ref[...] * (HEAD_DIM ** (-0.5))).T
+        last = own // 2
+        lax.fori_loop(0, last, step, 0)
+        shape = (2 * blk, heads * pad)
+        key_at = lax.broadcasted_iota(jnp.int32, shape, 0)
+        query_at = lax.rem(lax.broadcasted_iota(jnp.int32, shape, 1), pad)
+        two_blocks(last, key_at - query_at <= (own - 2 * last) * blk)
+        dq_ref[qb] = (dqt_ref[...] * (HEAD_DIM ** (-0.5))).T[:blk]
 
     for k in range(GROUPS):
 
@@ -589,16 +608,16 @@
     for r, ref in enumerate(dm_refs):
 
         def finish(b, _, r=r, ref=ref):
-            at = 2 * r + b
-            dq = dq_ref[at] if r < GROUPS else jnp.zeros((blk, width), F32)
-            joined = jnp.concatenate([dka_ref[at], dq, dva_ref[at]], 1)
+            rows = pl.ds(pl.multiple_of(key_ids[2 * r + b] * blk, 32), blk)
+            dq = dq_ref[2 * r + b] if r < GROUPS else jnp.zeros((blk, width), F32)
+            joined = jnp.concatenate([dka_ref[rows, :], dq, dva_ref[rows, :]], 1)
             ref[pl.ds(pl.multiple_of(b * blk, 32), blk), :] = joined.astype(BF)
             return 0
 
         lax.fori_loop(0, 2, finish, 0)
 
 
-def attend_back(q_id, k_loc, mixed, o, do, lse):
+def attend_back(q_id, key_ids, mixed, o, do, lse):
     rows, cols = mixed[0].shape
     blk, width = rows // 2, cols // 3
     q_blocks, k_blocks = 2 * GROUPS, 2 * len(mixed)
@@ -612,23 +631,25 @@
             out_specs=[whole((rows, cols))] * len(mixed),
             scratch_shapes=[
                 pltpu.VMEM((q_blocks, blk, width), BF),
-                pltpu.VMEM((k_blocks, blk, width), BF),
-                pltpu.VMEM((k_blocks, blk, width), BF),
+                pltpu.VMEM((k_blocks * blk, width), BF),
+                pltpu.VMEM((k_blocks * blk, width), BF),
                 pltpu.VMEM((k_blocks, width, blk), BF),
                 pltpu.VMEM((q_blocks, blk, width), F32),
-                pltpu.VMEM((k_blocks, blk, width), F32),
-                pltpu.VMEM((k_blocks, blk, width), F32),
-                pltpu.VMEM((width, blk), F32),
+                pltpu.VMEM((k_blocks * blk, width), F32),
+                pltpu.VMEM((k_blocks * blk, width), F32),
+                pltpu.VMEM((width, padded(blk)), F32),
+                pltpu.VMEM((width // HEAD_DIM * padded(blk), width), BF),
+                pltpu.VMEM((width // HEAD_DIM * padded(blk), width), BF),
             ],
         ),
         compiler_params=pltpu.CompilerParams(vmem_limit_bytes=56 << 20),
         cost_estimate=pl.CostEstimate(
-            flops=70 * q_blocks * k_blocks * blk * blk * width,
+            flops=48 * q_blocks * k_blocks * blk * blk * width,
             bytes_accessed=4 * len(mixed) * rows * cols,
             transcendentals=q_blocks * k_blocks * blk * blk * 2,
         ),
         name="attend_back",
-    )(q_id, k_loc, *mixed, *o, *do, lse)
+    )(q_id, key_ids, *mixed, *o, *do, lse)
 
 
 def swap(x, axis_name, size, k):
@@ -856,7 +877,7 @@
         )
         part_feed = scatter_part(place, dfeed)
         do = place.exchange(datts)
-        dm = attend_back(q_id, k_loc, mixed, o, do, lse)
+        dm = attend_back(q_id, key_ids, mixed, o, do, lse)
         dm = list(dm)
         if layer > 0:
             dm[0] = after(dm[0], part_feed)

time: 959 us -> 911 us (0.950)
  Pallas kernels: 337 us -> 265 us
  waiting for transfers between devices: 366 us -> 406 us
  starting transfers between devices: 86.4 us -> 71.3 us
    pallas_call x2, Pallas kernels: 142 us -> 96.2 us  [attend_back(): pl.pallas_call(attend_back_kernel, out_shape=[jax.ShapeDtypeStruct((rows,...]
    pallas_call x2, Pallas kernels: 81 us -> 53.9 us  [attend(): pl.pallas_call(attend_kernel, out_shape=[jax.ShapeDtypeStruct((rows, widt...]
    reduce_scatter x4, waiting for transfers between devices: 55.7 us -> 82.2 us  [scatter_ctx(): return lax.psum_scatter(x, 'ctx', scatter_dimension=0, tiled=True)]
    ppermute x63, starting transfers between devices: 85.3 us -> 70.6 us  [swap(): return lax.ppermute(x, axis_name, [(i, i ^ k) for i in range(size)])]
  transfers between devices with their start and end apart: 73 -> 73, of which waited for: 36 -> 40; matrix products, arithmetic and copies ran while one was open for 7% -> 8% of each run, Pallas kernels for 30% -> 23%
where the time goes in v3:
time: 911 us; the launch traced here: 902 us
  waiting for transfers between devices  406 us (45%)
  Pallas kernels  265 us (29%)
  local copies, waits for them, and re-layouts  121 us (13%)
  starting transfers between devices  71.3 us (8%)
  other arithmetic  22.2 us (2%)
  between operations  16.3 us (2%)
    ppermute x63, waiting for transfers between devices, swap(): return lax.ppermute(x, axis_name, [(i, i ^ k) for i in range(size)])  265 us
    pallas_call x2, Pallas kernels, attend_back(): pl.pallas_call(attend_back_kernel, out_shape=[jax.ShapeDtypeStruct((rows,...  96.2 us
    reduce_scatter x4, waiting for transfers between devices, scatter_ctx(): return lax.psum_scatter(x, 'ctx', scatter_dimension=0, tiled=True)  82.2 us
    ppermute x63, starting transfers between devices, swap(): return lax.ppermute(x, axis_name, [(i, i ^ k) for i in range(size)])  70.6 us
    all_gather x6, waiting for transfers between devices, gather_ctx(): return lax.all_gather(x, 'ctx', axis=0, tiled=False)  58.6 us
    pallas_call x2, Pallas kernels, mlp_back(): pl.pallas_call(mlp_back_kernel, out_shape=[jax.ShapeDtypeStruct((rows, gw...  54 us
    pallas_call x2, Pallas kernels, attend(): pl.pallas_call(attend_kernel, out_shape=[jax.ShapeDtypeStruct((rows, widt...  53.9 us
    unnamed x255, local copies, waits for them, and re-layouts  46 us
  transfers between devices with their start and end apart: 73, of which 40 were waited for; matrix products, arithmetic and copies ran while one was open for 8% of the time, Pallas kernels for 23%

profile of v3, /device:TPU:0, one launch (start us, length us, event | category | flops | bytes accessed | tf_op | source)
XLA Modules:
  0.0 901.6 jit_solution(6767871923926717797)
XLA Ops:
  16.9 3.3 fusion.27
  35.7 5.1 collective-permute-start.2
  41.5 11.0 %collective-permute-done.2.refs_3_ = bf16[304,768]{1,0:T(8,128)(2,1)S(1)} collective-permute-done((bf16[304,768]{1,0:T(8,128)(2,1)S(1)}, bf16[304,768]{1,0:T(8,128)(2,1)S(1)}, u32[]{:S(2)}, u32[]{:S(2)}) %collective-permute-start.2) | collective-permute-done | bytes 466976 | tf_op jit(solution)/shard_map/ppermute | solution.py:656
  52.5 28.2 %collective-permute-done.1.refs_2_ = bf16[304,768]{1,0:T(8,128)(2,1)S(1)} collective-permute-done((bf16[304,768]{1,0:T(8,128)(2,1)S(1)}, bf16[304,768]{1,0:T(8,128)(2,1)S(1)}, u32[]{:S(2)}, u32[]{:S(2)}) %collective-permute-start.1) | collective-permute-done | bytes 466976 | tf_op jit(solution)/shard_map/ppermute | solution.py:656
  82.5 39.1 %all-gather.13.cloned.1.call-done = bf16[3072,768]{1,0:T(8,128)(2,1)} async-done(((bf16[384,768]{1,0:T(8,128)(2,1)}), bf16[3072,768]{1,0:T(8,128)(2,1)}) %all-gather.13.cloned.1.call-update) | async-done | bytes 4718608 | tf_op jit(solution)/shard_map/all_gather | solution.py:681
  137.6 3.1 mix.2
  148.3 17.0 %collective-permute-done.13.refs_1_ = bf16[288,768]{1,0:T(8,128)(2,1)S(1)} collective-permute-done((bf16[288,768]{1,0:T(8,128)(2,1)S(1)}, bf16[288,768]{1,0:T(8,128)(2,1)S(1)}, u32[]{:S(2)}, u32[]{:S(2)}) %collective-permute-start.13) | collective-permute-done | bytes 442400 | tf_op jit(solution)/shard_map/ppermute | solution.py:656
  167.4 17.9 %collective-permute-done.5.refs_3_ = bf16[448,576]{1,0:T(8,128)(2,1)S(1)} collective-permute-done((bf16[448,576]{1,0:T(8,128)(2,1)S(1)}, bf16[448,576]{1,0:T(8,128)(2,1)S(1)}, u32[]{:S(2)}, u32[]{:S(2)}) %collective-permute-start.5) | collective-permute-done | bytes 516128 | tf_op jit(solution)/shard_map/ppermute | solution.py:656
  186.2 3.3 collective-permute-start.15
  189.5 11.2 %collective-permute-done.15.refs_3_ = bf16[288,768]{1,0:T(8,128)(2,1)S(1)} collective-permute-done((bf16[288,768]{1,0:T(8,128)(2,1)S(1)}, bf16[288,768]{1,0:T(8,128)(2,1)S(1)}, u32[]{:S(2)}, u32[]{:S(2)}) %collective-permute-start.15) | collective-permute-done | bytes 442400 | tf_op jit(solution)/shard_map/ppermute | solution.py:656
  213.8 26.6 %attend.2 = (bf16[448,192]{1,0:T(8,128)(2,1)S(1)}, bf16[448,192]{1,0:T(8,128)(2,1)S(1)}, bf16[448,192]{1,0:T(8,128)(2,1)S(1)}, bf16[448,192]{1,0:T(8,128)(2,1)S(1)}, f32[8,8,768]{2,1,0:T(8,128)S(1)}) custom-call(s32[8]{0:T(128)S(1)} %pad_add_fusion.1.q_id, s32[16]{0:T(128)S(1)} %select_reduce_fusion.k_loc, bf16[448,576]{1,0:T(8,128)(2,1)S(1)} %get-tuple-element.110.refs_0_, ...), custom_call_target="tpu_custom_call" | custom-call | flops 34527510528 | bytes 4128768 | tf_op jit(solution)/shard_map/attend/pallas_call | solution.py:493
  241.8 8.8 all-gather.17.cloned.1.call-done
  256.2 4.2 collective-permute-done.10.refs_1_
  260.4 5.8 collective-permute-done.11.refs_2_
  269.2 13.5 %mlp.2 = (f32[448,768]{1,0:T(8,128)S(1)}, bf16[448,768]{1,0:T(8,128)(2,1)S(1)}, f32[448,768]{1,0:T(8,128)S(1)}) custom-call(s32[4]{0:T(128)S(1)} %pad_add_fusion.group_ids, f32[448,768]{1,0:T(8,128)S(1)} %bitcast_convert_fusion.1.state_ref, bf16[4,192,768]{2,1,0:T(8,128)(2,1)S(1)} %copy-done.14, f32[1,768]{1,0:T(1,128)S(1)} %slice.294.bproj_ref, ...), custom_call_target="tpu_custom_call" | custom-call | flops 14269022208 | bytes 9437184 | tf_op jit(solution)/shard_map/mlp/pallas_call | solution.py:273
  283.6 3.2 mix.3
  291.1 24.6 %collective-permute-done.16.refs_1_ = bf16[448,576]{1,0:T(8,128)(2,1)S(1)} collective-permute-done((bf16[448,576]{1,0:T(8,128)(2,1)S(1)}, bf16[448,576]{1,0:T(8,128)(2,1)S(1)}, u32[]{:S(2)}, u32[]{:S(2)}) %collective-permute-start.16) | collective-permute-done | bytes 516128 | tf_op jit(solution)/shard_map/ppermute | solution.py:656
  317.9 19.0 %collective-permute-done.18.refs_3_ = bf16[448,576]{1,0:T(8,128)(2,1)S(1)} collective-permute-done((bf16[448,576]{1,0:T(8,128)(2,1)S(1)}, bf16[448,576]{1,0:T(8,128)(2,1)S(1)}, u32[]{:S(2)}, u32[]{:S(2)}) %collective-permute-start.18) | collective-permute-done | bytes 516128 | tf_op jit(solution)/shard_map/ppermute | solution.py:656
  338.8 27.3 %attend.3 = (bf16[448,192]{1,0:T(8,128)(2,1)S(1)}, bf16[448,192]{1,0:T(8,128)(2,1)}, bf16[448,192]{1,0:T(8,128)(2,1)}, bf16[448,192]{1,0:T(8,128)(2,1)}, f32[8,8,768]{2,1,0:T(8,128)S(1)}) custom-call(s32[8]{0:T(128)S(1)} %pad_add_fusion.1.q_id, s32[16]{0:T(128)S(1)} %select_reduce_fusion.k_loc, bf16[448,576]{1,0:T(8,128)(2,1)S(1)} %get-tuple-element.125.refs_0_, ...), custom_call_target="tpu_custom_call" | custom-call | flops 34527510528 | bytes 4128768 | tf_op jit(solution)/shard_map/attend/pallas_call | solution.py:493
  371.5 3.5 collective-permute-done.23.refs_1_
  374.9 4.4 collective-permute-done.24.refs_2_
  380.3 12.7 %mlp.3 = (f32[448,768]{1,0:T(8,128)S(1)}, bf16[448,768]{1,0:T(8,128)(2,1)S(1)}, f32[448,768]{1,0:T(8,128)S(1)}) custom-call(s32[4]{0:T(128)S(1)} %pad_add_fusion.group_ids, f32[448,768]{1,0:T(8,128)S(1)} %get-tuple-element.118.state_ref, bf16[4,192,768]{2,1,0:T(8,128)(2,1)S(1)} %get-tuple-element.122.proj_ref, f32[1,768]{1,0:T(1,128)S(1)} %slice.320.bproj_ref, ...), custom_call_target="tpu_custom_call" | custom-call | flops 14269022208 | bytes 9437184 | tf_op jit(solution)/shard_map/mlp/pallas_call | solution.py:273
  395.1 26.9 %mlp_back.2 = (bf16[448,192]{1,0:T(8,128)(2,1)S(1)}, bf16[448,192]{1,0:T(8,128)(2,1)S(1)}, bf16[448,192]{1,0:T(8,128)(2,1)S(1)}, bf16[448,192]{1,0:T(8,128)(2,1)...) custom-call(s32[4]{0:T(128)S(1)} %pad_add_fusion.group_ids, ...), custom_call_target="tpu_custom_call" | custom-call | flops 34879832064 | bytes 18874368 | tf_op jit(solution)/shard_map/mlp_back/pallas_call | solution.py:349
  427.2 5.1 collective-permute-done.26.refs_13_
  432.3 4.1 collective-permute-done.27.refs_14_
  437.1 48.5 %attend_back.2 = (bf16[448,576]{1,0:T(8,128)(2,1)}, bf16[448,576]{1,0:T(8,128)(2,1)}, bf16[448,576]{1,0:T(8,128)(2,1)}, bf16[448,576]{1,0:T(8,128)(2,1)}, bf16[4...) custom-call(s32[8]{0:T(128)} %copy-done.12, ...), custom_call_target="tpu_custom_call" | custom-call | flops 59190018048 | bytes 8257536 | tf_op jit(solution)/shard_map/attend_back/pallas_call | solution.py:624
  495.4 9.5 %reduce-scatter.5.cloned.1.call-done.part_ref = bf16[768,768]{1,0:T(8,128)(2,1)} async-done(((bf16[6144,768]{1,0:T(8,128)(2,1)}), bf16[768,768]{1,0:T(8,128)(2,1)}) %reduce-scatter.5.cloned.1.call-update) | async-done | bytes 1179664 | tf_op jit(solution)/shard_map/reduce_scatter | solution.py:678
  505.0 5.7 collective-permute-done.31.refs_1_
  510.7 12.9 %collective-permute-done.35.refs_3_ = bf16[448,576]{1,0:T(8,128)(2,1)S(1)} collective-permute-done((bf16[448,576]{1,0:T(8,128)(2,1)}, bf16[448,576]{1,0:T(8,128)(2,1)S(1)}, u32[]{:S(2)}, u32[]{:S(2)}) %collective-permute-start.35) | collective-permute-done | bytes 516128 | tf_op jit(solution)/shard_map/ppermute | solution.py:656
  524.4 11.7 %mix_back.2 = (bf16[8,384,768]{2,1,0:T(8,128)(2,1)}, f32[448,768]{1,0:T(8,128)}, f32[1,768]{1,0:T(1,128)S(1)}, f32[1,768]{1,0:T(1,128)S(1)}, f32[4,8,576]{2,1,0:T(8,128)S(1)}) custom-call(s32[4]{0:T(128)S(1)} %pad_add_fusion.group_ids, f32[448,768]{1,0:T(8,128)} %get-tuple-element.136.grad_ref, f32[448,768]{1,0:T(8,128)} %copy-done.3, ...), custom_call_target="tpu_custom_call" | custom-call | flops 9512681472 | bytes 9437184 | tf_op jit(solution)/shard_map/mix_back/pallas_call | solution.py:149
  538.7 27.1 %mlp_back.3 = (bf16[448,192]{1,0:T(8,128)(2,1)S(1)}, bf16[448,192]{1,0:T(8,128)(2,1)S(1)}, bf16[448,192]{1,0:T(8,128)(2,1)S(1)}, bf16[448,192]{1,0:T(8,128)(2,1)...) custom-call(s32[4]{0:T(128)S(1)} %pad_add_fusion.group_ids, ...), custom_call_target="tpu_custom_call" | custom-call | flops 34879832064 | bytes 18874368 | tf_op jit(solution)/shard_map/mlp_back/pallas_call | solution.py:349
  572.2 3.1 collective-permute-start.53
  579.6 3.9 collective-permute-done.38.refs_15_
  584.2 47.7 %attend_back.3 = (bf16[448,576]{1,0:T(8,128)(2,1)}, bf16[448,576]{1,0:T(8,128)(2,1)}, bf16[448,576]{1,0:T(8,128)(2,1)}, bf16[448,576]{1,0:T(8,128)(2,1)}, bf16[4...) custom-call(s32[8]{0:T(128)} %copy-done.12, ...), custom_call_target="tpu_custom_call" | custom-call | flops 59190018048 | bytes 8257536 | tf_op jit(solution)/shard_map/attend_back/pallas_call | solution.py:624
  634.0 3.3 collective-permute-start.56
  637.3 36.2 %reduce-scatter.9.cloned.1.call-done.part_ref = bf16[768,768]{1,0:T(8,128)(2,1)} async-done(((bf16[6144,768]{1,0:T(8,128)(2,1)}), bf16[768,768]{1,0:T(8,128)(2,1)}) %reduce-scatter.9.cloned.1.call-update) | async-done | bytes 1179664 | tf_op jit(solution)/shard_map/reduce_scatter | solution.py:678
  683.3 7.1 collective-permute-done.59
  690.4 14.4 %collective-permute-done.58 = bf16[384,384]{1,0:T(8,128)(2,1)S(1)} collective-permute-done((bf16[384,384]{1,0:T(8,128)(2,1)S(1)}, bf16[384,384]{1,0:T(8,128)(2,1)S(1)}, u32[]{:S(2)}, u32[]{:S(2)}) %collective-permute-start.58) | collective-permute-done | bytes 294944 | tf_op jit(solution)/shard_map/ppermute | solution.py:656
  713.5 18.9 %collective-permute-done.41.refs_1_ = bf16[448,576]{1,0:T(8,128)(2,1)S(1)} collective-permute-done((bf16[448,576]{1,0:T(8,128)(2,1)S(1)}, bf16[448,576]{1,0:T(8,128)(2,1)S(1)}, u32[]{:S(2)}, u32[]{:S(2)}) %collective-permute-start.41) | collective-permute-done | bytes 516128 | tf_op jit(solution)/shard_map/ppermute | solution.py:656
  732.4 13.1 %collective-permute-done.43.refs_2_ = bf16[448,576]{1,0:T(8,128)(2,1)S(1)} collective-permute-done((bf16[448,576]{1,0:T(8,128)(2,1)S(1)}, bf16[448,576]{1,0:T(8,128)(2,1)S(1)}, u32[]{:S(2)}, u32[]{:S(2)}) %collective-permute-start.43) | collective-permute-done | bytes 516128 | tf_op jit(solution)/shard_map/ppermute | solution.py:656
  746.4 12.4 %mix_back.3 = (bf16[8,384,768]{2,1,0:T(8,128)(2,1)}, f32[448,768]{1,0:T(8,128)}, f32[1,768]{1,0:T(1,128)S(1)}, f32[1,768]{1,0:T(1,128)S(1)}, f32[4,8,576]{2,1,0:T(8,128)S(1)}) custom-call(s32[4]{0:T(128)S(1)} %pad_add_fusion.group_ids, f32[448,768]{1,0:T(8,128)} %get-tuple-element.157.grad_ref, f32[448,768]{1,0:T(8,128)} %copy-done, ...), custom_call_target="tpu_custom_call" | custom-call | flops 9512681472 | bytes 9437184 | tf_op jit(solution)/shard_map/mix_back/pallas_call | solution.py:149
  758.8 10.7 %all-gather.21.cloned.1.call-done = bf16[7680,384]{1,0:T(8,128)(2,1)} async-done(((bf16[960,384]{1,0:T(8,128)(2,1)}), bf16[7680,384]{1,0:T(8,128)(2,1)}) %all-gather.21.cloned.1.call-update) | async-done | bytes 5898256 | tf_op jit(solution)/shard_map/all_gather | solution.py:681
  791.3 36.5 %reduce-scatter.11.cloned.1.call-done.part_ref = bf16[384,768]{1,0:T(8,128)(2,1)} async-done(((bf16[3072,768]{1,0:T(8,128)(2,1)}), bf16[384,768]{1,0:T(8,128)(2,1)}) %reduce-scatter.11.cloned.1.call-update) | async-done | bytes 589840 | tf_op jit(solution)/shard_map/reduce_scatter | solution.py:678
  829.2 3.4 collective-permute-start.62
  833.8 4.0 collective-permute-done.62
  837.8 7.4 collective-permute-done.61
  859.1 4.3 fusion.25
  869.4 3.3 convert_element_type.443
  (578 shorter events, 211.5 us)
Async XLA Ops:
  7.2 114.5 %all-gather.13.cloned.1.call-start = ((), (), s32[]{:S(2)}) async-start(), calls=%async_computation.8 | async-start | bytes 5308416 | tf_op jit(solution)/shard_map/all_gather | solution.py:681
  35.7 16.8 %collective-permute-start.2 = (bf16[304,768]{1,0:T(8,128)(2,1)S(1)}, bf16[304,768]{1,0:T(8,128)(2,1)S(1)}, u32[]{:S(2)}, u32[]{:S(2)}) collective-permute-start(bf16[304,768]{1,0:T(8,128)(2,1)S(1)} %pad_maximum_fusion.1.refs_0_), channel_id=1, source_target_pairs={{0,3},{1,2},{2,1},{3,0},{4,7},{5,6},{6,5},{7,4},{8,11},{9,10},{10,... | collective-permute-start | bytes 1400840 | tf_op jit(solution)/shard_map/ppermute | solution.py:656
  40.8 39.9 %collective-permute-start.1 = (bf16[304,768]{1,0:T(8,128)(2,1)S(1)}, bf16[304,768]{1,0:T(8,128)(2,1)S(1)}, u32[]{:S(2)}, u32[]{:S(2)}) collective-permute-start(bf16[304,768]{1,0:T(8,128)(2,1)S(1)} %pad_maximum_fusion.1.refs_0_), channel_id=1, source_target_pairs={{0,2},{1,3},{2,0},{3,1},{4,6},{5,7},{6,4},{7,5},{8,10},{9,11},{10,... | collective-permute-start | bytes 1400840 | tf_op jit(solution)/shard_map/ppermute | solution.py:656
  40.8 39.9 %collective-permute-start = (bf16[304,768]{1,0:T(8,128)(2,1)S(1)}, bf16[304,768]{1,0:T(8,128)(2,1)S(1)}, u32[]{:S(2)}, u32[]{:S(2)}) collective-permute-start(bf16[304,768]{1,0:T(8,128)(2,1)S(1)} %pad_maximum_fusion.1.refs_0_), channel_id=1, source_target_pairs={{0,1},{1,0},{2,3},{3,2},{4,5},{5,4},{6,7},{7,6},{8,9},{9,8},{10,11... | collective-permute-start | bytes 1400840 | tf_op jit(solution)/shard_map/ppermute | solution.py:656
  82.4 123.3 %all-gather.15.cloned.1.call-start = ((), (), s32[]{:S(2)}) async-start(), calls=%async_computation.9 | async-start | bytes 10616832 | tf_op jit(solution)/shard_map/all_gather | solution.py:681
  121.7 128.9 %all-gather.17.cloned.1.call-start = ((), (), s32[]{:S(2)}) async-start(), calls=%async_computation.10 | async-start | bytes 5308416 | tf_op jit(solution)/shard_map/all_gather | solution.py:681
  140.8 24.5 %collective-permute-start.3 = (bf16[448,576]{1,0:T(8,128)(2,1)S(1)}, bf16[448,576]{1,0:T(8,128)(2,1)S(1)}, u32[]{:S(2)}, u32[]{:S(2)}) collective-permute-start(bf16[448,576]{1,0:T(8,128)(2,1)S(1)} %get-tuple-element.111), channel_id=1, source_target_pairs={{0,8},{4,12},{8,0},{12,4},{16,24},{20,28},{24,16},{28,20},{1,9},{5... | collective-permute-start | bytes 1548296 | tf_op jit(solution)/shard_map/ppermute | solution.py:656
  142.2 24.4 %collective-permute-start.4 = (bf16[448,576]{1,0:T(8,128)(2,1)S(1)}, bf16[448,576]{1,0:T(8,128)(2,1)S(1)}, u32[]{:S(2)}, u32[]{:S(2)}) collective-permute-start(bf16[448,576]{1,0:T(8,128)(2,1)S(1)} %get-tuple-element.112), channel_id=1, source_target_pairs={{0,16},{4,20},{8,24},{12,28},{16,0},{20,4},{24,8},{28,12},{1,17},{... | collective-permute-start | bytes 1548296 | tf_op jit(solution)/shard_map/ppermute | solution.py:656
  142.8 42.6 %collective-permute-start.5 = (bf16[448,576]{1,0:T(8,128)(2,1)S(1)}, bf16[448,576]{1,0:T(8,128)(2,1)S(1)}, u32[]{:S(2)}, u32[]{:S(2)}) collective-permute-start(bf16[448,576]{1,0:T(8,128)(2,1)S(1)} %get-tuple-element.113), channel_id=1, source_target_pairs={{0,24},{4,28},{8,16},{12,20},{16,8},{20,12},{24,0},{28,4},{1,25},{... | collective-permute-start | bytes 1548296 | tf_op jit(solution)/shard_map/ppermute | solution.py:656
  144.4 20.8 %collective-permute-start.13 = (bf16[288,768]{1,0:T(8,128)(2,1)S(1)}, bf16[288,768]{1,0:T(8,128)(2,1)S(1)}, u32[]{:S(2)}, u32[]{:S(2)}) collective-permute-start(bf16[288,768]{1,0:T(8,128)(2,1)S(1)} %pad_maximum_fusion.2.refs_0_), channel_id=1, source_target_pairs={{0,1},{1,0},{2,3},{3,2},{4,5},{5,4},{6,7},{7,6},{8,9},{9,8},{10,11... | collective-permute-start | bytes 1327112 | tf_op jit(solution)/shard_map/ppermute | solution.py:656
  145.9 40.3 %collective-permute-start.14 = (bf16[288,768]{1,0:T(8,128)(2,1)S(1)}, bf16[288,768]{1,0:T(8,128)(2,1)S(1)}, u32[]{:S(2)}, u32[]{:S(2)}) collective-permute-start(bf16[288,768]{1,0:T(8,128)(2,1)S(1)} %pad_maximum_fusion.2.refs_0_), channel_id=1, source_target_pairs={{0,2},{1,3},{2,0},{3,1},{4,6},{5,7},{6,4},{7,5},{8,10},{9,11},{10,... | collective-permute-start | bytes 1327112 | tf_op jit(solution)/shard_map/ppermute | solution.py:656
  165.3 37.1 %collective-permute-start.6 = (bf16[448,576]{1,0:T(8,128)(2,1)S(1)}, bf16[448,576]{1,0:T(8,128)(2,1)S(1)}, u32[]{:S(2)}, u32[]{:S(2)}) collective-permute-start(bf16[448,576]{1,0:T(8,128)(2,1)S(1)} %get-tuple-element.110.refs_0_), channel_id=1, source_target_pairs={{0,4},{4,0},{8,12},{12,8},{16,20},{20,16},{24,28},{28,24},{1,5},{5... | collective-permute-start | bytes 1548296 | tf_op jit(solution)/shard_map/ppermute | solution.py:656
  165.3 37.9 %collective-permute-start.7 = (bf16[448,576]{1,0:T(8,128)(2,1)S(1)}, bf16[448,576]{1,0:T(8,128)(2,1)S(1)}, u32[]{:S(2)}, u32[]{:S(2)}) collective-permute-start(bf16[448,576]{1,0:T(8,128)(2,1)S(1)} %collective-permute-done.3.refs_1_), channel_id=1, source_target_pairs={{0,4},{4,0},{8,12},{12,8},{16,20},{20,16},{24,28},{28,24},{1,5},{5... | collective-permute-start | bytes 1548296 | tf_op jit(solution)/shard_map/ppermute | solution.py:656
  166.6 37.5 %collective-permute-start.8 = (bf16[448,576]{1,0:T(8,128)(2,1)S(1)}, bf16[448,576]{1,0:T(8,128)(2,1)S(1)}, u32[]{:S(2)}, u32[]{:S(2)}) collective-permute-start(bf16[448,576]{1,0:T(8,128)(2,1)S(1)} %collective-permute-done.4.refs_2_), channel_id=1, source_target_pairs={{0,4},{4,0},{8,12},{12,8},{16,20},{20,16},{24,28},{28,24},{1,5},{5... | collective-permute-start | bytes 1548296 | tf_op jit(solution)/shard_map/ppermute | solution.py:656
  185.4 19.5 %collective-permute-start.9 = (bf16[448,576]{1,0:T(8,128)(2,1)S(1)}, bf16[448,576]{1,0:T(8,128)(2,1)S(1)}, u32[]{:S(2)}, u32[]{:S(2)}) collective-permute-start(bf16[448,576]{1,0:T(8,128)(2,1)S(1)} %collective-permute-done.5.refs_3_), channel_id=1, source_target_pairs={{0,4},{4,0},{8,12},{12,8},{16,20},{20,16},{24,28},{28,24},{1,5},{5... | collective-permute-start | bytes 1548296 | tf_op jit(solution)/shard_map/ppermute | solution.py:656
  186.2 14.5 %collective-permute-start.15 = (bf16[288,768]{1,0:T(8,128)(2,1)S(1)}, bf16[288,768]{1,0:T(8,128)(2,1)S(1)}, u32[]{:S(2)}, u32[]{:S(2)}) collective-permute-start(bf16[288,768]{1,0:T(8,128)(2,1)S(1)} %pad_maximum_fusion.2.refs_0_), channel_id=1, source_target_pairs={{0,3},{1,2},{2,1},{3,0},{4,7},{5,6},{6,5},{7,4},{8,11},{9,10},{10,... | collective-permute-start | bytes 1327112 | tf_op jit(solution)/shard_map/ppermute | solution.py:656
  205.7 173.6 %all-gather.19.cloned.1.call-start = ((), (), s32[]{:S(2)}) async-start(), calls=%async_computation.11 | async-start | bytes 10616832 | tf_op jit(solution)/shard_map/all_gather | solution.py:681
  250.6 254.3 %reduce-scatter.5.cloned.1.call-start = ((), (), s32[]{:S(2)}) async-start(), calls=%async_computation.4 | async-start | bytes 10616832 | tf_op jit(solution)/shard_map/reduce_scatter | solution.py:678
  253.4 12.8 %collective-permute-start.11 = (bf16[448,192]{1,0:T(8,128)(2,1)S(1)}, bf16[448,192]{1,0:T(8,128)(2,1)S(1)}, u32[]{:S(2)}, u32[]{:S(2)}) collective-permute-start(bf16[448,192]{1,0:T(8,128)(2,1)S(1)} %get-tuple-element.116.refs_10_), channel_id=1, source_target_pairs={{0,16},{4,20},{8,24},{12,28},{16,0},{20,4},{24,8},{28,12},{1,17},{... | collective-permute-start | bytes 516104 | tf_op jit(solution)/shard_map/ppermute | solution.py:656
  254.0 12.9 %collective-permute-start.12 = (bf16[448,192]{1,0:T(8,128)(2,1)S(1)}, bf16[448,192]{1,0:T(8,128)(2,1)S(1)}, u32[]{:S(2)}, u32[]{:S(2)}) collective-permute-start(bf16[448,192]{1,0:T(8,128)(2,1)S(1)} %get-tuple-element.117.refs_11_), channel_id=1, source_target_pairs={{0,24},{4,28},{8,16},{12,20},{16,8},{20,12},{24,0},{28,4},{1,25},{... | collective-permute-start | bytes 516104 | tf_op jit(solution)/shard_map/ppermute | solution.py:656
  287.6 28.1 %collective-permute-start.16 = (bf16[448,576]{1,0:T(8,128)(2,1)S(1)}, bf16[448,576]{1,0:T(8,128)(2,1)S(1)}, u32[]{:S(2)}, u32[]{:S(2)}) collective-permute-start(bf16[448,576]{1,0:T(8,128)(2,1)S(1)} %get-tuple-element.126), channel_id=1, source_target_pairs={{0,8},{4,12},{8,0},{12,4},{16,24},{20,28},{24,16},{28,20},{1,9},{5... | collective-permute-start | bytes 1548296 | tf_op jit(solution)/shard_map/ppermute | solution.py:656
  288.5 29.3 %collective-permute-start.17 = (bf16[448,576]{1,0:T(8,128)(2,1)S(1)}, bf16[448,576]{1,0:T(8,128)(2,1)S(1)}, u32[]{:S(2)}, u32[]{:S(2)}) collective-permute-start(bf16[448,576]{1,0:T(8,128)(2,1)S(1)} %get-tuple-element.127), channel_id=1, source_target_pairs={{0,16},{4,20},{8,24},{12,28},{16,0},{20,4},{24,8},{28,12},{1,17},{... | collective-permute-start | bytes 1548296 | tf_op jit(solution)/shard_map/ppermute | solution.py:656
  291.1 45.7 %collective-permute-start.18 = (bf16[448,576]{1,0:T(8,128)(2,1)S(1)}, bf16[448,576]{1,0:T(8,128)(2,1)S(1)}, u32[]{:S(2)}, u32[]{:S(2)}) collective-permute-start(bf16[448,576]{1,0:T(8,128)(2,1)S(1)} %get-tuple-element.128), channel_id=1, source_target_pairs={{0,24},{4,28},{8,16},{12,20},{16,8},{20,12},{24,0},{28,4},{1,25},{... | collective-permute-start | bytes 1548296 | tf_op jit(solution)/shard_map/ppermute | solution.py:656
  291.1 45.7 %collective-permute-start.19 = (bf16[448,576]{1,0:T(8,128)(2,1)S(1)}, bf16[448,576]{1,0:T(8,128)(2,1)S(1)}, u32[]{:S(2)}, u32[]{:S(2)}) collective-permute-start(bf16[448,576]{1,0:T(8,128)(2,1)S(1)} %get-tuple-element.125.refs_0_), channel_id=1, source_target_pairs={{0,4},{4,0},{8,12},{12,8},{16,20},{20,16},{24,28},{28,24},{1,5},{5... | collective-permute-start | bytes 1548296 | tf_op jit(solution)/shard_map/ppermute | solution.py:656
  315.7 21.2 %collective-permute-start.20 = (bf16[448,576]{1,0:T(8,128)(2,1)S(1)}, bf16[448,576]{1,0:T(8,128)(2,1)S(1)}, u32[]{:S(2)}, u32[]{:S(2)}) collective-permute-start(bf16[448,576]{1,0:T(8,128)(2,1)S(1)} %collective-permute-done.16.refs_1_), channel_id=1, source_target_pairs={{0,4},{4,0},{8,12},{12,8},{16,20},{20,16},{24,28},{28,24},{1,5},{5... | collective-permute-start | bytes 1548296 | tf_op jit(solution)/shard_map/ppermute | solution.py:656
  317.9 19.1 %collective-permute-start.21 = (bf16[448,576]{1,0:T(8,128)(2,1)S(1)}, bf16[448,576]{1,0:T(8,128)(2,1)S(1)}, u32[]{:S(2)}, u32[]{:S(2)}) collective-permute-start(bf16[448,576]{1,0:T(8,128)(2,1)S(1)} %collective-permute-done.17.refs_2_), channel_id=1, source_target_pairs={{0,4},{4,0},{8,12},{12,8},{16,20},{20,16},{24,28},{28,24},{1,5},{5... | collective-permute-start | bytes 1548296 | tf_op jit(solution)/shard_map/ppermute | solution.py:656
  423.8 208.1 %reduce-scatter.7.cloned.1.call-start = ((), (), s32[]{:S(2)}) async-start(), calls=%async_computation.5 | async-start | bytes 5308416 | tf_op jit(solution)/shard_map/reduce_scatter | solution.py:678
  486.2 18.7 %collective-permute-start.29 = (bf16[448,576]{1,0:T(8,128)(2,1)}, bf16[448,576]{1,0:T(8,128)(2,1)S(1)}, u32[]{:S(2)}, u32[]{:S(2)}) collective-permute-start(bf16[448,576]{1,0:T(8,128)(2,1)} %get-tuple-element.147), channel_id=1, source_target_pairs={{0,4},{4,0},{8,12},{12,8},{16,20},{20,16},{24,28},{28,24},{1,5},{5... | collective-permute-start | bytes 1548296 | tf_op jit(solution)/shard_map/ppermute | solution.py:656
  489.9 20.8 %collective-permute-start.31 = (bf16[448,576]{1,0:T(8,128)(2,1)}, bf16[448,576]{1,0:T(8,128)(2,1)S(1)}, u32[]{:S(2)}, u32[]{:S(2)}) collective-permute-start(bf16[448,576]{1,0:T(8,128)(2,1)} %add_convert_fusion.6), channel_id=1, source_target_pairs={{0,8},{4,12},{8,0},{12,4},{16,24},{20,28},{24,16},{28,20},{1,9},{5... | collective-permute-start | bytes 1548296 | tf_op jit(solution)/shard_map/ppermute | solution.py:656
  491.9 18.8 %collective-permute-start.33 = (bf16[448,576]{1,0:T(8,128)(2,1)}, bf16[448,576]{1,0:T(8,128)(2,1)S(1)}, u32[]{:S(2)}, u32[]{:S(2)}) collective-permute-start(bf16[448,576]{1,0:T(8,128)(2,1)} %add_convert_fusion.5), channel_id=1, source_target_pairs={{0,16},{4,20},{8,24},{12,28},{16,0},{20,4},{24,8},{28,12},{1,17},{... | collective-permute-start | bytes 1548296 | tf_op jit(solution)/shard_map/ppermute | solution.py:656
  494.3 29.3 %collective-permute-start.35 = (bf16[448,576]{1,0:T(8,128)(2,1)}, bf16[448,576]{1,0:T(8,128)(2,1)S(1)}, u32[]{:S(2)}, u32[]{:S(2)}) collective-permute-start(bf16[448,576]{1,0:T(8,128)(2,1)} %add_convert_fusion.4), channel_id=1, source_target_pairs={{0,24},{4,28},{8,16},{12,20},{16,8},{20,12},{24,0},{28,4},{1,25},{... | collective-permute-start | bytes 1548296 | tf_op jit(solution)/shard_map/ppermute | solution.py:656
  536.2 137.3 %reduce-scatter.9.cloned.1.call-start = ((), (), s32[]{:S(2)}) async-start(), calls=%async_computation.6 | async-start | bytes 10616832 | tf_op jit(solution)/shard_map/reduce_scatter | solution.py:678
  567.5 201.9 %all-gather.21.cloned.1.call-start = ((), (), s32[]{:S(2)}) async-start(), calls=%async_computation.12 | async-start | bytes 6635520 | tf_op jit(solution)/shard_map/all_gather | solution.py:681
  568.4 15.1 %collective-permute-start.38 = (bf16[448,192]{1,0:T(8,128)(2,1)S(1)}, bf16[448,192]{1,0:T(8,128)(2,1)S(1)}, u32[]{:S(2)}, u32[]{:S(2)}) collective-permute-start(bf16[448,192]{1,0:T(8,128)(2,1)S(1)} %get-tuple-element.163), channel_id=1, source_target_pairs={{0,24},{4,28},{8,16},{12,20},{16,8},{20,12},{24,0},{28,4},{1,25},{... | collective-permute-start | bytes 516104 | tf_op jit(solution)/shard_map/ppermute | solution.py:656
  572.2 102.9 %collective-permute-start.53 = (bf16[384,384]{1,0:T(8,128)(2,1)}, bf16[384,384]{1,0:T(8,128)(2,1)}, u32[]{:S(2)}, u32[]{:S(2)}) collective-permute-start(bf16[384,384]{1,0:T(8,128)(2,1)} %get-tuple-element.236), channel_id=1, source_target_pairs={{0,3},{1,2},{2,1},{3,0},{4,7},{5,6},{6,5},{7,4},{8,11},{9,10},{10,... | collective-permute-start | bytes 884744 | tf_op jit(solution)/shard_map/ppermute | solution.py:656
  575.4 101.3 %collective-permute-start.52 = (bf16[384,384]{1,0:T(8,128)(2,1)S(1)}, bf16[384,384]{1,0:T(8,128)(2,1)}, u32[]{:S(2)}, u32[]{:S(2)}) collective-permute-start(bf16[384,384]{1,0:T(8,128)(2,1)S(1)} %get-tuple-element.237), channel_id=1, source_target_pairs={{0,2},{1,3},{2,0},{3,1},{4,6},{5,7},{6,4},{7,5},{8,10},{9,11},{10,... | collective-permute-start | bytes 884744 | tf_op jit(solution)/shard_map/ppermute | solution.py:656
  578.1 100.9 %collective-permute-start.51 = (bf16[384,384]{1,0:T(8,128)(2,1)S(1)}, bf16[384,384]{1,0:T(8,128)(2,1)S(1)}, u32[]{:S(2)}, u32[]{:S(2)}) collective-permute-start(bf16[384,384]{1,0:T(8,128)(2,1)S(1)} %get-tuple-element.235), channel_id=1, source_target_pairs={{0,1},{1,0},{2,3},{3,2},{4,5},{5,4},{6,7},{7,6},{8,9},{9,8},{10,11... | collective-permute-start | bytes 884744 | tf_op jit(solution)/shard_map/ppermute | solution.py:656
  634.0 45.2 %collective-permute-start.56 = (bf16[192,384]{1,0:T(8,128)(2,1)}, bf16[192,384]{1,0:T(8,128)(2,1)S(1)}, u32[]{:S(2)}, u32[]{:S(2)}) collective-permute-start(bf16[192,384]{1,0:T(8,128)(2,1)} %get-tuple-element.245), channel_id=1, source_target_pairs={{0,3},{1,2},{2,1},{3,0},{4,7},{5,6},{6,5},{7,4},{8,11},{9,10},{10,... | collective-permute-start | bytes 442376 | tf_op jit(solution)/shard_map/ppermute | solution.py:656
  637.3 45.0 %collective-permute-start.55 = (bf16[192,384]{1,0:T(8,128)(2,1)}, bf16[192,384]{1,0:T(8,128)(2,1)}, u32[]{:S(2)}, u32[]{:S(2)}) collective-permute-start(bf16[192,384]{1,0:T(8,128)(2,1)} %get-tuple-element.246), channel_id=1, source_target_pairs={{0,2},{1,3},{2,0},{3,1},{4,6},{5,7},{6,4},{7,5},{8,10},{9,11},{10,... | collective-permute-start | bytes 442376 | tf_op jit(solution)/shard_map/ppermute | solution.py:656
  676.7 13.7 %collective-permute-start.59 = (bf16[384,384]{1,0:T(8,128)(2,1)S(1)}, bf16[384,384]{1,0:T(8,128)(2,1)S(1)}, u32[]{:S(2)}, u32[]{:S(2)}) collective-permute-start(bf16[384,384]{1,0:T(8,128)(2,1)S(1)} %get-tuple-element.239), channel_id=1, source_target_pairs={{0,3},{1,2},{2,1},{3,0},{4,7},{5,6},{6,5},{7,4},{8,11},{9,10},{10,... | collective-permute-start | bytes 884744 | tf_op jit(solution)/shard_map/ppermute | solution.py:656
  679.1 25.7 %collective-permute-start.58 = (bf16[384,384]{1,0:T(8,128)(2,1)S(1)}, bf16[384,384]{1,0:T(8,128)(2,1)S(1)}, u32[]{:S(2)}, u32[]{:S(2)}) collective-permute-start(bf16[384,384]{1,0:T(8,128)(2,1)S(1)} %get-tuple-element.240), channel_id=1, source_target_pairs={{0,2},{1,3},{2,0},{3,1},{4,6},{5,7},{6,4},{7,5},{8,10},{9,11},{10,... | collective-permute-start | bytes 884744 | tf_op jit(solution)/shard_map/ppermute | solution.py:656
  679.2 25.6 %collective-permute-start.57 = (bf16[384,384]{1,0:T(8,128)(2,1)S(1)}, bf16[384,384]{1,0:T(8,128)(2,1)S(1)}, u32[]{:S(2)}, u32[]{:S(2)}) collective-permute-start(bf16[384,384]{1,0:T(8,128)(2,1)S(1)} %get-tuple-element.238), channel_id=1, source_target_pairs={{0,1},{1,0},{2,3},{3,2},{4,5},{5,4},{6,7},{7,6},{8,9},{9,8},{10,11... | collective-permute-start | bytes 884744 | tf_op jit(solution)/shard_map/ppermute | solution.py:656
  706.0 121.9 %reduce-scatter.11.cloned.1.call-start = ((), (), s32[]{:S(2)}) async-start(), calls=%async_computation.7 | async-start | bytes 5308416 | tf_op jit(solution)/shard_map/reduce_scatter | solution.py:678
  708.6 23.8 %collective-permute-start.41 = (bf16[448,576]{1,0:T(8,128)(2,1)S(1)}, bf16[448,576]{1,0:T(8,128)(2,1)S(1)}, u32[]{:S(2)}, u32[]{:S(2)}) collective-permute-start(bf16[448,576]{1,0:T(8,128)(2,1)S(1)} %add_convert_fusion.2), channel_id=1, source_target_pairs={{0,8},{4,12},{8,0},{12,4},{16,24},{20,28},{24,16},{28,20},{1,9},{5... | collective-permute-start | bytes 1548296 | tf_op jit(solution)/shard_map/ppermute | solution.py:656
  710.3 35.3 %collective-permute-start.43 = (bf16[448,576]{1,0:T(8,128)(2,1)S(1)}, bf16[448,576]{1,0:T(8,128)(2,1)S(1)}, u32[]{:S(2)}, u32[]{:S(2)}) collective-permute-start(bf16[448,576]{1,0:T(8,128)(2,1)S(1)} %add_convert_fusion.1), channel_id=1, source_target_pairs={{0,16},{4,20},{8,24},{12,28},{16,0},{20,4},{24,8},{28,12},{1,17},{... | collective-permute-start | bytes 1548296 | tf_op jit(solution)/shard_map/ppermute | solution.py:656
  711.8 33.7 %collective-permute-start.45 = (bf16[448,576]{1,0:T(8,128)(2,1)S(1)}, bf16[448,576]{1,0:T(8,128)(2,1)S(1)}, u32[]{:S(2)}, u32[]{:S(2)}) collective-permute-start(bf16[448,576]{1,0:T(8,128)(2,1)S(1)} %add_convert_fusion), channel_id=1, source_target_pairs={{0,24},{4,28},{8,16},{12,20},{16,8},{20,12},{24,0},{28,4},{1,25},{... | collective-permute-start | bytes 1548296 | tf_op jit(solution)/shard_map/ppermute | solution.py:656
  769.5 117.4 %all-gather.23.cloned.1.call-start = ((), (), s32[]{:S(2)}) async-start(), calls=%async_computation.13 | async-start | bytes 1327104 | tf_op jit(solution)/shard_map/all_gather | solution.py:681
  832.6 12.6 %collective-permute-start.61 = (bf16[192,384]{1,0:T(8,128)(2,1)S(1)}, bf16[192,384]{1,0:T(8,128)(2,1)S(1)}, u32[]{:S(2)}, u32[]{:S(2)}) collective-permute-start(bf16[192,384]{1,0:T(8,128)(2,1)S(1)} %get-tuple-element.243), channel_id=1, source_target_pairs={{0,2},{1,3},{2,0},{3,1},{4,6},{5,7},{6,4},{7,5},{8,10},{9,11},{10,... | collective-permute-start | bytes 442376 | tf_op jit(solution)/shard_map/ppermute | solution.py:656
  (133 other events, 1664.3 us)
Sparse Core Ops, SparseCore 0:
  82.6 39.0 all-gather.12
  124.1 75.7 all-gather.14
  205.8 44.7 all-gather.16
  252.9 82.5 all-gather.18
  423.2 81.6 reduce-scatter.4
  536.3 56.7 reduce-scatter.6
  597.0 76.4 reduce-scatter.8
  706.1 63.3 all-gather.20
  773.9 53.8 reduce-scatter.10
  846.1 23.0 all-gather.22
